TPU v7x, 32 devices: a whole 2x2x4 slice. The times are simulated.
32 devices in a mesh: rows: 4 (over z), cols: 8 (over y, x, core).
Axes of the slice: x: 2, y: 2, z: 4, core: 2. Of those that a mesh axis runs over, the one named last changes fastest.
Arguments:
- features: bfloat16 [16384, 256], P(('rows', 'cols')), may hold values from -6 to 6
- coords: float32 [3, 16384], P(None, ('rows', 'cols')), may hold values from -6 to 6
- valid_mask: int32 [16384], P(('rows', 'cols')), may hold values from 0 to 1, as said below
- neighbors: int32 [16, 16384], P(None, ('rows', 'cols')), may hold values from 0 to 511, as said below
- cotangent: bfloat16 [16384, 256], P(('rows', 'cols')), may hold values from -6 to 6
- weights: bfloat16 [338784], replicated
- master: float32 [338784], P(('rows', 'cols'))
- first_moment: float32 [338784], P(('rows', 'cols'))
- second_moment: float32 [338784], P(('rows', 'cols')), as said below
Outputs:
- block_out: bfloat16 [16384, 256], P(('rows', 'cols'))
- grad_features: bfloat16 [16384, 256], P(('rows', 'cols'))
- grad_norm: float32 [], replicated
- new_master: float32 [338784], P(('rows', 'cols'))
- new_first: float32 [338784], P(('rows', 'cols'))
- new_second: float32 [338784], P(('rows', 'cols'))
- new_weights: bfloat16 [338784], replicated
Inputs may be any that keep to these rules, and one draw needn't show every extreme that they name: `valid_mask`: the real points of each device are its first slots; each device has at least 64 of them, and some device has all 512. `neighbors`: indices of rows of the point's own device; the first neighbour of each point is the point itself, and every neighbour lies within 48 rows of it. `second_moment`: Positive.
All inputs are finite; a program needn't handle non-finite values.
Results may differ from a plain program's by a relative error of at most 0.0097.
Values may be sent and summed in bfloat16 or wider, within the bound.
A program may use at most 192 MiB of HBM per device.

v0:
```python
import jax
import jax.numpy as jnp
from jax import lax
from jax.sharding import PartitionSpec as P

WIDTH = 256
GROUPS = 32
NEAREST = 16


bn_eps = 1e-05
clip_norm = 0.01
learn_rate = 0.05
beta_one = 0.9
beta_two = 0.999
adam_eps = 1e-08
decay_rate = 0.01
step_count = 10
masked_logit = -1000000000.0
highest = lax.Precision.HIGHEST


def rounded(value):
    return lax.optimization_barrier(value.astype(jnp.bfloat16)).astype(jnp.float32)


def split_params(packed):
    square_size = WIDTH * WIDTH
    norm_size = 2 * WIDTH + 3 + GROUPS
    squares = packed[0 : 5 * square_size].reshape(5, WIDTH, WIDTH)
    offset = 5 * square_size
    att_in = packed[offset : offset + WIDTH * GROUPS].reshape(WIDTH, GROUPS)
    offset = offset + WIDTH * GROUPS
    att_out = packed[offset : offset + GROUPS * GROUPS].reshape(GROUPS, GROUPS)
    offset = offset + GROUPS * GROUPS
    pos_in = packed[offset : offset + 9].reshape(3, 3)
    offset = offset + 9
    pos_out = packed[offset : offset + 3 * WIDTH].reshape(3, WIDTH)
    offset = offset + 3 * WIDTH
    scales = packed[offset : offset + norm_size]
    offset = offset + norm_size
    shifts = packed[offset : offset + norm_size]
    return (squares, att_in, att_out, pos_in, pos_out, scales, shifts)


def norm_parts(vector):
    return (
        vector[0:WIDTH],
        vector[WIDTH : WIDTH + 3],
        vector[WIDTH + 3 : WIDTH + 3 + GROUPS],
        vector[WIDTH + 3 + GROUPS : 2 * WIDTH + 3 + GROUPS],
    )


def normalize(sample, sum_one, sum_two, members, factor, offset):
    center = sum_one / members
    spread = sum_two / members - center * center
    return factor * (sample - center) * lax.rsqrt(spread + bn_eps) + offset


def adam_update(param, moment, second, grad):
    moment_new = beta_one * moment + (1.0 - beta_one) * grad
    second_new = beta_two * second + (1.0 - beta_two) * grad * grad
    moment_hat = moment_new / (1.0 - beta_one**step_count)
    second_hat = second_new / (1.0 - beta_two**step_count)
    param_new = param - learn_rate * (
        moment_hat / (jnp.sqrt(second_hat) + adam_eps) + decay_rate * param
    )
    return (param_new, moment_new, second_new)


def shards(
    features, coords, valid_mask, neighbors, cotangent, weights, master, first_moment, second_moment
):
    packed = weights.astype(jnp.float32)
    squares, att_in, att_out, pos_in, pos_out, scales, shifts = split_params(packed)
    gain_one, gain_pos, gain_att, gain_out = norm_parts(scales)
    shift_one, shift_pos, shift_att, shift_out = norm_parts(shifts)
    points = features.shape[0]
    valid_rows = valid_mask.astype(jnp.float32)
    neighbor_rows = neighbors.T
    neighbor_valid = valid_rows[neighbor_rows]
    pair_valid = valid_rows[:, None] * neighbor_valid
    first_slot = (lax.broadcasted_iota(jnp.int32, (points, NEAREST), 1) == 0).astype(jnp.float32)
    allowed = jnp.maximum(neighbor_valid, first_slot)
    rel_pos = coords[:, neighbor_rows] - coords[:, :, None]
    inputs_f = features.astype(jnp.float32)
    point_mask = valid_rows[:, None]
    pair_mask = pair_valid[:, :, None]

    def piece_one(source, w_lin):
        return jnp.dot(source, w_lin, preferred_element_type=jnp.float32)

    def piece_pos(w_pos):
        return jnp.einsum("cpk,cd->dpk", rel_pos, w_pos, precision=highest)

    pre_one, pull_one = jax.vjp(piece_one, inputs_f, squares[0])
    pos_pre, pull_pos = jax.vjp(piece_pos, pos_in)
    stats_one = lax.psum(
        (
            jnp.sum(point_mask * pre_one, axis=0),
            jnp.sum(point_mask * pre_one * pre_one, axis=0),
            jnp.sum(pair_valid[None] * pos_pre, axis=(1, 2)),
            jnp.sum(pair_valid[None] * pos_pre * pos_pre, axis=(1, 2)),
            jnp.sum(valid_rows),
            jnp.sum(pair_valid),
        ),
        ("rows", "cols"),
    )
    sum_a, sqr_a, sum_p, sqr_p, point_count, pair_count = stats_one

    def piece_hidden(pre_in, sum_aa, sqr_aa, gain_a, shift_a):
        return jax.nn.silu(normalize(pre_in, sum_aa, sqr_aa, point_count, gain_a, shift_a))

    hidden_f, pull_hidden = jax.vjp(piece_hidden, pre_one, sum_a, sqr_a, gain_one, shift_one)
    hidden = rounded(hidden_f)

    def piece_project(source, w_query, w_key, w_value):
        return (
            jnp.dot(source, w_query, preferred_element_type=jnp.float32),
            jnp.dot(source, w_key, preferred_element_type=jnp.float32),
            jnp.dot(source, w_value, preferred_element_type=jnp.float32),
        )

    (query_f, key_f, value_f), pull_project = jax.vjp(
        piece_project, hidden, squares[1], squares[2], squares[3]
    )
    queries = rounded(query_f)
    key_rows = rounded(key_f)
    values = rounded(value_f)

    def piece_encode(pos_in_pre, sum_pp, sqr_pp, gain_p, shift_p, w_enc):
        pos_act = jax.nn.silu(
            normalize(
                pos_in_pre,
                sum_pp[:, None, None],
                sqr_pp[:, None, None],
                pair_count,
                gain_p[:, None, None],
                shift_p[:, None, None],
            )
        )
        return jnp.einsum("cpk,cd->pkd", pos_act, w_enc, precision=highest)

    encoding, pull_encode = jax.vjp(
        piece_encode, pos_pre, sum_p, sqr_p, gain_pos, shift_pos, pos_out
    )

    def piece_relation(query_rows, key_all, encode_rows):
        return query_rows[:, None, :] - key_all[neighbor_rows] + encode_rows

    relation_f, pull_relation = jax.vjp(piece_relation, queries, key_rows, encoding)
    relation = rounded(relation_f)

    def piece_weigh(rel_rows, w_rel):
        return jnp.einsum("pkc,cg->pkg", rel_rows, w_rel, preferred_element_type=jnp.float32)

    pre_att, pull_weigh = jax.vjp(piece_weigh, relation, att_in)
    sum_w, sqr_w = lax.psum(
        (
            jnp.sum(pair_mask * pre_att, axis=(0, 1)),
            jnp.sum(pair_mask * pre_att * pre_att, axis=(0, 1)),
        ),
        ("rows", "cols"),
    )

    def piece_activ(pre_in, sum_ww, sqr_ww, gain_w, shift_w):
        return jax.nn.silu(normalize(pre_in, sum_ww, sqr_ww, pair_count, gain_w, shift_w))

    activ_f, pull_activ = jax.vjp(piece_activ, pre_att, sum_w, sqr_w, gain_att, shift_att)
    activ = rounded(activ_f)

    def piece_logit(act_rows, w_logit):
        return jnp.einsum("pkg,gh->pkh", act_rows, w_logit, preferred_element_type=jnp.float32)

    logits, pull_logit = jax.vjp(piece_logit, activ, att_out)

    def piece_mix(logit_rows, value_rows, encode_rows):
        masked = jnp.where(allowed[:, :, None] > 0.5, logit_rows, masked_logit)
        top_val = jnp.max(masked, axis=1, keepdims=True)
        expon = jnp.exp(masked - top_val)
        attention = expon / jnp.sum(expon, axis=1, keepdims=True)
        mixed = (value_rows[neighbor_rows] + encode_rows).reshape(
            points, NEAREST, GROUPS, WIDTH // GROUPS
        )
        return jnp.einsum("pkg,pkgc->pgc", attention, mixed, precision=highest).reshape(
            points, WIDTH
        )

    attended_f, pull_mix = jax.vjp(piece_mix, logits, values, encoding)
    attended = rounded(attended_f)

    def piece_final(att_rows, w_final):
        return jnp.dot(att_rows, w_final, preferred_element_type=jnp.float32)

    pre_out, pull_final = jax.vjp(piece_final, attended, squares[4])
    sum_o, sqr_o = lax.psum(
        (jnp.sum(point_mask * pre_out, axis=0), jnp.sum(point_mask * pre_out * pre_out, axis=0)),
        ("rows", "cols"),
    )

    def piece_four(pre_in, source, sum_oo, sqr_oo, gain_o, shift_o):
        return point_mask * jax.nn.silu(
            source + normalize(pre_in, sum_oo, sqr_oo, point_count, gain_o, shift_o)
        )

    outputs, pull_four = jax.vjp(piece_four, pre_out, inputs_f, sum_o, sqr_o, gain_out, shift_out)
    d_pre_out, d_resid, d_sum_o, d_sqr_o, d_gain_out, d_shift_out = pull_four(
        cotangent.astype(jnp.float32)
    )
    back_out = lax.psum((d_sum_o, d_sqr_o), ("rows", "cols"))
    d_pre_out = rounded(d_pre_out + point_mask * (back_out[0] + 2.0 * pre_out * back_out[1]))
    d_attended, d_final = pull_final(d_pre_out)
    d_logits, d_values, d_enc_mix = pull_mix(d_attended)
    d_activ, d_att_out = pull_logit(rounded(d_logits))
    d_pre_att, d_sum_w, d_sqr_w, d_gain_att, d_shift_att = pull_activ(d_activ)
    back_att = lax.psum((d_sum_w, d_sqr_w), ("rows", "cols"))
    d_pre_att = rounded(d_pre_att + pair_mask * (back_att[0] + 2.0 * pre_att * back_att[1]))
    d_relation, d_att_in = pull_weigh(d_pre_att)
    d_queries, d_keys, d_enc_rel = pull_relation(d_relation)
    d_encoding = d_enc_mix + d_enc_rel
    d_pos_pre, d_sum_p, d_sqr_p, d_gain_pos, d_shift_pos, d_pos_out = pull_encode(d_encoding)
    d_hidden, d_query, d_key, d_value = pull_project(
        (rounded(d_queries), rounded(d_keys), rounded(d_values))
    )
    d_pre_one, d_sum_a, d_sqr_a, d_gain_one, d_shift_one = pull_hidden(d_hidden)
    back_one = lax.psum((d_sum_a, d_sqr_a, d_sum_p, d_sqr_p), ("rows", "cols"))
    d_pre_one = rounded(d_pre_one + point_mask * (back_one[0] + 2.0 * pre_one * back_one[1]))
    d_pos_pre = d_pos_pre + pair_valid[None] * (
        back_one[2][:, None, None] + 2.0 * pos_pre * back_one[3][:, None, None]
    )
    d_source, d_lin = pull_one(d_pre_one)
    (d_pos_in,) = pull_pos(d_pos_pre)
    grad_inputs = d_resid + d_source
    pieces_all = [
        d_lin.ravel(),
        d_query.ravel(),
        d_key.ravel(),
        d_value.ravel(),
        d_final.ravel(),
        d_att_in.ravel(),
        d_att_out.ravel(),
        d_pos_in.ravel(),
        d_pos_out.ravel(),
        d_gain_one,
        d_gain_pos,
        d_gain_att,
        d_gain_out,
        d_shift_one,
        d_shift_pos,
        d_shift_att,
        d_shift_out,
    ]
    used_len = sum((piece.shape[0] for piece in pieces_all))
    local_grads = jnp.concatenate(
        pieces_all + [jnp.zeros((weights.shape[0] - used_len,), jnp.float32)]
    )
    shard_len = master.shape[0]
    owner = lax.axis_index(("rows", "cols"))
    total_grads = lax.psum(local_grads, ("rows", "cols"))
    norm_value = jnp.sqrt(jnp.sum(total_grads * total_grads))
    grad_shard = lax.dynamic_slice_in_dim(total_grads, owner * shard_len, shard_len)
    clipped = grad_shard * jnp.minimum(1.0, clip_norm / norm_value)
    new_master, new_first, new_second = adam_update(master, first_moment, second_moment, clipped)
    new_weights = lax.all_gather(
        new_master.astype(jnp.bfloat16), ("rows", "cols"), axis=0, tiled=True
    )
    return (
        outputs.astype(jnp.bfloat16),
        grad_inputs.astype(jnp.bfloat16),
        norm_value,
        new_master,
        new_first,
        new_second,
        new_weights,
    )


def solution(mesh):
    in_specs = (
        P(("rows", "cols"), None),
        P(None, ("rows", "cols")),
        P(("rows", "cols")),
        P(None, ("rows", "cols")),
        P(("rows", "cols"), None),
        P(),
        P(("rows", "cols")),
        P(("rows", "cols")),
        P(("rows", "cols")),
    )
    out_specs = (
        P(("rows", "cols"), None),
        P(("rows", "cols"), None),
        P(),
        P(("rows", "cols")),
        P(("rows", "cols")),
        P(("rows", "cols")),
        P(),
    )
    return jax.shard_map(shards, mesh=mesh, in_specs=in_specs, out_specs=out_specs, check_vma=False)
```

profile of v0, /device:TPU:1, one launch (start us, length us, event | category | flops | bytes accessed | tf_op | source)
XLA Modules:
  0.0 1033.2 jit_solution(7610125774478367793)
XLA Ops:
  7.9 0.8 fusion.84
  8.7 0.8 fusion.85
  9.6 1.3 convert_reduce_fusion.1
  12.2 0.8 slice.98
  13.0 1.5 fusion.82
  15.2 0.8 compare_select_fusion
  16.9 51.2 %gather_fusion = f32[8192]{0:T(1024)S(1)} fusion(f32[512]{0:T(512)S(1)} %convert_element_type.94, s32[8192]{0:T(1024)S(1)} %broadcast_clamp_fusion), kind=kCustom, calls=%fused_computation | custom fusion | bytes 98304 | tf_op jit(solution)/shard_map/gather | solution.py:82
  71.8 27.7 %gather_fusion.2 = f32[8192,3]{1,0:T(8,128)} fusion(f32[3,512]{0,1:T(8,128)S(1)} %copy.74, s32[8192]{0:T(1024)S(1)} %broadcast_clamp_fusion), kind=kCustom, calls=%fused_computation.2 | custom fusion | bytes 229376 | tf_op jit(solution)/shard_map/gather | solution.py:86
  99.5 2.8 copy.75
  103.1 41.1 %all-reduce.6 = (f32[3]{0:T(128)S(1)}, f32[]{:T(128)}, f32[3]{0:T(128)S(1)}, f32[256]{0:T(256)S(1)}, f32[]{:T(128)}, /*index=5*/f32[256]{0:T(256)S(1)}) all-reduce(f32[3]{0:T(128)S(1)} %get-tuple-element.28, f32[]{:T(128)} %get-tuple-element.76, f32[3]{0:T(128)S(1)} %get-tuple-element.27, ...), channel_id=1, replica_groups=mesh['rows'=4,'cols'=8] {'rows','cols'}, use_global_device_ids=true, to_apply=%region_7.0 | all-reduce | flops 520 | bytes 4160 | tf_op jit(solution)/shard_map/psum | solution.py:99
  144.3 1.2 fusion.76
  146.4 31.3 %gather_fusion.1 = f32[8192,256]{1,0:T(8,128)} fusion(f32[512,256]{1,0:T(8,128)S(1)} %convert_element_type.102, s32[8192]{0:T(1024)S(1)} %broadcast_clamp_fusion), kind=kCustom, calls=%fused_computation.1 | custom fusion | bytes 16809984 | tf_op jit(solution)/shard_map/jvp()/gather | solution.py:150
  177.7 10.0 copy.73
  187.7 1.2 fusion.78
  188.9 9.5 add_convert_fusion
  198.5 2.0 copy-done.2
  200.4 1.0 fusion.13
  201.4 40.6 %all-reduce.5 = (f32[32]{0:T(128)S(1)}, f32[32]{0:T(128)S(1)}) all-reduce(f32[32]{0:T(128)S(1)} %get-tuple-element.10, f32[32]{0:T(128)S(1)} %get-tuple-element.9), channel_id=1, replica_groups=mesh['rows'=4,'cols'=8] {'rows','cols'}, use_global_device_ids=true, to_apply=%region_13.14 | all-reduce | flops 64 | bytes 512 | tf_op jit(solution)/shard_map/psum | solution.py:159
  242.1 1.2 fusion.74
  245.2 1.0 squeeze.18
  247.1 31.4 %gather_fusion.3 = f32[8192,256]{1,0:T(8,128)} fusion(f32[512,256]{1,0:T(8,128)S(1)} %convert_element_type.106, s32[8192]{0:T(1024)S(1)} %broadcast_clamp_fusion), kind=kCustom, calls=%fused_computation.3 | custom fusion | bytes 16809984 | tf_op jit(solution)/shard_map/jvp()/gather | solution.py:183
  278.5 10.0 copy.82
  288.5 7.4 fusion.1
  296.6 1.1 fusion.19
  297.7 39.9 %all-reduce.4 = (f32[256]{0:T(256)S(1)}, f32[256]{0:T(256)S(1)}) all-reduce(f32[256]{0:T(256)S(1)} %get-tuple-element.20, f32[256]{0:T(256)S(1)} %get-tuple-element.19), channel_id=1, replica_groups=mesh['rows'=4,'cols'=8] {'rows','cols'}, use_global_device_ids=true, to_apply=%region_19.20 | all-reduce | flops 512 | bytes 4096 | tf_op jit(solution)/shard_map/psum | solution.py:197
  338.2 3.0 multiply_reduce_fusion.7
  342.5 40.1 %all-reduce.3 = (f32[256]{0:T(256)S(1)}, f32[256]{0:T(256)S(1)}) all-reduce(f32[256]{0:T(256)S(1)} %broadcast_divide_fusion.1, f32[256]{0:T(256)S(1)} %get-tuple-element.61), channel_id=1, replica_groups=mesh['rows'=4,'cols'=8] {'rows','cols'}, use_global_device_ids=true, to_apply=%region_25.26 | all-reduce | flops 512 | bytes 4096 | tf_op jit(solution)/shard_map/psum | solution.py:211
  382.6 1.2 add_convert_fusion.3
  383.8 1.9 convolution_bitcast_fusion
  385.7 1.2 fusion.24
  387.2 12.2 %multiply_bitcast_fusion = (f32[512,16,256]{0,2,1:T(8,128)}, f32[512,16,32,8]{0,3,2,1:T(8,128)}, f32[512,32,16]{0,1,2:T(8,128)S(1)}) fusion(f32[512,32,16]{0,1,2:T(8,128)S(1)} %divide_bitcast_fusion, f32[512,32,8]{0,2,1:T(8,128)S(1)} %copy.84, f32[512,16,256]{0,2,1:T(8,128)} %copy.82, f32[512,16,256]{0,2,1:T(8,128)} %get-tuple-element.101), kind=kLoop, calls=%fused_computation.6 | loop fusion | flops 8126464 | bytes 36175872 | tf_op jit(solution)/shard_map/transpose(jvp())/reshape | solution.py:183
  401.0 1.6 multiply_reduce_fusion.2
  403.9 40.1 %all-reduce.2 = (f32[32]{0:T(128)S(1)}, f32[32]{0:T(128)S(1)}) all-reduce(f32[32]{0:T(128)S(1)} %broadcast_divide_fusion.4, f32[32]{0:T(128)S(1)} %get-tuple-element.57), channel_id=1, replica_groups=mesh['rows'=4,'cols'=8] {'rows','cols'}, use_global_device_ids=true, to_apply=%region_33.34 | all-reduce | flops 64 | bytes 512 | tf_op jit(solution)/shard_map/psum | solution.py:217
  444.4 3.4 convolution_bitcast_fusion.5
  447.8 7.3 fusion.81
  455.2 9.3 copy.92
  464.6 7.9 fusion.10
  472.8 2.4 copy-done.1
  475.1 5.5 multiply_reduce_fusion.14
  480.7 33.3 %copy.85 = f32[512,16,32,8]{1,0,3,2:T(8,128)} copy(f32[512,16,32,8]{0,3,2,1:T(8,128)} %get-tuple-element.81) | data formatting | bytes 16777216 | tf_op jit(solution)/shard_map/transpose(jvp(pkg,pkgc->pgc))/transpose | solution.py:186
  514.0 54.5 %reshape.293 = f32[8192,256]{0,1:T(8,128)} reshape(f32[512,16,32,8]{1,0,3,2:T(8,128)} %copy.85) | data formatting | bytes 16777216 | tf_op jit(solution)/shard_map/transpose(jvp())/reshape | solution.py:183
  568.5 9.2 copy.86
  577.7 44.7 %scatter_custom_fusion = f32[512,256]{1,0:T(8,128)S(1)} fusion(s32[8192]{0:T(1024)} %copy-done.33, f32[8192,256]{1,0:T(8,128)} %copy.86, f32[]{:T(128)} %constant.27.clone.1), kind=kCustom, calls=%fused_computation.89 | custom fusion | flops 2097152 | bytes 524800 | tf_op jit(solution)/shard_map/transpose(jvp())/scatter-add | solution.py:183
  623.0 0.8 copy.122
  624.0 1.2 fusion.62
  625.2 1.2 broadcast_divide_fusion.6
  626.7 0.8 copy.119
  627.6 11.5 %copy.88 = f32[512,16,256]{2,1,0:T(8,128)} copy(f32[512,16,256]{2,0,1:T(8,128)} %get-tuple-element.79) | data formatting | bytes 16777216 | tf_op jit(solution)/shard_map/transpose(jvp())/neg | solution.py:150
  639.1 45.0 %scatter_custom_fusion.1 = f32[512,256]{1,0:T(8,128)S(1)} fusion(s32[8192]{0:T(1024)} %copy-done.33, f32[8192,256]{1,0:T(8,128)} %bitcast.142, f32[]{:T(128)} %constant.27.clone.1), kind=kCustom, calls=%fused_computation.87 | custom fusion | flops 2097152 | bytes 524800 | tf_op jit(solution)/shard_map/transpose(jvp())/scatter-add | solution.py:150
  684.5 0.8 copy.120
  685.3 0.8 copy.121
  686.5 2.1 multiply_reduce_fusion.8
  688.6 1.3 fusion.57
  690.5 40.4 %all-reduce.1 = (f32[256]{0:T(256)S(1)}, f32[256]{0:T(256)S(1)}, f32[3]{0:T(128)S(1)}, f32[3]{0:T(128)S(1)}) all-reduce(f32[256]{0:T(256)S(1)} %broadcast_divide_fusion, f32[256]{0:T(256)S(1)} %get-tuple-element.55, f32[3]{0:T(128)} %broadcast_divide_fusion.6, ...), channel_id=1, replica_groups=mesh['rows'=4,'cols'=8] {'rows','cols'}, use_global_device_ids=true, to_apply=%region_39.40 | all-reduce | flops 518 | bytes 4144 | tf_op jit(solution)/shard_map/psum | solution.py:227
  730.8 1.2 add_convert_fusion.2
  732.6 1.7 convolution_bitcast_fusion.8
  734.5 21.5 %concatenate.3 = f32[338784]{0:T(1024)} concatenate(f32[65536]{0:T(1024)S(1)} %bitcast.151, f32[65536]{0:T(1024)} %bitcast.148, f32[65536]{0:T(1024)S(1)} %bitcast.149, f32[65536]{0:T(1024)S(1)} %bitcast.150, f32[65536]{0:T(1024)} %bitcast.147, f32[8192]{0:T(1024)S(1)} %reshape.253, f32[1024]{0:T(1024)S(1)} %reshape.254, f32[9]{0:T(128)S(1)} %reshape.255, f32[768]{0:T(1024)S(1)} %reshape.256, ...), dimensions={0} | concatenate | bytes 2710272 | tf_op jit(solution)/shard_map/concatenate | solution.py:255
  756.1 132.6 %all-reduce.10.cloned.1.call-done = f32[338784]{0:T(1024)} async-done(((f32[338784]{0:T(1024)}), f32[338784]{0:T(1024)}) %all-reduce.10.cloned.1.call-update) | async-done | bytes 1355152 | tf_op jit(solution)/shard_map/psum | solution.py:260
  888.7 2.3 multiply_reduce_fusion.1
  891.8 1.6 fusion.69
  893.9 0.8 copy-done.9
  894.8 1.0 fusion.6
  895.7 127.1 %all-reduce.12.cloned.1.call-done = bf16[338784]{0:T(1024)(128)(2,1)} async-done(((bf16[338784]{0:T(1024)(128)(2,1)}), bf16[338784]{0:T(1024)(128)(2,1)}) %all-reduce.12.cloned.1.call-update) | async-done | bytes 677584
  1022.8 2.0 copy.128
  (216 shorter events, 21.7 us)
Async XLA Ops:
  7.2 881.5 %all-reduce.10.cloned.1.call-start = ((), (), s32[]{:S(2)}) async-start(), calls=%async_computation | async-start | bytes 2711552 | tf_op jit(solution)/shard_map/psum | solution.py:260
  8.7 234.5 %copy-start.57 = (f32[32]{0:T(128)}, f32[32]{0:T(128)S(1)}, u32[]{:S(2)}) copy-start(f32[32]{0:T(128)S(1)} %get-tuple-element.93) | copy-start | bytes 388
  8.7 234.5 %copy-start.66 = (f32[32]{0:T(128)}, f32[32]{0:T(128)S(1)}, u32[]{:S(2)}) copy-start(f32[32]{0:T(128)S(1)} %get-tuple-element.94) | copy-start | bytes 388
  9.6 179.3 %copy-start.47 = (f32[3]{0:T(128)}, f32[3]{0:T(128)S(1)}, u32[]{:S(2)}) copy-start(f32[3]{0:T(128)S(1)} %get-tuple-element.95) | copy-start | bytes 40
  9.6 179.3 %copy-start.53 = (f32[3]{0:T(128)}, f32[3]{0:T(128)S(1)}, u32[]{:S(2)}) copy-start(f32[3]{0:T(128)S(1)} %get-tuple-element.96) | copy-start | bytes 40
  14.5 131.0 %copy-start.42 = (f32[256]{0:T(256)}, f32[256]{0:T(256)S(1)}, u32[]{:S(2)}) copy-start(f32[256]{0:T(256)S(1)} %get-tuple-element.85) | copy-start | bytes 3076
  14.5 131.0 %copy-start.64 = (f32[256]{0:T(256)}, f32[256]{0:T(256)S(1)}, u32[]{:S(2)}) copy-start(f32[256]{0:T(256)S(1)} %get-tuple-element.86) | copy-start | bytes 3076
  16.9 52.2 %copy-start.26 = (bf16[338784]{0:T(1024)(128)(2,1)S(1)}, bf16[338784]{0:T(1024)(128)(2,1)}, u32[]{:S(2)}) copy-start(bf16[338784]{0:T(1024)(128)(2,1)} %param.14) | copy-start | bytes 2032708
  16.9 54.4 %slice-start = ((bf16[338784]{0:T(1024)(128)(2,1)}), bf16[8192]{0:T(1024)(128)(2,1)S(1)}, s32[]{:S(2)}) async-start(bf16[338784]{0:T(1024)(128)(2,1)} %param.14), calls=%async_computation.2 | async-start | bytes 32768 | tf_op jit(solution)/shard_map/slice | solution.py:32
  16.9 54.6 %copy-start.55 = (f32[3,512]{1,0:T(4,128)S(1)}, f32[3,512]{1,0:T(4,128)}, u32[]{:S(2)}) copy-start(f32[3,512]{1,0:T(4,128)} %param.10) | copy-start | bytes 18436
  68.0 34.3 %copy-start.10 = (bf16[512,256]{1,0:T(8,128)(2,1)S(1)}, bf16[512,256]{1,0:T(8,128)(2,1)}, u32[]{:S(2)}) copy-start(bf16[512,256]{1,0:T(8,128)(2,1)} %param.9) | copy-start | bytes 786436
  71.3 127.1 %copy-start.27 = (bf16[256,32]{1,0:T(8,128)(2,1)}, bf16[256,32]{1,0:T(8,128)(2,1)S(1)}, u32[]{:S(2)}) copy-start(bf16[256,32]{1,0:T(8,128)(2,1)S(1)} %reshape.244) | copy-start | bytes 49156
  71.7 74.3 %copy-start.20 = (bf16[256,256]{1,0:T(8,128)(2,1)}, bf16[256,256]{1,0:T(8,128)(2,1)S(1)}, u32[]{:S(2)}) copy-start(bf16[256,256]{1,0:T(8,128)(2,1)S(1)} %squeeze.17) | copy-start | bytes 393220
  71.7 74.6 %copy-start.29 = (bf16[256,256]{1,0:T(8,128)(2,1)}, bf16[256,256]{1,0:T(8,128)(2,1)S(1)}, u32[]{:S(2)}) copy-start(bf16[256,256]{1,0:T(8,128)(2,1)S(1)} %squeeze.16) | copy-start | bytes 393220
  71.8 74.2 %copy-start.16 = (bf16[256,256]{1,0:T(8,128)(2,1)}, bf16[256,256]{1,0:T(8,128)(2,1)S(1)}, u32[]{:S(2)}) copy-start(bf16[256,256]{1,0:T(8,128)(2,1)S(1)} %squeeze.15) | copy-start | bytes 393220
  102.4 43.6 %copy-start.32 = (f32[512,16,3]{0,2,1:T(4,128)}, f32[512,16,3]{0,2,1:T(4,128)S(1)}, u32[]{:S(2)}) copy-start(f32[512,16,3]{0,2,1:T(4,128)S(1)} %copy.75) | copy-start | bytes 294916
  102.7 43.0 %copy-start.5 = (f32[512,256]{1,0:T(8,128)}, f32[512,256]{1,0:T(8,128)S(1)}, u32[]{:S(2)}) copy-start(f32[512,256]{1,0:T(8,128)S(1)} %get-tuple-element.99) | copy-start | bytes 1572868
  103.1 85.8 %copy-start.14 = (f32[3,512,16]{1,0,2:T(4,128)}, f32[3,512,16]{1,0,2:T(4,128)S(1)}, u32[]{:S(2)}) copy-start(f32[3,512,16]{1,0,2:T(4,128)S(1)} %get-tuple-element.98) | copy-start | bytes 294916
  145.5 32.2 %copy-start.40 = (f32[256]{0:T(256)}, f32[256]{0:T(256)S(1)}, u32[]{:S(2)}) copy-start(f32[256]{0:T(256)S(1)} %get-tuple-element.70) | copy-start | bytes 3076
  145.5 32.2 %copy-start.45 = (f32[256]{0:T(256)}, f32[256]{0:T(256)S(1)}, u32[]{:S(2)}) copy-start(f32[256]{0:T(256)S(1)} %get-tuple-element.72) | copy-start | bytes 3076
  188.9 9.6 copy-start.38
  188.9 9.6 copy-start.50
  198.5 2.0 copy-start.2
  201.4 42.3 %copy-start.3 = (f32[512,16,32]{0,2,1:T(8,128)}, f32[512,16,32]{0,2,1:T(8,128)S(1)}, u32[]{:S(2)}) copy-start(f32[512,16,32]{0,2,1:T(8,128)S(1)} %get-tuple-element.102) | copy-start | bytes 3145732
  288.5 8.1 copy-start.34
  288.5 49.7 %copy-start.44 = (f32[256]{0:T(256)S(1)}, f32[256]{0:T(256)}, u32[]{:S(2)}) copy-start(f32[256]{0:T(256)} %get-tuple-element.84) | copy-start | bytes 3076
  288.5 49.7 %copy-start.65 = (f32[256]{0:T(256)S(1)}, f32[256]{0:T(256)}, u32[]{:S(2)}) copy-start(f32[256]{0:T(256)} %get-tuple-element.87) | copy-start | bytes 3076
  341.2 58.1 %copy-start.7 = (f32[512,256]{1,0:T(8,128)}, f32[512,256]{1,0:T(8,128)S(1)}, u32[]{:S(2)}) copy-start(f32[512,256]{1,0:T(8,128)S(1)} %get-tuple-element.63) | copy-start | bytes 1572868
  387.1 12.2 %copy-start.31 = (f32[512,32]{0,1:T(8,128)S(1)}, f32[512,32]{0,1:T(8,128)}, u32[]{:S(2)}) copy-start(f32[512,32]{0,1:T(8,128)} %multiply_divide_fusion) | copy-start | bytes 196612
  387.1 12.5 %copy-start.13 = (f32[512,32]{0,1:T(8,128)S(1)}, f32[512,32]{0,1:T(8,128)}, u32[]{:S(2)}) copy-start(f32[512,32]{0,1:T(8,128)} %copy-done.12) | copy-start | bytes 196612
  399.3 1.6 copy-start.56
  399.3 1.6 copy-start.58
  399.3 1.6 copy-start.60
  399.3 1.6 copy-start.62
  399.7 2.9 copy-start.69
  401.0 46.8 %copy-start.28 = (bf16[256,32]{1,0:T(8,128)(2,1)S(1)}, bf16[256,32]{1,0:T(8,128)(2,1)}, u32[]{:S(2)}) copy-start(bf16[256,32]{1,0:T(8,128)(2,1)} %copy-done.27) | copy-start | bytes 49156
  455.1 9.4 copy-start.15
  455.2 9.4 copy-start.39
  455.2 9.3 copy-start.48
  455.2 9.3 copy-start.51
  455.2 9.3 copy-start.54
  464.5 8.2 copy-start
  464.5 10.6 %copy-start.1 = (f32[512,16,256]{2,0,1:T(8,128)S(1)}, f32[512,16,256]{2,0,1:T(8,128)}, u32[]{:S(2)}) copy-start(f32[512,16,256]{2,0,1:T(8,128)} %copy.92) | copy-start | bytes 25165828
  568.5 54.3 %copy-start.19 = (bf16[256,256]{1,0:T(8,128)(2,1)S(1)}, bf16[256,256]{1,0:T(8,128)(2,1)}, u32[]{:S(2)}) copy-start(bf16[256,256]{1,0:T(8,128)(2,1)} %copy-done.18) | copy-start | bytes 393220
  568.5 54.5 %copy-start.23 = (f32[32,2,8,128]{3,2,1,0:T(8,128)S(1)}, f32[32,2,8,128]{3,2,1,0:T(8,128)}, u32[]{:S(2)}) copy-start(f32[32,2,8,128]{3,2,1,0:T(8,128)} %convolution_bitcast_fusion) | copy-start | bytes 786436
  568.5 55.6 %copy-start.68 = (f32[3]{0:T(128)S(1)}, f32[3]{0:T(128)}, u32[]{:S(2)}) copy-start(f32[3]{0:T(128)} %get-tuple-element.74) | copy-start | bytes 40
  627.5 58.6 %copy-start.21 = (bf16[256,256]{1,0:T(8,128)(2,1)S(1)}, bf16[256,256]{1,0:T(8,128)(2,1)}, u32[]{:S(2)}) copy-start(bf16[256,256]{1,0:T(8,128)(2,1)} %copy-done.20) | copy-start | bytes 393220
  627.5 58.9 %copy-start.6 = (f32[512,256]{1,0:T(8,128)S(1)}, f32[512,256]{1,0:T(8,128)}, u32[]{:S(2)}) copy-start(f32[512,256]{1,0:T(8,128)} %copy-done.5) | copy-start | bytes 1572868
  627.5 58.9 %copy-start.30 = (bf16[256,256]{1,0:T(8,128)(2,1)S(1)}, bf16[256,256]{1,0:T(8,128)(2,1)}, u32[]{:S(2)}) copy-start(bf16[256,256]{1,0:T(8,128)(2,1)} %copy-done.29) | copy-start | bytes 393220
  627.5 58.9 %copy-start.41 = (f32[256]{0:T(256)S(1)}, f32[256]{0:T(256)}, u32[]{:S(2)}) copy-start(f32[256]{0:T(256)} %copy-done.40) | copy-start | bytes 3076
  627.5 58.9 %copy-start.43 = (f32[256]{0:T(256)S(1)}, f32[256]{0:T(256)}, u32[]{:S(2)}) copy-start(f32[256]{0:T(256)} %copy-done.42) | copy-start | bytes 3076
  627.5 58.9 %copy-start.46 = (f32[256]{0:T(256)S(1)}, f32[256]{0:T(256)}, u32[]{:S(2)}) copy-start(f32[256]{0:T(256)} %copy-done.45) | copy-start | bytes 3076
  639.1 93.0 %copy-start.11 = (bf16[512,256]{1,0:T(8,128)(2,1)S(1)}, bf16[512,256]{1,0:T(8,128)(2,1)}, u32[]{:S(2)}) copy-start(bf16[512,256]{1,0:T(8,128)(2,1)} %param.9) | copy-start | bytes 786436
  639.1 93.5 %copy-start.49 = (f32[3]{0:T(128)S(1)}, f32[3]{0:T(128)}, u32[]{:S(2)}) copy-start(f32[3]{0:T(128)} %copy-done.47) | copy-start | bytes 40
  639.1 93.5 %copy-start.52 = (f32[3]{0:T(128)S(1)}, f32[3]{0:T(128)}, u32[]{:S(2)}) copy-start(f32[3]{0:T(128)} %copy-done.50) | copy-start | bytes 40
  639.1 95.4 %copy-start.63 = (f32[256]{0:T(256)S(1)}, f32[256]{0:T(256)}, u32[]{:S(2)}) copy-start(f32[256]{0:T(256)} %get-tuple-element.12) | copy-start | bytes 3076
  684.5 207.3 %copy-start.35 = (f32[10587]{0:T(1024)S(1)}, f32[10587]{0:T(1024)}, u32[]{:S(2)}) copy-start(f32[10587]{0:T(1024)} %param.15) | copy-start | bytes 127048
  684.5 207.3 %copy-start.36 = (f32[10587]{0:T(1024)S(1)}, f32[10587]{0:T(1024)}, u32[]{:S(2)}) copy-start(f32[10587]{0:T(1024)} %param.16) | copy-start | bytes 127048
  684.5 207.3 %copy-start.37 = (f32[10587]{0:T(1024)S(1)}, f32[10587]{0:T(1024)}, u32[]{:S(2)}) copy-start(f32[10587]{0:T(1024)} %param.17) | copy-start | bytes 127048
  686.2 48.3 %copy-start.24 = (f32[32,2,8,128]{3,1,2,0:T(2,128)S(1)}, f32[32,2,8,128]{3,1,2,0:T(2,128)}, u32[]{:S(2)}) copy-start(f32[32,2,8,128]{3,1,2,0:T(2,128)} %copy.120) | copy-start | bytes 786436
  686.2 208.6 %copy-start.8 = (f32[512,256]{1,0:T(8,128)S(1)}, f32[512,256]{1,0:T(8,128)}, u32[]{:S(2)}) copy-start(f32[512,256]{1,0:T(8,128)} %copy-done.7) | copy-start | bytes 1572868
  686.2 208.6 %copy-start.17 = (bf16[256,256]{1,0:T(8,128)(2,1)S(1)}, bf16[256,256]{1,0:T(8,128)(2,1)}, u32[]{:S(2)}) copy-start(bf16[256,256]{1,0:T(8,128)(2,1)} %copy-done.16) | copy-start | bytes 393220
  686.5 48.0 %copy-start.25 = (f32[32,2,8,128]{3,1,2,0:T(2,128)S(1)}, f32[32,2,8,128]{3,1,2,0:T(2,128)}, u32[]{:S(2)}) copy-start(f32[32,2,8,128]{3,1,2,0:T(2,128)} %copy.121) | copy-start | bytes 786436
  756.1 266.8 %all-reduce.12.cloned.1.call-start = ((), (), s32[]{:S(2)}) async-start(), calls=%async_computation.1 | async-start | bytes 1355776
  (9 other events, 7.7 us)
Sparse Core Ops, SparseCore 0:
  756.2 132.4 all-reduce.9
  894.9 127.9 all-reduce.11
where the time goes:
time: 1040 us; the launch traced here: 1030 us
  local copies, waits for them, and re-layouts  328 us (32%)
  waiting for transfers between devices  260 us (25%)
  blocking collectives  242 us (23%)
  other arithmetic  136 us (13%)
  matrix products  48.8 us (5%)
  between operations  17.4 us (2%)
    psum x1, waiting for transfers between devices, shards(): total_grads = lax.psum(local_grads, ('rows', 'cols'))  133 us
    unnamed x3, waiting for transfers between devices  127 us
    reshape x3, local copies, waits for them, and re-layouts, piece_mix(): (value_rows[neighbor_rows] + encode_rows).reshape(points, NEAREST, GROUPS...  73 us
    gather x3, local copies, waits for them, and re-layouts, shards(): neighbor_valid = valid_rows[neighbor_rows]  51.4 us
    scatter-add x1, other arithmetic, piece_relation(): return query_rows[:, None, :] - key_all[neighbor_rows] + encode_rows  45 us
    scatter-add x1, other arithmetic, piece_mix(): value_rows[neighbor_rows] + encode_rows  44.7 us
    gather x2, local copies, waits for them, and re-layouts, piece_mix(): value_rows[neighbor_rows] + encode_rows  41.3 us
    gather x2, local copies, waits for them, and re-layouts, piece_relation(): return query_rows[:, None, :] - key_all[neighbor_rows] + encode_rows  41.3 us
  transfers between devices with their start and end apart: 2, of which 2 were waited for; matrix products, arithmetic and copies ran while one was open for 0% of the time, Pallas kernels for 0%

commit v1 on v0

v1 whole, which is shorter than its diff:
```python
import functools

import jax
import jax.numpy as jnp
from jax import lax
from jax.experimental import pallas as pl
from jax.experimental.pallas import tpu as pltpu
from jax.sharding import PartitionSpec as P

WIDTH = 256
GROUPS = 32
NEAREST = 16
PER_GROUP = WIDTH // GROUPS
LANES = 128
WINDOW = 256
PAIRS = NEAREST * LANES

SQUARE = WIDTH * WIDTH
OFF_ATT_IN = 5 * SQUARE
OFF_ATT_OUT = OFF_ATT_IN + WIDTH * GROUPS
OFF_TAIL = OFF_ATT_OUT + GROUPS * GROUPS
NORMS = 2 * WIDTH + 3 + GROUPS
TAIL_POS_OUT = 9
TAIL_GAINS = TAIL_POS_OUT + 3 * WIDTH
TAIL_SHIFTS = TAIL_GAINS + NORMS
TAIL_USED = TAIL_SHIFTS + NORMS
TAIL_PAD = 2048
SLICE = 2048
SLICE_ROWS = SLICE // LANES
CHUNK = 1024

bn_eps = 1e-05
clip_norm = 0.01
learn_rate = 0.05
beta_one = 0.9
beta_two = 0.999
adam_eps = 1e-08
decay_rate = 0.01
step_count = 10
masked_logit = -1000000000.0

f32 = jnp.float32
bf16 = jnp.bfloat16
MESH = pl.DeviceIdType.MESH


def contract(a, b, left, right):
    return lax.dot_general(a, b, (((left,), (right,)), ((), ())), preferred_element_type=f32)


def nn(a, b):
    return contract(a, b, 1, 0)


def nt(a, b):
    return contract(a, b, 1, 1)


def tn(a, b):
    return contract(a, b, 0, 0)


def split(value, parts):
    pieces = []
    for _ in range(parts):
        piece = value.astype(bf16)
        pieces.append(piece)
        value = value - piece.astype(f32)
    return pieces


def silu_parts(value):
    gate = 0.5 * jnp.tanh(0.5 * value) + 0.5
    return value * gate, gate


def silu_slope(value, gate):
    return gate * (1.0 + value * (1.0 - gate))


def iota(shape, dim):
    return lax.broadcasted_iota(jnp.int32, shape, dim)


def row_to_col(row, count):
    wide = jnp.broadcast_to(row, (count, row.shape[1]))
    same = iota(wide.shape, 0) == iota(wide.shape, 1)
    return jnp.sum(jnp.where(same, wide, 0.0), axis=1, keepdims=True)


def col_to_row(col, offset):
    wide = jnp.broadcast_to(col, (col.shape[0], LANES))
    same = iota(wide.shape, 0) + offset == iota(wide.shape, 1)
    return jnp.sum(jnp.where(same, wide, 0.0), axis=0, keepdims=True)


def row_sum(value):
    return jnp.sum(value, axis=0, keepdims=True)


def lane_fold(value):
    total = value[:, 0:LANES]
    for k in range(1, value.shape[1] // LANES):
        total = total + value[:, k * LANES : (k + 1) * LANES]
    return total


def lane_sum(value):
    return jnp.sum(lane_fold(value), axis=1, keepdims=True)


def tiles(value):
    return jnp.concatenate([value] * NEAREST, axis=1)


def adam(param, moment, second, grad):
    moment_new = beta_one * moment + (1.0 - beta_one) * grad
    second_new = beta_two * second + (1.0 - beta_two) * grad * grad
    moment_hat = moment_new / (1.0 - beta_one**step_count)
    second_hat = second_new / (1.0 - beta_two**step_count)
    param_new = param - learn_rate * (
        moment_hat / (jnp.sqrt(second_hat) + adam_eps) + decay_rate * param
    )
    return param_new, moment_new, second_new


def peer(me, step, count):
    if count & (count - 1) == 0:
        return me ^ (count - step)
    return lax.rem(me + step, count)


def block_kernel(
    n_rows, n_cols,
    feat_h, coords_h, valid_h, nbrs_h, cot_h, weights_h, master_h, first_h, second_h,
    out_h, gfeat_h, gnorm_h, new_master_h, new_first_h, new_second_h, slabs_h,
    feat, coords, valid, nbrs, cot, w_first, pos_first, weights, state, news, outs, norm_s, in_sem, out_sem,
    stat_send, stat_buf, stat_ssem, stat_rsem,
    tail1d, mats, onehot, vgat, att, wpre, uact, dyw, rel, pos, act, pmask, allow, dmix,
    a1_s, z_s, h_s, q_s, k_s, o_s, do_s, dv_s, sk_s, bd_s, xs, dz_s, dz16,
    flat, pair_got, part16, got16, sums, owned, tail_g, slab_f, shard_w, all_w,
    pair_ssem, pair_rsem, rs_ssem, rs_rsem, own_ssem, own_rsem, ag_ssem, ag_rsem, fw_ssem, fw_rsem,
):
    n = n_rows * n_cols
    half = n // 2
    row_id, col_id = lax.axis_index("rows"), lax.axis_index("cols")
    me = row_id * n_cols + col_id
    core = lax.rem(col_id, 2)
    chip = me // 2
    points = feat.shape[0]
    blocks = points // LANES
    starts = [min(max(LANES * b - (WINDOW - LANES) // 2, 0), points - WINDOW) for b in range(blocks)]
    total_len = weights.shape[0]
    shard_len = master_h.shape[0]
    shard_rows = -(-tail_g.shape[0] // LANES)
    sliced = flat.shape[0]
    slots = got16.shape[0]
    sides = own_ssem.shape[1]
    span = own_rsem.shape[0]

    def place(device):
        return (device // n_cols, lax.rem(device, n_cols))

    loads = []

    def load(source, target):
        copy = pltpu.make_async_copy(source, target, in_sem.at[len(loads)])
        copy.start()
        loads.append(copy)
        return copy

    stores = []

    def store(source, target):
        copy = pltpu.make_async_copy(source, target, out_sem.at[len(stores)])
        copy.start()
        stores.append(copy)

    early = [
        load(feat_h, feat),
        load(weights_h.at[pl.ds(0, SQUARE)], w_first),
        load(weights_h.at[pl.ds(OFF_TAIL, 1024)], pos_first),
        load(nbrs_h, nbrs),
        load(coords_h, coords),
        load(valid_h, valid),
    ]

    barrier = pltpu.get_barrier_semaphore()

    def greet(k, carry):
        pl.semaphore_signal(barrier, inc=1, device_id=place(peer(me, k, n)), device_id_type=MESH)
        return carry

    lax.fori_loop(1, n, greet, 0)
    late = [load(weights_h, weights), load(cot_h, cot)]
    for source, target in ((master_h, 0), (first_h, 1), (second_h, 2)):
        late.append(load(source, state[target]))
    owned[...] = jnp.zeros(owned.shape, f32)
    for copy in early:
        copy.wait()

    sent = []

    def all_sum(index, message):
        rows = message.shape[0]
        stat_send[index, 0:rows] = message
        stat_buf[index, me, 0:rows] = message

        def post(k, carry):
            pltpu.make_async_remote_copy(
                src_ref=stat_send.at[index, pl.ds(0, rows)],
                dst_ref=stat_buf.at[index, me, pl.ds(0, rows)],
                send_sem=stat_ssem.at[index],
                recv_sem=stat_rsem.at[index],
                device_id=place(peer(me, k, n)),
                device_id_type=MESH,
            ).start()
            return carry

        lax.fori_loop(1, n, post, 0)
        sent.append((index, rows))

        def collect():
            span = stat_buf.at[index, pl.ds(0, n - 1), pl.ds(0, rows)]
            pltpu.make_async_copy(span, span, stat_rsem.at[index]).wait()
            return jnp.sum(stat_buf[index, :, 0:rows], axis=0)

        return collect

    sibling = (row_id, col_id + 1 - 2 * core)
    per_matrix = SQUARE // SLICE // 2

    def put_matrix(m, grad):
        flat[m * per_matrix : (m + 1) * per_matrix] = grad.reshape(per_matrix, 2, SLICE_ROWS, LANES)

    def exchange(group, begin, count):
        copy = pltpu.make_async_remote_copy(
            src_ref=flat.at[pl.ds(begin, count), 1 - core],
            dst_ref=pair_got.at[pl.ds(begin, count)],
            send_sem=pair_ssem.at[group],
            recv_sem=pair_rsem.at[group],
            device_id=sibling,
            device_id_type=MESH,
        )
        copy.start()
        return copy, begin, count

    def send_slice(index, slot, other):
        pltpu.make_async_remote_copy(
            src_ref=part16.at[index],
            dst_ref=got16.at[slot, chip],
            send_sem=rs_ssem.at[slot],
            recv_sem=rs_rsem.at[slot],
            device_id=place(2 * other + core),
            device_id_type=MESH,
        ).start()

    def send_group(pair):
        copy, begin, count = pair
        copy.wait()
        part16[pl.ds(begin, count)] = (
            flat[pl.ds(begin, count), core] + pair_got[pl.ds(begin, count)]
        ).astype(bf16)
        if count % half == 0 and begin % half == 0:
            for slot in range(begin // half, (begin + count) // half):

                def post(k, carry, slot=slot):
                    other = peer(chip, k, half)
                    send_slice(slot * half + other, slot, other)
                    return carry

                lax.fori_loop(1, half, post, 0)
        else:

            def post_any(k, carry):
                index = begin + k
                slot, other = index // half, lax.rem(index, half)

                @pl.when(other != chip)
                def _():
                    send_slice(index, slot, other)

                return carry

            lax.fori_loop(0, count, post_any, 0)

    def drain_stats(index, rows):
        span = stat_buf.at[index, pl.ds(0, n - 1), pl.ds(0, rows)]
        pltpu.make_async_copy(span, span, stat_ssem.at[index]).wait()

    w_in = w_first[...].reshape(WIDTH, WIDTH)
    mats[0] = w_in
    w_in = mats[0]
    pos_in = pos_first[...].reshape(1024 // LANES, LANES)[0:1].astype(f32)
    lane8 = iota((8, 1), 0)

    def pos_in_col(c):
        return jnp.where(lane8 < 3, row_to_col(pos_in[:, 3 * c : 3 * c + 8], 8), 0.0)

    valid_rows = valid[...].reshape(points // LANES, LANES).astype(f32)
    n_valid = jnp.sum(jnp.sum(valid_rows, axis=0, keepdims=True), axis=1, keepdims=True)
    point_mask = (iota((points, 1), 0).astype(f32) < n_valid).astype(f32)
    lane_mask = (iota((1, points), 1).astype(f32) < n_valid).astype(f32)

    a1 = nn(feat[...], w_in)
    a1_s[...] = a1
    masked = point_mask * a1
    sum_a, sqr_a = row_sum(masked), row_sum(masked * a1)

    window_row = iota((WINDOW, LANES), 0)
    for b in range(blocks):
        for j in range(NEAREST):
            index = nbrs[j : j + 1, b * LANES : (b + 1) * LANES] - starts[b]
            onehot[b, :, j * LANES : (j + 1) * LANES] = jnp.where(
                window_row == index, 1.0, 0.0
            ).astype(bf16)

    coords8 = jnp.concatenate([coords[...], jnp.zeros((5, points), f32)], axis=0)
    table = jnp.concatenate(
        split(coords8, 3) + [jnp.broadcast_to(lane_mask, (8, points)).astype(bf16)], axis=0
    )
    slot0 = (iota((1, PAIRS), 1) < LANES).astype(f32)
    pos_in_cols = [pos_in_col(c) for c in range(3)]
    sum_p = jnp.zeros((8, 1), f32)
    sqr_p = jnp.zeros((8, 1), f32)
    pairs_local = jnp.zeros((1, 1), f32)
    for b in range(blocks):
        here = slice(b * LANES, (b + 1) * LANES)
        fetched = nn(table[:, starts[b] : starts[b] + WINDOW], onehot[b])
        place_n = fetched[0:8] + fetched[8:16] + fetched[16:24]
        mask_n = fetched[24:32]
        r = place_n - tiles(coords8[:, here])
        pm = mask_n * tiles(lane_mask[:, here])
        p = pos_in_cols[0] * r[0:1] + pos_in_cols[1] * r[1:2] + pos_in_cols[2] * r[2:3]
        rel[b] = r
        pos[b] = p
        pmask[b] = pm
        allow[b] = jnp.maximum(mask_n, slot0)
        sum_p = sum_p + lane_sum(pm * p)
        sqr_p = sqr_p + lane_sum(pm * p * p)
        pairs_local = pairs_local + lane_sum(pm[0:1])

    lane = iota((1, LANES), 1)
    last = (
        col_to_row(sum_p, 0)
        + col_to_row(sqr_p, 8)
        + jnp.where(lane == 16, n_valid, 0.0)
        + jnp.where(lane == 17, pairs_local, 0.0)
    )

    def fold(row):
        return jnp.concatenate([row[:, 0:LANES], row[:, LANES:WIDTH]], axis=0)

    def unfold(rows):
        return jnp.concatenate([rows[0:1], rows[1:2]], axis=1)

    pl.semaphore_wait(barrier, n - 1)
    collect_first = all_sum(0, jnp.concatenate([fold(sum_a), fold(sqr_a), last], axis=0))
    for copy in late:
        copy.wait()
    for m in range(1, 5):
        mats[m] = weights[pl.ds(m * SQUARE, SQUARE)].reshape(WIDTH, WIDTH)
    w_q, w_k, w_v, w_o = (mats[m] for m in range(1, 5))
    att_in = weights[pl.ds(OFF_ATT_IN, WIDTH * GROUPS)].reshape(WIDTH * GROUPS // LANES, LANES)
    att_in_f = att_in.astype(f32).reshape(WIDTH, GROUPS)
    att_in_t = att_in_f.T.astype(bf16)
    att_out_f = (
        weights[pl.ds(OFF_ATT_OUT, GROUPS * GROUPS)]
        .reshape(GROUPS * GROUPS // LANES, LANES)
        .astype(f32)
        .reshape(GROUPS, GROUPS)
    )
    att_out = att_out_f.astype(bf16)
    att_out_t = att_out_f.T.astype(bf16)
    tail1d[pl.ds(0, 1024)] = weights[pl.ds(OFF_TAIL, 1024)]
    rest = total_len - OFF_TAIL - 1024
    tail1d[pl.ds(1024, rest)] = weights[pl.ds(OFF_TAIL + 1024, rest)]
    tail = tail1d[pl.ds(0, TAIL_PAD)].reshape(TAIL_PAD // LANES, LANES).astype(f32)
    tail = jnp.concatenate([tail[k : k + 1] for k in range(TAIL_PAD // LANES)], axis=1)
    pos_rows = [tail[:, TAIL_POS_OUT + WIDTH * d : TAIL_POS_OUT + WIDTH * (d + 1)] for d in range(3)]
    def norm_pieces(start):
        ends = [0, WIDTH, WIDTH + 3, WIDTH + 3 + GROUPS, NORMS]
        return [tail[:, start + ends[k] : start + ends[k + 1]] for k in range(4)]

    gain_a, gain_p, gain_w, gain_o = norm_pieces(TAIL_GAINS)
    shift_a, shift_p, shift_w, shift_o = norm_pieces(TAIL_SHIFTS)

    def pad_col(row):
        wide = jnp.concatenate([row, jnp.zeros((1, 5), f32)], axis=1)
        return row_to_col(wide, 8)

    gain_p, shift_p = pad_col(gain_p), pad_col(shift_p)
    gain_w, shift_w = row_to_col(gain_w, GROUPS), row_to_col(shift_w, GROUPS)

    stats = collect_first()

    def pick(row, at):
        return jnp.sum(jnp.where(lane == at, row, 0.0), axis=1, keepdims=True)

    point_count, pair_count = pick(stats[4:5], 16), pick(stats[4:5], 17)
    inv_points, inv_pairs = 1.0 / point_count, 1.0 / pair_count

    def moments(total, square, inv):
        mean = total * inv
        return mean, lax.rsqrt(square * inv - mean * mean + bn_eps)

    mean_a, rs_a = moments(unfold(stats[0:2]), unfold(stats[2:4]), inv_points)
    mean_p, rs_p = moments(
        row_to_col(stats[4:5, 0:8], 8), row_to_col(stats[4:5, 8:16], 8), inv_pairs
    )

    h = silu_parts((a1_s[...] - mean_a) * rs_a * gain_a + shift_a)[0].astype(bf16)
    h_s[...] = h
    q = nn(h, w_q).astype(bf16)
    k = nn(h, w_k).astype(bf16)
    q_s[...] = q
    k_s[...] = k
    q_att = nt(att_in_t, q)
    k_att = jnp.concatenate(split(nt(att_in_t, k), 3), axis=0)
    pos_mat = jnp.concatenate(pos_rows + [jnp.zeros((13, WIDTH), f32)], axis=0).astype(bf16)
    pos_att = nt(att_in_t, pos_mat)
    pos_att_cols = [pos_att[:, d : d + 1] for d in range(3)]

    sum_w = jnp.zeros((GROUPS, LANES), f32)
    sqr_w = jnp.zeros((GROUPS, LANES), f32)
    for b in range(blocks):
        here = slice(b * LANES, (b + 1) * LANES)
        active = silu_parts((pos[b] - mean_p) * rs_p * gain_p + shift_p)[0]
        act[b] = active
        fetched = nn(k_att[:, starts[b] : starts[b] + WINDOW], onehot[b])
        w = tiles(q_att[:, here]) - (
            fetched[0:GROUPS] + fetched[GROUPS : 2 * GROUPS] + fetched[2 * GROUPS : 3 * GROUPS]
        )
        for d in range(3):
            w = w + pos_att_cols[d] * active[d : d + 1]
        wpre[b] = w
        mw = w * pmask[b, 0:1]
        sum_w = sum_w + lane_fold(mw)
        sqr_w = sqr_w + lane_fold(mw * w)

    def pair_row(one, two):
        one = jnp.sum(one, axis=1, keepdims=True)
        two = jnp.sum(two, axis=1, keepdims=True)
        return col_to_row(one, 0) + col_to_row(two, GROUPS)

    collect_w = all_sum(1, pair_row(sum_w, sqr_w))
    v_t = nn(h, w_v).T.astype(bf16)
    for b in range(blocks):
        vgat[b] = nn(v_t[:, starts[b] : starts[b] + WINDOW], onehot[b])
    stats = collect_w()
    mean_w, rs_w = moments(
        row_to_col(stats[:, 0:GROUPS], GROUPS),
        row_to_col(stats[:, GROUPS : 2 * GROUPS], GROUPS),
        inv_pairs,
    )

    group_of = iota((WIDTH, 2 * GROUPS), 0) // PER_GROUP
    spread = jnp.where(group_of == iota((WIDTH, 2 * GROUPS), 1) % GROUPS, 1.0, 0.0).astype(bf16)
    own_group = iota((GROUPS, WIDTH), 1) // PER_GROUP == iota((GROUPS, WIDTH), 0)
    gather_groups = jnp.where(own_group, 1.0, 0.0).astype(bf16)
    pos_spread = jnp.concatenate(
        [jnp.where(own_group, jnp.broadcast_to(pos_rows[d], (GROUPS, WIDTH)), 0.0) for d in range(3)],
        axis=0,
    ).astype(bf16)

    def cols(j):
        return slice(j * LANES, (j + 1) * LANES)

    for b in range(blocks):
        here = slice(b * LANES, (b + 1) * LANES)
        u = silu_parts((wpre[b] - mean_w) * rs_w * gain_w + shift_w)[0].astype(bf16)
        uact[b] = u
        logit = jnp.where(allow[b, 0:1] > 0.5, nn(att_out_t, u), masked_logit)
        top = logit[:, cols(0)]
        for j in range(1, NEAREST):
            top = jnp.maximum(top, logit[:, cols(j)])
        weight = jnp.exp(logit - tiles(top))
        share = 1.0 / functools.reduce(jnp.add, [weight[:, cols(j)] for j in range(NEAREST)])
        att[b] = weight * tiles(share)
        mixed = jnp.zeros((WIDTH, LANES), f32)
        enc = [jnp.zeros((GROUPS, LANES), f32) for _ in range(3)]
        for j in range(NEAREST):
            a = att[b, :, cols(j)]
            wide = nn(spread, jnp.concatenate(split(a, 2), axis=0))
            mixed = mixed + wide * vgat[b, :, cols(j)]
            for d in range(3):
                enc[d] = enc[d] + a * act[b, d : d + 1, cols(j)]
        enc = jnp.concatenate(enc, axis=0)
        bd_s[:, here] = enc
        for piece in split(enc, 3):
            mixed = mixed + tn(pos_spread, piece)
        o_s[:, here] = mixed.astype(bf16)

    z = tn(o_s[...], w_o)
    z_s[...] = z
    masked = point_mask * z
    collect_o = all_sum(2, jnp.concatenate([fold(row_sum(masked)), fold(row_sum(masked * z))], axis=0))
    stats = collect_o()
    mean_o, rs_o = moments(unfold(stats[0:2]), unfold(stats[2:4]), inv_points)

    zhat = (z_s[...] - mean_o) * rs_o
    y = feat[...].astype(f32) + zhat * gain_o + shift_o
    value, gate = silu_parts(y)
    outs[0] = (point_mask * value).astype(bf16)
    store(outs.at[0], out_h)
    dy = point_mask * cot[...].astype(f32) * silu_slope(y, gate)
    dz_s[...] = dy
    shift_grad_o, gain_grad_o = row_sum(dy), row_sum(dy * zhat)
    stats = all_sum(3, jnp.concatenate([fold(shift_grad_o), fold(gain_grad_o)], axis=0))()
    one, two = unfold(stats[0:2]) * inv_points, unfold(stats[2:4]) * inv_points
    zhat = (z_s[...] - mean_o) * rs_o
    dz = (gain_o * rs_o * (dz_s[...] - point_mask * (one + zhat * two))).astype(bf16)
    dz16[...] = dz
    do_s[...] = nt(w_o, dz)
    dv_s[...] = jnp.zeros(dv_s.shape, f32)

    sum_w = jnp.zeros((GROUPS, LANES), f32)
    sqr_w = jnp.zeros((GROUPS, LANES), f32)
    d_att_out = jnp.zeros((GROUPS, GROUPS), f32)
    for b in range(blocks):
        here = slice(b * LANES, (b + 1) * LANES)
        do = do_s[:, here]
        do_pos = sum(nn(pos_spread, piece) for piece in split(do, 2))
        da, mix = [], []
        for j in range(NEAREST):
            a = att[b, :, cols(j)]
            wide = nn(spread, jnp.concatenate(split(a, 2), axis=0))
            xs[:, cols(j)] = (wide * do).astype(bf16)
            grad = nn(gather_groups, (vgat[b, :, cols(j)] * do).astype(bf16))
            back = []
            for d in range(3):
                part = do_pos[d * GROUPS : (d + 1) * GROUPS]
                grad = grad + part * act[b, d : d + 1, cols(j)]
                back.append(row_sum(part * a))
            da.append(grad)
            mix.append(jnp.concatenate(back + [jnp.zeros((5, LANES), f32)], axis=0))
        dmix[b] = jnp.concatenate(mix, axis=1)
        dv_s[pl.ds(starts[b], WINDOW)] += nt(onehot[b], xs[...])
        mean_da = functools.reduce(jnp.add, [da[j] * att[b, :, cols(j)] for j in range(NEAREST)])
        ds = jnp.concatenate(
            [att[b, :, cols(j)] * (da[j] - mean_da) for j in range(NEAREST)], axis=1
        ).astype(bf16)
        d_att_out = d_att_out + nt(uact[b], ds)
        what = (wpre[b] - mean_w) * rs_w
        y = what * gain_w + shift_w
        gate = silu_parts(y)[1]
        dy = nn(att_out, ds) * silu_slope(y, gate)
        dyw[b] = dy
        sum_w = sum_w + lane_fold(dy)
        sqr_w = sqr_w + lane_fold(dy * what)

    back_w = pair_row(sum_w, sqr_w)
    collect_w = all_sum(4, back_w)
    dv = dv_s[...].astype(bf16)
    put_matrix(4, nn(o_s[...], dz16[...]))
    put_matrix(3, tn(h_s[...], dv))
    late_pair = exchange(0, 3 * 16, 2 * 16)
    send_group(late_pair)
    stats = collect_w()
    one = row_to_col(stats[:, 0:GROUPS], GROUPS) * inv_pairs
    two = row_to_col(stats[:, GROUPS : 2 * GROUPS], GROUPS) * inv_pairs

    sk_s[...] = jnp.zeros(sk_s.shape, f32)
    pos_att_rows = split(pos_att[:, 0:8].T, 3)
    pos_att_rows = jnp.concatenate(pos_att_rows, axis=0)
    dw_sums = []
    d_pos_att = jnp.zeros((24, GROUPS), f32)
    sum_p = jnp.zeros((8, 1), f32)
    sqr_p = jnp.zeros((8, 1), f32)
    for b in range(blocks):
        what = (wpre[b] - mean_w) * rs_w
        dw_f = gain_w * rs_w * (dyw[b] - pmask[b, 0:1] * (one + what * two))
        dw = dw_f.astype(bf16)
        sk_s[pl.ds(starts[b], WINDOW)] += nt(onehot[b], dw)
        dw_sums.append(lane_slots(dw.astype(f32)))
        active = act[b]
        d_pos_att = d_pos_att + nt(jnp.concatenate(split(active, 3), axis=0), dw)
        back = nn(pos_att_rows, dw)
        d_act = dmix[b] + back[0:8] + back[8:16] + back[16:24]
        phat = (pos[b] - mean_p) * rs_p
        y = phat * gain_p + shift_p
        gate = silu_parts(y)[1]
        dy = d_act * silu_slope(y, gate)
        dmix[b] = dy
        sum_p = sum_p + lane_sum(dy)
        sqr_p = sqr_p + lane_sum(dy * phat)
    dq_att = jnp.concatenate(dw_sums, axis=1)
    dq_split = split(dq_att, 2)
    dk_split = split(-sk_s[...], 2)
    dq = sum(tn(piece, att_in_t) for piece in dq_split).astype(bf16)
    dk = sum(nn(piece, att_in_t) for piece in dk_split).astype(bf16)
    dh = nt(dq, w_q) + nt(dk, w_k) + nt(dv, w_v)
    ahat = (a1_s[...] - mean_a) * rs_a
    y = ahat * gain_a + shift_a
    gate = silu_parts(y)[1]
    dy = dh * silu_slope(y, gate)
    z_s[...] = dy
    shift_grad_a, gain_grad_a = row_sum(dy), row_sum(dy * ahat)
    last = col_to_row(sum_p, 0) + col_to_row(sqr_p, 8)
    collect_a = all_sum(
        5, jnp.concatenate([fold(shift_grad_a), fold(gain_grad_a), last], axis=0)
    )

    put_matrix(1, tn(h_s[...], dq))
    put_matrix(2, tn(h_s[...], dk))
    send_group(exchange(1, per_matrix, 2 * per_matrix))
    d_pos_att = d_pos_att[0:8] + d_pos_att[8:16] + d_pos_att[16:24]
    d_pos_split = split(d_pos_att, 3)
    d_att_in = sum(contract(q_s[...], piece, 0, 1) for piece in dq_split)
    d_att_in = d_att_in + sum(tn(k_s[...], piece) for piece in dk_split)
    d_att_in = d_att_in + sum(tn(pos_mat[0:8], piece) for piece in d_pos_split)
    d_pos_out = sum(nn(piece, att_in_t) for piece in d_pos_split)
    do_split = split(do_s[...], 2)
    bd_split = split(bd_s[...], 2)
    cross = nt(bd_split[0], do_split[0]) + nt(bd_split[0], do_split[1]) + nt(bd_split[1], do_split[0])
    d_pos_rows = [
        d_pos_out[d : d + 1]
        + row_sum(jnp.where(own_group, cross[d * GROUPS : (d + 1) * GROUPS], 0.0))
        for d in range(3)
    ]
    small = 5 * per_matrix
    pieces_rows = [
        d_att_in.reshape(WIDTH * GROUPS // LANES, LANES),
        d_att_out.reshape(GROUPS * GROUPS // LANES, LANES),
    ]
    along, along_hat, offsets = [], [], []
    for c in range(3):
        one = [jnp.zeros((8, 1), f32) for _ in range(3)]
        for b in range(blocks):
            masked = pmask[b] * rel[b, c : c + 1]
            one[0] = one[0] + lane_sum(dmix[b] * rel[b, c : c + 1])
            one[1] = one[1] + lane_sum(masked * ((pos[b] - mean_p) * rs_p))
            one[2] = one[2] + lane_sum(masked)
        along.append(one[0])
        along_hat.append(one[1])
        offsets.append(one[2])
    stats = collect_a()
    one, two = unfold(stats[0:2]) * inv_points, unfold(stats[2:4]) * inv_points
    ahat = (a1_s[...] - mean_a) * rs_a
    da1 = (gain_a * rs_a * (z_s[...] - point_mask * (one + ahat * two))).astype(bf16)
    put_matrix(0, tn(feat[...], da1))
    one = row_to_col(stats[4:5, 0:8], 8) * inv_pairs
    two = row_to_col(stats[4:5, 8:16], 8) * inv_pairs
    pieces = []
    for c in range(3):
        d_pos_in = gain_p * rs_p * (along[c] - one * offsets[c] - two * along_hat[c])
        pieces.append(col_to_row(d_pos_in, 0)[:, 0:3])
    pieces = pieces + d_pos_rows
    pieces = pieces + [
        gain_grad_a, col_to_row(sqr_p, 0)[:, 0:3], back_w[:, GROUPS : 2 * GROUPS], gain_grad_o,
        shift_grad_a, col_to_row(sum_p, 0)[:, 0:3], back_w[:, 0:GROUPS], shift_grad_o,
        jnp.zeros((1, TAIL_PAD - TAIL_USED), f32),
    ]
    pieces_rows.append(jnp.concatenate(pieces, axis=1).reshape(TAIL_PAD // LANES, LANES))
    used_rows = OFF_TAIL // LANES + TAIL_PAD // LANES - 5 * SQUARE // LANES
    spare_rows = (sliced - small) * 2 * SLICE_ROWS - used_rows
    pieces_rows.append(jnp.zeros((spare_rows, LANES), f32))
    flat[small:sliced] = jnp.concatenate(pieces_rows, axis=0).reshape(
        sliced - small, 2, SLICE_ROWS, LANES
    )
    first_pair, small_pair = exchange(2, 0, per_matrix), exchange(3, small, sliced - small)
    send_group(first_pair)
    send_group(small_pair)
    outs[1] = (dz_s[...] + nt(da1, w_in)).astype(bf16)
    store(outs.at[1], gfeat_h)

    squares = jnp.zeros((1, 1), f32)
    for slot in list(range(1, slots)) + [0]:
        index = slot * half + chip
        if (slot + 1) * half <= sliced:
            here = None
        else:
            here = index < sliced

        def take(slot=slot, index=index):
            got = got16.at[slot, pl.ds(0, half - 1)]
            pltpu.make_async_copy(got, got, rs_rsem.at[slot]).wait()
            total = flat[index, core] + pair_got[index]

            def add(k, total):
                return total + got16[slot, peer(chip, k, half)].astype(f32)

            sums[slot] = lax.fori_loop(1, half, add, total, unroll=half <= 16)

        if here is None:
            take()
        else:
            sums[slot] = jnp.zeros((SLICE_ROWS, LANES), f32)
            pl.when(here)(take)
        squares = squares + lane_sum(row_sum(sums[slot] * sums[slot]))

    collect_norm = all_sum(6, jnp.where(lane == 0, squares, 0.0))

    def slice_of(slot):
        return 2 * (slot * half + chip) + core

    def each_owner(slot, act_on):
        number = slice_of(slot)
        low = number * SLICE // shard_len
        high = jnp.minimum((number * SLICE + SLICE - 1) // shard_len, n - 1)
        for side in range(sides):
            owner = low + side

            @pl.when((number * SLICE < total_len) & (owner <= high))
            def _(owner=owner, side=side):
                act_on(owner, number - owner * shard_len // SLICE, side)

    def owned_rows(k):
        return owned.at[pl.ds(pl.multiple_of(k * SLICE_ROWS, SLICE_ROWS), SLICE_ROWS)]

    def own_copy(slot, owner, k, side):
        return pltpu.make_async_remote_copy(
            src_ref=sums.at[slot],
            dst_ref=owned_rows(k),
            send_sem=own_ssem.at[slot, side],
            recv_sem=own_rsem.at[k],
            device_id=place(owner),
            device_id_type=MESH,
        )

    for slot in range(slots):

        def hand_over(owner, k, side, slot=slot):
            @pl.when(owner != me)
            def _():
                own_copy(slot, owner, k, side).start()

            @pl.when(owner == me)
            def _():
                owned_rows(k)[...] = sums[slot]

        each_owner(slot, hand_over)

    begin = me * shard_len
    first_slice = begin // SLICE
    last_slice = (begin + shard_len - 1) // SLICE
    for k in range(span):
        number = first_slice + k

        @pl.when((number <= last_slice) & (lax.rem(number, n) != me))
        def _(k=k):
            rows = owned.at[pl.ds(k * SLICE_ROWS, SLICE_ROWS)]
            pltpu.make_async_copy(rows, rows, own_rsem.at[k]).wait()

    offset = begin - first_slice * SLICE
    skip = lax.rem(offset, LANES)
    lanes_all = iota((shard_rows, LANES), 1)
    rows = owned[pl.ds(offset // LANES, shard_rows), :]
    turned = pltpu.roll(rows, lax.rem(LANES - skip, LANES), 1)
    below = pltpu.roll(turned, shard_rows - 1, 0)
    grad = jnp.where(lanes_all < LANES - skip, turned, below)
    inside = iota(grad.shape, 0) * LANES + lanes_all < shard_len
    grad = jnp.where(inside, grad, 0.0)

    stats = collect_norm()
    norm = jnp.sqrt(pick(stats, 0))
    norm_s[...] = jnp.broadcast_to(norm, norm_s.shape)
    grad = grad * jnp.minimum(1.0, clip_norm / norm)

    main = shard_len // 1024 * 1024
    spare = shard_len - main
    tail_g[...] = grad.reshape(shard_rows * LANES)
    for start, size in ((0, main), (main, spare)):
        if size == 0:
            continue
        at = pl.ds(start, size)
        p_new, m_new, s_new = adam(state[0][at], state[1][at], state[2][at], tail_g[at])
        news[0][at] = p_new
        news[1][at] = m_new
        news[2][at] = s_new
        tail_g[at] = p_new
    moved = jnp.where(inside, tail_g[...].reshape(shard_rows, LANES), 0.0)
    turned = pltpu.roll(moved, skip, 1)
    above = pltpu.roll(turned, 1, 0)
    slab_f[...] = jnp.zeros(slab_f.shape, f32)
    slab_f[pl.ds(lax.rem(begin, CHUNK) // LANES, shard_rows), :] = jnp.where(
        lanes_all < skip, above, turned
    )
    shard_w[...] = slab_f[...].astype(bf16)
    all_w[core, chip] = slab_f[...].astype(bf16)

    def send_new(k, carry):
        pltpu.make_async_remote_copy(
            src_ref=shard_w,
            dst_ref=all_w.at[core, chip],
            send_sem=ag_ssem,
            recv_sem=ag_rsem.at[chip],
            device_id=place(2 * peer(chip, k, half) + core),
            device_id_type=MESH,
        ).start()
        return carry

    lax.fori_loop(1, half, send_new, 0)
    store(norm_s, gnorm_h)
    for source, target in ((0, new_master_h), (1, new_first_h), (2, new_second_h)):
        store(news[source], target)

    def forward(other):
        return pltpu.make_async_remote_copy(
            src_ref=all_w.at[core, other],
            dst_ref=all_w.at[core, other],
            send_sem=fw_ssem,
            recv_sem=fw_rsem,
            device_id=sibling,
            device_id_type=MESH,
        )

    forward(chip).start()

    def pass_on(k, carry):
        other = peer(chip, half - k, half)
        pltpu.make_async_copy(shard_w, shard_w, ag_rsem.at[other]).wait()
        forward(other).start()
        return carry

    lax.fori_loop(1, half, pass_on, 0)
    pltpu.make_async_copy(all_w.at[core], all_w.at[core], fw_rsem).wait()
    store(all_w, slabs_h)

    for index, rows in sent:
        drain_stats(index, rows)
    for copy in stores:
        copy.wait()
    pltpu.make_async_copy(all_w.at[core], all_w.at[core], fw_ssem).wait()
    rest = all_w.at[core, pl.ds(0, half - 1)]
    pltpu.make_async_copy(rest, rest, ag_ssem).wait()
    for slot in range(slots):
        count = min(sliced - slot * half, half)

        def drain(k, carry, slot=slot):
            pltpu.make_async_copy(part16.at[0], part16.at[0], rs_ssem.at[slot]).wait()
            return carry

        lax.fori_loop(0, count - (chip < count).astype(jnp.int32), drain, 0)

        def own_drain(owner, k, side, slot=slot):
            @pl.when(owner != me)
            def _():
                own_copy(slot, owner, k, side).wait_send()

        each_owner(slot, own_drain)


def finish_kernel(
    n, shard_len,
    out_t, gfeat_t, gnorm_t, master_t, first_t, second_t, slabs_t,
    out_h, gfeat_h, gnorm, master_h, first_h, second_h, weights_h,
    out, gfeat, norm_s, master, first, second, slabs, joined, in_sem, out_sem,
):
    loads = [
        pltpu.make_async_copy(source, target, in_sem.at[k])
        for k, (source, target) in enumerate(
            (
                (slabs_t, slabs),
                (out_t, out),
                (gfeat_t, gfeat),
                (master_t, master),
                (first_t, first),
                (second_t, second),
                (gnorm_t, norm_s),
            )
        )
    ]
    stores = [
        pltpu.make_async_copy(source, target, out_sem.at[k])
        for k, (source, target) in enumerate(
            (
                (joined, weights_h),
                (out, out_h),
                (gfeat, gfeat_h),
                (master, master_h),
                (first, first_h),
                (second, second_h),
            )
        )
    ]
    for copy in loads:
        copy.start()
    for k in range(1, 6):
        loads[k].wait()
        stores[k].start()
    loads[6].wait()
    gnorm[...] = norm_s[0:1, 0:1]
    loads[0].wait()
    total_len = joined.shape[0]
    rows = CHUNK // LANES

    def chunk(c):
        value = None
        for owner in range(c * CHUNK // shard_len, min((c * CHUNK + CHUNK - 1) // shard_len, n - 1) + 1):
            k = c - owner * shard_len // CHUNK
            part = slabs[owner % 2, owner // 2, rows * k : rows * (k + 1)].astype(f32)
            value = part if value is None else value + part
        return value

    whole = total_len // (2 * CHUNK)
    for c in range(whole):
        both = jnp.concatenate([chunk(2 * c), chunk(2 * c + 1)], axis=0)
        joined[pl.ds(2 * CHUNK * c, 2 * CHUNK)] = both.astype(bf16).reshape(2 * CHUNK)
    left = total_len - whole * 2 * CHUNK
    if left:
        parts = [chunk(2 * whole)]
        parts.append(chunk(2 * whole + 1) if left > CHUNK else jnp.zeros((rows, LANES), f32))
        both = jnp.concatenate(parts, axis=0).astype(bf16).reshape(2 * CHUNK)
        joined[pl.ds(2 * CHUNK * whole, left)] = both[0:left]
    stores[0].start()
    for copy in stores:
        copy.wait()


def lane_slots(value):
    return functools.reduce(
        jnp.add, [value[:, j * LANES : (j + 1) * LANES] for j in range(NEAREST)]
    )


def shards(
    n_rows, n_cols,
    features, coords, valid_mask, neighbors, cotangent, weights, master, first_moment, second_moment,
):
    n = n_rows * n_cols
    half = n // 2
    points = features.shape[0]
    blocks = points // LANES
    shard_len = master.shape[0]
    total_len = weights.shape[0]

    def up(value, unit):
        return -(-value // unit) * unit

    shard_rows = up(-(-shard_len // LANES) + 1, 8)
    slab_rows = up(shard_rows + CHUNK // LANES, 16)
    sliced = up(-(-total_len // SLICE), 2) // 2
    slots = -(-sliced // half)
    sides = (SLICE + shard_len - 2) // shard_len + 1
    span = (SLICE + shard_len - 2) // SLICE + 1
    hbm = pl.BlockSpec(memory_space=pltpu.HBM)
    vmem = pl.BlockSpec(memory_space=pltpu.VMEM)
    dma = pltpu.SemaphoreType.DMA
    shape = jax.ShapeDtypeStruct

    def pairs(rows, dtype=f32):
        return pltpu.VMEM((blocks, rows, PAIRS), dtype)

    def shard():
        return [pltpu.VMEM(master.shape, f32) for _ in range(3)]

    scratch = [
        pltpu.VMEM(features.shape, bf16),
        pltpu.VMEM(coords.shape, f32),
        pltpu.VMEM(valid_mask.shape, jnp.int32),
        pltpu.VMEM(neighbors.shape, jnp.int32),
        pltpu.VMEM(features.shape, bf16),
        pltpu.VMEM((SQUARE,), bf16),
        pltpu.VMEM((1024,), bf16),
        pltpu.VMEM(weights.shape, bf16),
        shard(),
        shard(),
        pltpu.VMEM((2, *features.shape), bf16),
        pltpu.VMEM((1, LANES), f32),
        dma((11,)),
        dma((7,)),
        pltpu.VMEM((7, 8, LANES), f32),
        pltpu.VMEM((7, n, 8, LANES), f32),
        dma((7,)),
        dma((7,)),
        pltpu.VMEM((TAIL_PAD,), bf16),
        pltpu.VMEM((5, WIDTH, WIDTH), bf16),
        pairs(WINDOW, bf16),
        pairs(WIDTH),
        pairs(GROUPS),
        pairs(GROUPS),
        pairs(GROUPS, bf16),
        pairs(GROUPS),
        pairs(8),
        pairs(8),
        pairs(8),
        pairs(8),
        pairs(8),
        pairs(8),
        pltpu.VMEM((points, WIDTH), f32),
        pltpu.VMEM((points, WIDTH), f32),
        pltpu.VMEM((points, WIDTH), bf16),
        pltpu.VMEM((points, WIDTH), bf16),
        pltpu.VMEM((points, WIDTH), bf16),
        pltpu.VMEM((WIDTH, points), bf16),
        pltpu.VMEM((WIDTH, points), f32),
        pltpu.VMEM((points, WIDTH), f32),
        pltpu.VMEM((points, GROUPS), f32),
        pltpu.VMEM((3 * GROUPS, points), f32),
        pltpu.VMEM((WIDTH, PAIRS), bf16),
        pltpu.VMEM((points, WIDTH), f32),
        pltpu.VMEM((points, WIDTH), bf16),
        pltpu.VMEM((sliced, 2, SLICE_ROWS, LANES), f32),
        pltpu.VMEM((sliced, SLICE_ROWS, LANES), f32),
        pltpu.VMEM((sliced, SLICE_ROWS, LANES), bf16),
        pltpu.VMEM((slots, half, SLICE_ROWS, LANES), bf16),
        pltpu.VMEM((slots, SLICE_ROWS, LANES), f32),
        pltpu.VMEM((up(max(span * SLICE_ROWS, SLICE_ROWS + shard_rows), SLICE_ROWS), LANES), f32),
        pltpu.VMEM((shard_rows * LANES,), f32),
        pltpu.VMEM((slab_rows, LANES), f32),
        pltpu.VMEM((slab_rows, LANES), bf16),
        pltpu.VMEM((2, half, slab_rows, LANES), bf16),
        dma((4,)),
        dma((4,)),
        dma((slots,)),
        dma((slots,)),
        dma((slots, sides)),
        dma((span,)),
        dma,
        dma((half,)),
        dma,
        dma,
    ]
    results = pl.pallas_call(
        functools.partial(block_kernel, n_rows, n_cols),
        out_shape=(
            shape(features.shape, bf16),
            shape(features.shape, bf16),
            shape((1, LANES), f32),
            shape(master.shape, f32),
            shape(master.shape, f32),
            shape(master.shape, f32),
            shape((2, half, slab_rows, LANES), bf16),
        ),
        in_specs=[hbm] * 9,
        out_specs=[hbm] * 7,
        scratch_shapes=scratch,
        compiler_params=pltpu.CompilerParams(
            collective_id=0, has_side_effects=True, vmem_limit_bytes=56 * 2**20
        ),
    )(features, coords, valid_mask, neighbors, cotangent, weights, master, first_moment, second_moment)
    results = pl.pallas_call(
        functools.partial(finish_kernel, n, shard_len),
        out_shape=(
            shape(features.shape, bf16),
            shape(features.shape, bf16),
            shape((1, 1), f32),
            shape(master.shape, f32),
            shape(master.shape, f32),
            shape(master.shape, f32),
            shape(weights.shape, bf16),
        ),
        in_specs=[hbm] * 7,
        out_specs=[hbm, hbm, vmem, hbm, hbm, hbm, hbm],
        scratch_shapes=[
            pltpu.VMEM(features.shape, bf16),
            pltpu.VMEM(features.shape, bf16),
            pltpu.VMEM((1, LANES), f32),
            pltpu.VMEM(master.shape, f32),
            pltpu.VMEM(master.shape, f32),
            pltpu.VMEM(master.shape, f32),
            pltpu.VMEM((2, half, slab_rows, LANES), bf16),
            pltpu.VMEM(weights.shape, bf16),
            dma((7,)),
            dma((6,)),
        ],
        compiler_params=pltpu.CompilerParams(vmem_limit_bytes=62 * 2**20),
    )(*results)
    return results[0], results[1], results[2].reshape(()), *results[3:]


def solution(mesh):
    both = ("rows", "cols")
    rows_split, cols_split, flat_split = P(both, None), P(None, both), P(both)
    return jax.shard_map(
        functools.partial(shards, mesh.shape["rows"], mesh.shape["cols"]),
        mesh=mesh,
        in_specs=(
            rows_split, cols_split, flat_split, cols_split, rows_split, P(),
            flat_split, flat_split, flat_split,
        ),
        out_specs=(rows_split, rows_split, P(), flat_split, flat_split, flat_split, P()),
        check_vma=False,
    )
```

time: 1040 us -> 76.4 us (0.07)
  local copies, waits for them, and re-layouts: 328 us -> 0 us
  waiting for transfers between devices: 260 us -> 0 us
  blocking collectives: 242 us -> 0 us
  other arithmetic: 136 us -> 0 us
  Pallas kernels: 0 us -> 75.4 us
  matrix products: 48.8 us -> 0 us
  between operations: 17.4 us -> 0.8 us
    psum x6 -> x0, blocking collectives: 242 us -> none  [the longest x1 41.1 us: shards(): lax.psum((jnp.sum(point_mask * pre_one, axis=0), jnp.sum(point_mask * pre...]
    gather x9 -> x0, local copies, waits for them, and re-layouts: 165 us -> none  [the longest x3 51.4 us: shards(): neighbor_valid = valid_rows[neighbor_rows]]
    psum x1 -> x0, waiting for transfers between devices: 133 us -> none  [shards(): total_grads = lax.psum(local_grads, ('rows', 'cols'))]
    unnamed x3 -> x0, waiting for transfers between devices: 127 us -> none
    scatter-add x2 -> x0, other arithmetic: 89.8 us -> none  [the longest x1 45 us: piece_relation(): return query_rows[:, None, :] - key_all[neighbor_rows] + encode_rows]
    pallas_call x0 -> x2, Pallas kernels: none -> 75.4 us  [the longest x1 72.6 us: shards(): pl.pallas_call(functools.partial(block_kernel, n_rows, n_cols), out_shape...]
    reshape x12 -> x0, local copies, waits for them, and re-layouts: 74.2 us -> none  [the longest x3 73 us: piece_mix(): (value_rows[neighbor_rows] + encode_rows).reshape(points, NEAREST, GROUPS...]
    dot_general x26 -> x0, matrix products: 48.8 us -> none  [the longest x3 23 us: piece_encode(): return jnp.einsum('cpk,cd->pkd', pos_act, w_enc, precision=highest)]
  transfers between devices with their start and end apart: 2 -> 0, of which waited for: 2 -> 0; matrix products, arithmetic and copies ran while one was open for 0% -> 0% of each run, Pallas kernels for 0% -> 0%
where the time goes in v1:
time: 76.4 us; the launch traced here: 76.2 us
  Pallas kernels  75.4 us (99%)
  between operations  0.8 us (1%)
    pallas_call x1, Pallas kernels, shards(): pl.pallas_call(functools.partial(block_kernel, n_rows, n_cols), out_shape...  72.6 us
    pallas_call x1, Pallas kernels, shards(): pl.pallas_call(functools.partial(finish_kernel, n, shard_len), out_shape=...  2.88 us

profile of v1, /device:TPU:1, one launch (start us, length us, event | category | flops | bytes accessed | tf_op | source)
XLA Modules:
  0.0 76.2 jit_solution(15357105249278909640)
XLA Ops:
  0.6 72.6 %shard_map.144 = (bf16[512,256]{1,0:T(8,128)(2,1)}, bf16[512,256]{1,0:T(8,128)(2,1)}, f32[1,128]{1,0:T(1,128)}, f32[10587]{0:T(1024)}, f32[10587]{0:T(1024)}, /*...) custom-call(bf16[512,256]{1,0:T(8,128)(2,1)} %feat_h.1, f32[3,512]{1,0:T(4,128)} %coords_h.1, s32[512]{0:T(512)} %valid_h.1, ...), custom_call_target="tpu_custom_call" | custom-call | tf_op jit(solution)/shard_map/pallas_call | solution.py:1015
  73.2 2.9 %shard_map.145 = (bf16[512,256]{1,0:T(8,128)(2,1)}, bf16[512,256]{1,0:T(8,128)(2,1)}, f32[1,1]{1,0:T(1,128)}, f32[10587]{0:T(1024)}, f32[10587]{0:T(1024)}, /*index=5*/f32[10587]{0:T(1024)}, bf16[338784]{0:T(1024)(128)(2,1)}) custom-call(bf16[512,256]{1,0:T(8,128)(2,1)} %get-tuple-element.21.out_t, bf16[512,256]{1,0:T(8,128)(2,1)} %get-tuple-element.22.gfeat_t, ...), custom_call_target="tpu_custom_call" | custom-call | tf_op jit(solution)/shard_map/pallas_call | solution.py:1033

commit v2 on v1

--- a/solution.py
+++ b/solution.py
@@ -133,11 +133,11 @@
 def block_kernel(
     n_rows, n_cols,
     feat_h, coords_h, valid_h, nbrs_h, cot_h, weights_h, master_h, first_h, second_h,
-    out_h, gfeat_h, gnorm_h, new_master_h, new_first_h, new_second_h, slabs_h,
+    out_h, gfeat_h, gnorm_h, new_master_h, new_first_h, new_second_h, weights_out,
     feat, coords, valid, nbrs, cot, w_first, pos_first, weights, state, news, outs, norm_s, in_sem, out_sem,
     stat_send, stat_buf, stat_ssem, stat_rsem,
     tail1d, mats, onehot, vgat, att, wpre, uact, dyw, rel, pos, act, pmask, allow, dmix,
-    a1_s, z_s, h_s, q_s, k_s, o_s, do_s, dv_s, sk_s, bd_s, xs, dz_s, dz16,
+    a1_s, z_s, h_s, h_ts, q_s, k_s, ba_s, o_s, do_s, dv_s, sk_s, bd_s, dp_s, ds_s, xs, dz_s, dz16,
     flat, pair_got, part16, got16, sums, owned, tail_g, slab_f, shard_w, all_w,
     pair_ssem, pair_rsem, rs_ssem, rs_rsem, own_ssem, own_rsem, ag_ssem, ag_rsem, fw_ssem, fw_rsem,
 ):
@@ -161,6 +161,13 @@
     def place(device):
         return (device // n_cols, lax.rem(device, n_cols))
 
+    barrier = pltpu.get_barrier_semaphore()
+
+    def greet(k, carry):
+        pl.semaphore_signal(barrier, inc=1, device_id=place(peer(me, k, n)), device_id_type=MESH)
+        return carry
+
+    lax.fori_loop(1, n, greet, 0)
     loads = []
 
     def load(source, target):
@@ -185,13 +192,6 @@
         load(valid_h, valid),
     ]
 
-    barrier = pltpu.get_barrier_semaphore()
-
-    def greet(k, carry):
-        pl.semaphore_signal(barrier, inc=1, device_id=place(peer(me, k, n)), device_id_type=MESH)
-        return carry
-
-    lax.fori_loop(1, n, greet, 0)
     late = [load(weights_h, weights), load(cot_h, cot)]
     for source, target in ((master_h, 0), (first_h, 1), (second_h, 2)):
         late.append(load(source, state[target]))
@@ -392,6 +392,19 @@
     gain_p, shift_p = pad_col(gain_p), pad_col(shift_p)
     gain_w, shift_w = row_to_col(gain_w, GROUPS), row_to_col(shift_w, GROUPS)
 
+    new_at = iota((WIDTH, WIDTH), 0)
+    reorder = jnp.where(
+        iota((WIDTH, WIDTH), 1) == new_at % GROUPS * PER_GROUP + new_at // GROUPS, 1.0, 0.0
+    ).astype(bf16)
+    w_o_new = nn(reorder, w_o)
+    mats[4] = w_o_new.astype(bf16)
+    mats[5] = w_o_new.T.astype(bf16)
+    mats[6] = w_q.astype(f32).T.astype(bf16)
+    mats[7] = w_k.astype(f32).T.astype(bf16)
+    mats[8] = nt(reorder, w_v).astype(bf16)
+    pos_mat = jnp.concatenate(pos_rows + [jnp.zeros((13, WIDTH), f32)], axis=0).astype(bf16)
+    pos_cols = nt(reorder, pos_mat)
+    pos_cols = [pos_cols[:, d : d + 1] for d in range(3)]
     stats = collect_first()
 
     def pick(row, at):
@@ -409,17 +422,21 @@
         row_to_col(stats[4:5, 0:8], 8), row_to_col(stats[4:5, 8:16], 8), inv_pairs
     )
 
-    h = silu_parts((a1_s[...] - mean_a) * rs_a * gain_a + shift_a)[0].astype(bf16)
-    h_s[...] = h
-    q = nn(h, w_q).astype(bf16)
-    k = nn(h, w_k).astype(bf16)
-    q_s[...] = q
-    k_s[...] = k
-    q_att = nt(att_in_t, q)
-    k_att = jnp.concatenate(split(nt(att_in_t, k), 3), axis=0)
-    pos_mat = jnp.concatenate(pos_rows + [jnp.zeros((13, WIDTH), f32)], axis=0).astype(bf16)
+    h = silu_parts((a1_s[...] - mean_a) * rs_a * gain_a + shift_a)[0]
+    h_s[...] = h.astype(bf16)
+    h_t = h.T.astype(bf16)
+    q_t = nn(mats[6], h_t).astype(bf16)
+    k_t = nn(mats[7], h_t).astype(bf16)
+    q_s[...] = q_t
+    k_s[...] = k_t
+    h_ts[...] = h_t
+    q_att = nn(att_in_t, q_t)
+    k_att = jnp.concatenate(split(nn(att_in_t, k_t), 3), axis=0)
     pos_att = nt(att_in_t, pos_mat)
     pos_att_cols = [pos_att[:, d : d + 1] for d in range(3)]
+    back_att = jnp.concatenate([nn(att_in_t, mats[6]), nn(att_in_t, mats[7])], axis=0)
+    for k, piece in enumerate(split(back_att, 2)):
+        ba_s[k] = piece
 
     sum_w = jnp.zeros((GROUPS, LANES), f32)
     sqr_w = jnp.zeros((GROUPS, LANES), f32)
@@ -444,7 +461,7 @@
         return col_to_row(one, 0) + col_to_row(two, GROUPS)
 
     collect_w = all_sum(1, pair_row(sum_w, sqr_w))
-    v_t = nn(h, w_v).T.astype(bf16)
+    v_t = nn(mats[8], h_ts[...]).astype(bf16)
     for b in range(blocks):
         vgat[b] = nn(v_t[:, starts[b] : starts[b] + WINDOW], onehot[b])
     stats = collect_w()
@@ -454,14 +471,13 @@
         inv_pairs,
     )
 
-    group_of = iota((WIDTH, 2 * GROUPS), 0) // PER_GROUP
-    spread = jnp.where(group_of == iota((WIDTH, 2 * GROUPS), 1) % GROUPS, 1.0, 0.0).astype(bf16)
-    own_group = iota((GROUPS, WIDTH), 1) // PER_GROUP == iota((GROUPS, WIDTH), 0)
-    gather_groups = jnp.where(own_group, 1.0, 0.0).astype(bf16)
-    pos_spread = jnp.concatenate(
-        [jnp.where(own_group, jnp.broadcast_to(pos_rows[d], (GROUPS, WIDTH)), 0.0) for d in range(3)],
-        axis=0,
-    ).astype(bf16)
+    def each_channel(value):
+        return jnp.concatenate([value] * PER_GROUP, axis=0)
+
+    def over_channels(value):
+        return functools.reduce(
+            jnp.add, [value[c * GROUPS : (c + 1) * GROUPS] for c in range(PER_GROUP)]
+        )
 
     def cols(j):
         return slice(j * LANES, (j + 1) * LANES)
@@ -481,17 +497,15 @@
         enc = [jnp.zeros((GROUPS, LANES), f32) for _ in range(3)]
         for j in range(NEAREST):
             a = att[b, :, cols(j)]
-            wide = nn(spread, jnp.concatenate(split(a, 2), axis=0))
-            mixed = mixed + wide * vgat[b, :, cols(j)]
+            mixed = mixed + each_channel(a) * vgat[b, :, cols(j)]
             for d in range(3):
                 enc[d] = enc[d] + a * act[b, d : d + 1, cols(j)]
-        enc = jnp.concatenate(enc, axis=0)
-        bd_s[:, here] = enc
-        for piece in split(enc, 3):
-            mixed = mixed + tn(pos_spread, piece)
-        o_s[:, here] = mixed.astype(bf16)
-
-    z = tn(o_s[...], w_o)
+        bd_s[:, here] = jnp.concatenate(enc, axis=0)
+        for d in range(3):
+            mixed = mixed + pos_cols[d] * each_channel(enc[d])
+        o_s[here, :] = mixed.T.astype(bf16)
+
+    z = nn(o_s[...], mats[4])
     z_s[...] = z
     masked = point_mask * z
     collect_o = all_sum(2, jnp.concatenate([fold(row_sum(masked)), fold(row_sum(masked * z))], axis=0))
@@ -511,36 +525,26 @@
     zhat = (z_s[...] - mean_o) * rs_o
     dz = (gain_o * rs_o * (dz_s[...] - point_mask * (one + zhat * two))).astype(bf16)
     dz16[...] = dz
-    do_s[...] = nt(w_o, dz)
-    dv_s[...] = jnp.zeros(dv_s.shape, f32)
+    do_s[...] = nn(dz, mats[5]).T
 
     sum_w = jnp.zeros((GROUPS, LANES), f32)
     sqr_w = jnp.zeros((GROUPS, LANES), f32)
-    d_att_out = jnp.zeros((GROUPS, GROUPS), f32)
     for b in range(blocks):
         here = slice(b * LANES, (b + 1) * LANES)
         do = do_s[:, here]
-        do_pos = sum(nn(pos_spread, piece) for piece in split(do, 2))
-        da, mix = [], []
+        do_pos = [over_channels(do * pos_cols[d]) for d in range(3)]
+        dp_s[:, here] = jnp.concatenate(do_pos, axis=0)
+        da = []
         for j in range(NEAREST):
-            a = att[b, :, cols(j)]
-            wide = nn(spread, jnp.concatenate(split(a, 2), axis=0))
-            xs[:, cols(j)] = (wide * do).astype(bf16)
-            grad = nn(gather_groups, (vgat[b, :, cols(j)] * do).astype(bf16))
-            back = []
+            grad = over_channels(do * vgat[b, :, cols(j)])
             for d in range(3):
-                part = do_pos[d * GROUPS : (d + 1) * GROUPS]
-                grad = grad + part * act[b, d : d + 1, cols(j)]
-                back.append(row_sum(part * a))
+                grad = grad + do_pos[d] * act[b, d : d + 1, cols(j)]
             da.append(grad)
-            mix.append(jnp.concatenate(back + [jnp.zeros((5, LANES), f32)], axis=0))
-        dmix[b] = jnp.concatenate(mix, axis=1)
-        dv_s[pl.ds(starts[b], WINDOW)] += nt(onehot[b], xs[...])
         mean_da = functools.reduce(jnp.add, [da[j] * att[b, :, cols(j)] for j in range(NEAREST)])
         ds = jnp.concatenate(
             [att[b, :, cols(j)] * (da[j] - mean_da) for j in range(NEAREST)], axis=1
         ).astype(bf16)
-        d_att_out = d_att_out + nt(uact[b], ds)
+        ds_s[b] = ds
         what = (wpre[b] - mean_w) * rs_w
         y = what * gain_w + shift_w
         gate = silu_parts(y)[1]
@@ -551,10 +555,28 @@
 
     back_w = pair_row(sum_w, sqr_w)
     collect_w = all_sum(4, back_w)
-    dv = dv_s[...].astype(bf16)
-    put_matrix(4, nn(o_s[...], dz16[...]))
+    put_matrix(4, tn(nn(o_s[...], reorder).astype(bf16), dz16[...]))
+    dv_s[...] = jnp.zeros(dv_s.shape, f32)
+    for b in range(blocks):
+        here = slice(b * LANES, (b + 1) * LANES)
+        do = do_s[:, here]
+        for j in range(NEAREST):
+            xs[:, cols(j)] = (each_channel(att[b, :, cols(j)]) * do).astype(bf16)
+        dv_s[pl.ds(starts[b], WINDOW)] += nt(onehot[b], xs[...])
+    dv = nn(dv_s[...].astype(bf16), reorder).astype(bf16)
     put_matrix(3, tn(h_s[...], dv))
-    late_pair = exchange(0, 3 * 16, 2 * 16)
+    late_pair = exchange(0, 3 * per_matrix, 2 * per_matrix)
+    dv_s[...] = nt(dv, w_v)
+    d_att_out = jnp.zeros((GROUPS, GROUPS), f32)
+    for b in range(blocks):
+        here = slice(b * LANES, (b + 1) * LANES)
+        d_att_out = d_att_out + nt(uact[b], ds_s[b])
+        mix = []
+        for j in range(NEAREST):
+            a = att[b, :, cols(j)]
+            back = [row_sum(dp_s[d * GROUPS : (d + 1) * GROUPS, here] * a) for d in range(3)]
+            mix.append(jnp.concatenate(back + [jnp.zeros((5, LANES), f32)], axis=0))
+        dmix[b] = jnp.concatenate(mix, axis=1)
     send_group(late_pair)
     stats = collect_w()
     one = row_to_col(stats[:, 0:GROUPS], GROUPS) * inv_pairs
@@ -564,7 +586,6 @@
     pos_att_rows = split(pos_att[:, 0:8].T, 3)
     pos_att_rows = jnp.concatenate(pos_att_rows, axis=0)
     dw_sums = []
-    d_pos_att = jnp.zeros((24, GROUPS), f32)
     sum_p = jnp.zeros((8, 1), f32)
     sqr_p = jnp.zeros((8, 1), f32)
     for b in range(blocks):
@@ -573,8 +594,7 @@
         dw = dw_f.astype(bf16)
         sk_s[pl.ds(starts[b], WINDOW)] += nt(onehot[b], dw)
         dw_sums.append(lane_slots(dw.astype(f32)))
-        active = act[b]
-        d_pos_att = d_pos_att + nt(jnp.concatenate(split(active, 3), axis=0), dw)
+        ds_s[b] = dw
         back = nn(pos_att_rows, dw)
         d_act = dmix[b] + back[0:8] + back[8:16] + back[16:24]
         phat = (pos[b] - mean_p) * rs_p
@@ -585,11 +605,10 @@
         sum_p = sum_p + lane_sum(dy)
         sqr_p = sqr_p + lane_sum(dy * phat)
     dq_att = jnp.concatenate(dw_sums, axis=1)
-    dq_split = split(dq_att, 2)
-    dk_split = split(-sk_s[...], 2)
-    dq = sum(tn(piece, att_in_t) for piece in dq_split).astype(bf16)
-    dk = sum(nn(piece, att_in_t) for piece in dk_split).astype(bf16)
-    dh = nt(dq, w_q) + nt(dk, w_k) + nt(dv, w_v)
+    both_att = jnp.concatenate([dq_att.T, -sk_s[...]], axis=1)
+    both_split = split(both_att, 2)
+    dh = nn(both_split[0], ba_s[0]) + nn(both_split[1], ba_s[0]) + nn(both_split[0], ba_s[1])
+    dh = dh + dv_s[...]
     ahat = (a1_s[...] - mean_a) * rs_a
     y = ahat * gain_a + shift_a
     gate = silu_parts(y)[1]
@@ -601,23 +620,32 @@
         5, jnp.concatenate([fold(shift_grad_a), fold(gain_grad_a), last], axis=0)
     )
 
+    dq_split = split(dq_att, 2)
+    dk_split = [piece[:, GROUPS : 2 * GROUPS] for piece in both_split]
+    dq = sum(tn(piece, att_in_t) for piece in dq_split).astype(bf16)
+    dk = sum(nn(piece, att_in_t) for piece in dk_split).astype(bf16)
     put_matrix(1, tn(h_s[...], dq))
     put_matrix(2, tn(h_s[...], dk))
     send_group(exchange(1, per_matrix, 2 * per_matrix))
+    d_pos_att = sum(
+        nt(jnp.concatenate(split(act[b], 3), axis=0), ds_s[b]) for b in range(blocks)
+    )
     d_pos_att = d_pos_att[0:8] + d_pos_att[8:16] + d_pos_att[16:24]
     d_pos_split = split(d_pos_att, 3)
-    d_att_in = sum(contract(q_s[...], piece, 0, 1) for piece in dq_split)
-    d_att_in = d_att_in + sum(tn(k_s[...], piece) for piece in dk_split)
+    d_att_in = sum(nt(q_s[...], piece) for piece in dq_split)
+    d_att_in = d_att_in + sum(nn(k_s[...], piece) for piece in dk_split)
     d_att_in = d_att_in + sum(tn(pos_mat[0:8], piece) for piece in d_pos_split)
     d_pos_out = sum(nn(piece, att_in_t) for piece in d_pos_split)
     do_split = split(do_s[...], 2)
     bd_split = split(bd_s[...], 2)
     cross = nt(bd_split[0], do_split[0]) + nt(bd_split[0], do_split[1]) + nt(bd_split[1], do_split[0])
-    d_pos_rows = [
-        d_pos_out[d : d + 1]
-        + row_sum(jnp.where(own_group, cross[d * GROUPS : (d + 1) * GROUPS], 0.0))
-        for d in range(3)
+    own_group = iota((GROUPS, WIDTH), 1) % GROUPS == iota((GROUPS, WIDTH), 0)
+    cross = [
+        row_sum(jnp.where(own_group, cross[d * GROUPS : (d + 1) * GROUPS], 0.0)) for d in range(3)
     ]
+    cross = jnp.concatenate(cross + [jnp.zeros((5, WIDTH), f32)], axis=0)
+    d_pos_out = d_pos_out + sum(nn(piece, reorder) for piece in split(cross, 3))
+    d_pos_rows = [d_pos_out[d : d + 1] for d in range(3)]
     small = 5 * per_matrix
     pieces_rows = [
         d_att_in.reshape(WIDTH * GROUPS // LANES, LANES),
@@ -639,6 +667,7 @@
     ahat = (a1_s[...] - mean_a) * rs_a
     da1 = (gain_a * rs_a * (z_s[...] - point_mask * (one + ahat * two))).astype(bf16)
     put_matrix(0, tn(feat[...], da1))
+    first_pair = exchange(2, 0, per_matrix)
     one = row_to_col(stats[4:5, 0:8], 8) * inv_pairs
     two = row_to_col(stats[4:5, 8:16], 8) * inv_pairs
     pieces = []
@@ -658,7 +687,7 @@
     flat[small:sliced] = jnp.concatenate(pieces_rows, axis=0).reshape(
         sliced - small, 2, SLICE_ROWS, LANES
     )
-    first_pair, small_pair = exchange(2, 0, per_matrix), exchange(3, small, sliced - small)
+    small_pair = exchange(3, small, sliced - small)
     send_group(first_pair)
     send_group(small_pair)
     outs[1] = (dz_s[...] + nt(da1, w_in)).astype(bf16)
@@ -779,43 +808,92 @@
     shard_w[...] = slab_f[...].astype(bf16)
     all_w[core, chip] = slab_f[...].astype(bf16)
 
-    def send_new(k, carry):
+    in_row = n_cols // 2
+    row_chip = col_id // 2
+
+    def send_slab(source, slab, row, chip_in_row):
         pltpu.make_async_remote_copy(
-            src_ref=shard_w,
-            dst_ref=all_w.at[core, chip],
+            src_ref=source,
+            dst_ref=all_w.at[core, slab],
             send_sem=ag_ssem,
-            recv_sem=ag_rsem.at[chip],
-            device_id=place(2 * peer(chip, k, half) + core),
+            recv_sem=ag_rsem.at[slab],
+            device_id=(row, 2 * chip_in_row + core),
             device_id_type=MESH,
         ).start()
-        return carry
-
-    lax.fori_loop(1, half, send_new, 0)
-    store(norm_s, gnorm_h)
-    for source, target in ((0, new_master_h), (1, new_first_h), (2, new_second_h)):
-        store(news[source], target)
 
     def forward(other):
-        return pltpu.make_async_remote_copy(
+        pltpu.make_async_remote_copy(
             src_ref=all_w.at[core, other],
             dst_ref=all_w.at[core, other],
             send_sem=fw_ssem,
             recv_sem=fw_rsem,
             device_id=sibling,
             device_id_type=MESH,
-        )
-
-    forward(chip).start()
+        ).start()
+
+    def arrived(other):
+        pltpu.make_async_copy(shard_w, shard_w, ag_rsem.at[other]).wait()
+
+    def send_along(k, carry):
+        send_slab(shard_w, chip, peer(row_id, k, n_rows), row_chip)
+        return carry
+
+    def send_within(k, carry):
+        send_slab(shard_w, chip, row_id, peer(row_chip, k, in_row))
+        return carry
+
+    lax.fori_loop(1, n_rows, send_along, 0)
+    lax.fori_loop(1, in_row, send_within, 0)
+    forward(chip)
+    store(norm_s, gnorm_h)
+    for source, target in ((0, new_master_h), (1, new_first_h), (2, new_second_h)):
+        store(news[source], target)
+
+    def spread_row(k, carry):
+        other = peer(row_id, n_rows - k, n_rows) * in_row + row_chip
+        arrived(other)
+
+        def send_on(i, carry):
+            send_slab(all_w.at[core, other], other, row_id, peer(row_chip, i, in_row))
+            return carry
+
+        lax.fori_loop(1, in_row, send_on, 0)
+        forward(other)
+        return carry
+
+    lax.fori_loop(1, n_rows, spread_row, 0)
 
     def pass_on(k, carry):
-        other = peer(chip, half - k, half)
-        pltpu.make_async_copy(shard_w, shard_w, ag_rsem.at[other]).wait()
-        forward(other).start()
+        step = k // (in_row - 1)
+        row = jnp.where(step == 0, row_id, peer(row_id, n_rows - step, n_rows))
+        other = row * in_row + peer(row_chip, in_row - 1 - lax.rem(k, in_row - 1), in_row)
+        arrived(other)
+        forward(other)
         return carry
 
-    lax.fori_loop(1, half, pass_on, 0)
+    lax.fori_loop(0, n_rows * (in_row - 1), pass_on, 0)
     pltpu.make_async_copy(all_w.at[core], all_w.at[core], fw_rsem).wait()
-    store(all_w, slabs_h)
+    rows = CHUNK // LANES
+
+    def chunk(c):
+        value = None
+        last_owner = min((c * CHUNK + CHUNK - 1) // shard_len, n - 1)
+        for owner in range(c * CHUNK // shard_len, last_owner + 1):
+            k = c - owner * shard_len // CHUNK
+            part = all_w[owner % 2, owner // 2, rows * k : rows * (k + 1)].astype(f32)
+            value = part if value is None else value + part
+        return value
+
+    whole = total_len // (2 * CHUNK)
+    for c in range(whole):
+        both = jnp.concatenate([chunk(2 * c), chunk(2 * c + 1)], axis=0)
+        weights_out[pl.ds(2 * CHUNK * c, 2 * CHUNK)] = both.astype(bf16).reshape(2 * CHUNK)
+    left = total_len - whole * 2 * CHUNK
+    if left:
+        parts = [chunk(2 * whole)]
+        parts.append(chunk(2 * whole + 1) if left > CHUNK else jnp.zeros((rows, LANES), f32))
+        both = jnp.concatenate(parts, axis=0).astype(bf16).reshape(2 * CHUNK)
+        weights_out[pl.ds(2 * CHUNK * whole, left)] = both[0:left]
 
     for index, rows in sent:
         drain_stats(index, rows)
@@ -842,69 +920,29 @@
 
 
 def finish_kernel(
-    n, shard_len,
-    out_t, gfeat_t, gnorm_t, master_t, first_t, second_t, slabs_t,
+    out_t, gfeat_t, gnorm_t, master_t, first_t, second_t, weights_t,
     out_h, gfeat_h, gnorm, master_h, first_h, second_h, weights_h,
-    out, gfeat, norm_s, master, first, second, slabs, joined, in_sem, out_sem,
+    norm_s, sem,
 ):
-    loads = [
-        pltpu.make_async_copy(source, target, in_sem.at[k])
+    copies = [
+        pltpu.make_async_copy(source, target, sem.at[k])
         for k, (source, target) in enumerate(
             (
-                (slabs_t, slabs),
-                (out_t, out),
-                (gfeat_t, gfeat),
-                (master_t, master),
-                (first_t, first),
-                (second_t, second),
+                (weights_t, weights_h),
+                (out_t, out_h),
+                (gfeat_t, gfeat_h),
+                (master_t, master_h),
+                (first_t, first_h),
+                (second_t, second_h),
                 (gnorm_t, norm_s),
             )
         )
     ]
-    stores = [
-        pltpu.make_async_copy(source, target, out_sem.at[k])
-        for k, (source, target) in enumerate(
-            (
-                (joined, weights_h),
-                (out, out_h),
-                (gfeat, gfeat_h),
-                (master, master_h),
-                (first, first_h),
-                (second, second_h),
-            )
-        )
-    ]
-    for copy in loads:
+    for copy in copies:
         copy.start()
-    for k in range(1, 6):
-        loads[k].wait()
-        stores[k].start()
-    loads[6].wait()
+    copies[-1].wait()
     gnorm[...] = norm_s[0:1, 0:1]
-    loads[0].wait()
-    total_len = joined.shape[0]
-    rows = CHUNK // LANES
-
-    def chunk(c):
-        value = None
-        for owner in range(c * CHUNK // shard_len, min((c * CHUNK + CHUNK - 1) // shard_len, n - 1) + 1):
-            k = c - owner * shard_len // CHUNK
-            part = slabs[owner % 2, owner // 2, rows * k : rows * (k + 1)].astype(f32)
-            value = part if value is None else value + part
-        return value
-
-    whole = total_len // (2 * CHUNK)
-    for c in range(whole):
-        both = jnp.concatenate([chunk(2 * c), chunk(2 * c + 1)], axis=0)
-        joined[pl.ds(2 * CHUNK * c, 2 * CHUNK)] = both.astype(bf16).reshape(2 * CHUNK)
-    left = total_len - whole * 2 * CHUNK
-    if left:
-        parts = [chunk(2 * whole)]
-        parts.append(chunk(2 * whole + 1) if left > CHUNK else jnp.zeros((rows, LANES), f32))
-        both = jnp.concatenate(parts, axis=0).astype(bf16).reshape(2 * CHUNK)
-        joined[pl.ds(2 * CHUNK * whole, left)] = both[0:left]
-    stores[0].start()
-    for copy in stores:
+    for copy in copies[:-1]:
         copy.wait()
 
 
@@ -965,7 +1003,7 @@
         dma((7,)),
         dma((7,)),
         pltpu.VMEM((TAIL_PAD,), bf16),
-        pltpu.VMEM((5, WIDTH, WIDTH), bf16),
+        pltpu.VMEM((9, WIDTH, WIDTH), bf16),
         pairs(WINDOW, bf16),
         pairs(WIDTH),
         pairs(GROUPS),
@@ -981,13 +1019,17 @@
         pltpu.VMEM((points, WIDTH), f32),
         pltpu.VMEM((points, WIDTH), f32),
         pltpu.VMEM((points, WIDTH), bf16),
+        pltpu.VMEM((WIDTH, points), bf16),
+        pltpu.VMEM((WIDTH, points), bf16),
+        pltpu.VMEM((WIDTH, points), bf16),
+        pltpu.VMEM((2, 2 * GROUPS, WIDTH), bf16),
         pltpu.VMEM((points, WIDTH), bf16),
-        pltpu.VMEM((points, WIDTH), bf16),
-        pltpu.VMEM((WIDTH, points), bf16),
         pltpu.VMEM((WIDTH, points), f32),
         pltpu.VMEM((points, WIDTH), f32),
         pltpu.VMEM((points, GROUPS), f32),
         pltpu.VMEM((3 * GROUPS, points), f32),
+        pltpu.VMEM((3 * GROUPS, points), f32),
+        pairs(GROUPS, bf16),
         pltpu.VMEM((WIDTH, PAIRS), bf16),
         pltpu.VMEM((points, WIDTH), f32),
         pltpu.VMEM((points, WIDTH), bf16),
@@ -1021,17 +1063,17 @@
             shape(master.shape, f32),
             shape(master.shape, f32),
             shape(master.shape, f32),
-            shape((2, half, slab_rows, LANES), bf16),
+            pltpu.VMEM(weights.shape, bf16),
         ),
         in_specs=[hbm] * 9,
-        out_specs=[hbm] * 7,
+        out_specs=[pl.BlockSpec(memory_space=pl.ANY)] * 6 + [vmem],
         scratch_shapes=scratch,
         compiler_params=pltpu.CompilerParams(
-            collective_id=0, has_side_effects=True, vmem_limit_bytes=56 * 2**20
+            collective_id=0, has_side_effects=True, vmem_limit_bytes=40 * 2**20
         ),
-    )(features, coords, valid_mask, neighbors, cotangent, weights, master, first_moment, second_moment)
+    )(*(pltpu.with_memory_space_constraint(x, pltpu.HBM) for x in (features, coords, valid_mask, neighbors, cotangent, weights, master, first_moment, second_moment)))
     results = pl.pallas_call(
-        functools.partial(finish_kernel, n, shard_len),
+        finish_kernel,
         out_shape=(
             shape(features.shape, bf16),
             shape(features.shape, bf16),
@@ -1041,21 +1083,10 @@
             shape(master.shape, f32),
             shape(weights.shape, bf16),
         ),
-        in_specs=[hbm] * 7,
+        in_specs=[pl.BlockSpec(memory_space=pl.ANY)] * 7,
         out_specs=[hbm, hbm, vmem, hbm, hbm, hbm, hbm],
-        scratch_shapes=[
-            pltpu.VMEM(features.shape, bf16),
-            pltpu.VMEM(features.shape, bf16),
-            pltpu.VMEM((1, LANES), f32),
-            pltpu.VMEM(master.shape, f32),
-            pltpu.VMEM(master.shape, f32),
-            pltpu.VMEM(master.shape, f32),
-            pltpu.VMEM((2, half, slab_rows, LANES), bf16),
-            pltpu.VMEM(weights.shape, bf16),
-            dma((7,)),
-            dma((6,)),
-        ],
-        compiler_params=pltpu.CompilerParams(vmem_limit_bytes=62 * 2**20),
+        scratch_shapes=[pltpu.VMEM((1, LANES), f32), dma((7,))],
+        compiler_params=pltpu.CompilerParams(vmem_limit_bytes=8 * 2**20),
     )(*results)
     return results[0], results[1], results[2].reshape(()), *results[3:]
 

time: 76.4 us -> 70.7 us (0.925)
  Pallas kernels: 75.4 us -> 69.7 us
    pallas_call x1, Pallas kernels: 72.6 us -> 68.1 us  [shards(): pl.pallas_call(functools.partial(block_kernel, n_rows, n_cols), out_shape...]
    pallas_call x1, Pallas kernels: 2.88 us -> 1.61 us  [shards(): pl.pallas_call(finish_kernel, out_shape=(shape(features.shape, bf16), sha...]
where the time goes in v2:
time: 70.7 us; the launch traced here: 70.5 us
  Pallas kernels  69.7 us (99%)
  between operations  0.8 us (1%)
    pallas_call x1, Pallas kernels, shards(): pl.pallas_call(functools.partial(block_kernel, n_rows, n_cols), out_shape...  68.1 us
    pallas_call x1, Pallas kernels, shards(): pl.pallas_call(finish_kernel, out_shape=(shape(features.shape, bf16), sha...  1.61 us

profile of v2, /device:TPU:1, one launch (start us, length us, event | category | flops | bytes accessed | tf_op | source)
XLA Modules:
  0.0 70.5 jit_solution(17944048359438890771)
XLA Ops:
  0.6 68.1 %shard_map.144 = (bf16[512,256]{1,0:T(8,128)(2,1)S(1)}, bf16[512,256]{1,0:T(8,128)(2,1)S(1)}, f32[1,128]{1,0:T(1,128)S(1)}, f32[10587]{0:T(1024)S(1)}, f32[10587...) custom-call(bf16[512,256]{1,0:T(8,128)(2,1)} %feat_h.1, f32[3,512]{1,0:T(4,128)} %coords_h.1, ...), custom_call_target="tpu_custom_call" | custom-call | tf_op jit(solution)/shard_map/pallas_call | solution.py:1057
  68.8 1.6 %shard_map.145 = (bf16[512,256]{1,0:T(8,128)(2,1)}, bf16[512,256]{1,0:T(8,128)(2,1)}, f32[1,1]{1,0:T(1,128)}, f32[10587]{0:T(1024)}, f32[10587]{0:T(1024)}, /*index=5*/f32[10587]{0:T(1024)}, bf16[338784]{0:T(1024)(128)(2,1)}) custom-call(bf16[512,256]{1,0:T(8,128)(2,1)S(1)} %get-tuple-element.21.out_t, bf16[512,256]{1,0:T(8,128)(2,1)S(1)} %get-tuple-element.22.gfeat_t, ...), custom_call_target="tpu_custom_call" | custom-call | tf_op jit(solution)/shard_map/pallas_call | solution.py:1075

commit v3 on v2

--- a/solution.py
+++ b/solution.py
@@ -27,6 +27,8 @@
 TAIL_PAD = 2048
 SLICE = 2048
 SLICE_ROWS = SLICE // LANES
+LOW_ROWS = SLICE // WIDTH * 2 * GROUPS // LANES
+DENSE_FROM = 3
 CHUNK = 1024
 
 bn_eps = 1e-05
@@ -137,9 +139,9 @@
     feat, coords, valid, nbrs, cot, w_first, pos_first, weights, state, news, outs, norm_s, in_sem, out_sem,
     stat_send, stat_buf, stat_ssem, stat_rsem,
     tail1d, mats, onehot, vgat, att, wpre, uact, dyw, rel, pos, act, pmask, allow, dmix,
-    a1_s, z_s, h_s, h_ts, q_s, k_s, ba_s, o_s, do_s, dv_s, sk_s, bd_s, dp_s, ds_s, xs, dz_s, dz16,
-    flat, pair_got, part16, got16, sums, owned, tail_g, slab_f, shard_w, all_w,
-    pair_ssem, pair_rsem, rs_ssem, rs_rsem, own_ssem, own_rsem, ag_ssem, ag_rsem, fw_ssem, fw_rsem,
+    ft_s, slope_a, slope_p, a1_s, z_s, h_s, h_ts, q_s, k_s, ba_s, o_s, do_s, dv_s, sk_s, bd_s, dp_s, ds_s, xs, dz_s, dz16,
+    mu_s, flat, pair_got, part16, got16, first_f, first_got, wide16, got_wide, low_f, low_got, low_sum, got_low, sums, owned, tail_g, slab_f, shard_w, all_w,
+    pair_ssem, pair_rsem, rs_ssem, rs_rsem, wd_ssem, wd_rsem, low_ssem, low_rsem, own_ssem, own_rsem, ag_ssem, ag_rsem, fw_ssem, fw_rsem,
 ):
     n = n_rows * n_cols
     half = n // 2
@@ -153,8 +155,11 @@
     total_len = weights.shape[0]
     shard_len = master_h.shape[0]
     shard_rows = -(-tail_g.shape[0] // LANES)
-    sliced = flat.shape[0]
+    per_matrix = SQUARE // SLICE // 2
+    dense = DENSE_FROM * per_matrix
+    sliced = dense + flat.shape[0]
     slots = got16.shape[0]
+    low_kinds = got_low.shape[0]
     sides = own_ssem.shape[1]
     span = own_rsem.shape[0]
 
@@ -228,61 +233,99 @@
         return collect
 
     sibling = (row_id, col_id + 1 - 2 * core)
-    per_matrix = SQUARE // SLICE // 2
-
     def put_matrix(m, grad):
-        flat[m * per_matrix : (m + 1) * per_matrix] = grad.reshape(per_matrix, 2, SLICE_ROWS, LANES)
-
-    def exchange(group, begin, count):
+        at = (m - DENSE_FROM) * per_matrix
+        flat[at : at + per_matrix] = grad.reshape(per_matrix, 2, SLICE_ROWS, LANES)
+
+    def swap(group, source, target):
         copy = pltpu.make_async_remote_copy(
-            src_ref=flat.at[pl.ds(begin, count), 1 - core],
-            dst_ref=pair_got.at[pl.ds(begin, count)],
+            src_ref=source.at[:, 1 - core],
+            dst_ref=target,
             send_sem=pair_ssem.at[group],
             recv_sem=pair_rsem.at[group],
             device_id=sibling,
             device_id_type=MESH,
         )
         copy.start()
-        return copy, begin, count
-
-    def send_slice(index, slot, other):
-        pltpu.make_async_remote_copy(
-            src_ref=part16.at[index],
-            dst_ref=got16.at[slot, chip],
-            send_sem=rs_ssem.at[slot],
-            recv_sem=rs_rsem.at[slot],
-            device_id=place(2 * other + core),
-            device_id_type=MESH,
-        ).start()
-
-    def send_group(pair):
-        copy, begin, count = pair
-        copy.wait()
-        part16[pl.ds(begin, count)] = (
-            flat[pl.ds(begin, count), core] + pair_got[pl.ds(begin, count)]
-        ).astype(bf16)
-        if count % half == 0 and begin % half == 0:
-            for slot in range(begin // half, (begin + count) // half):
-
-                def post(k, carry, slot=slot):
-                    other = peer(chip, k, half)
-                    send_slice(slot * half + other, slot, other)
-                    return carry
-
-                lax.fori_loop(1, half, post, 0)
+        return copy
+
+    def to_chips(begin, count, send):
+        if count == half and begin % half == 0:
+
+            def post(k, carry):
+                other = peer(chip, k, half)
+                send(begin + other, other)
+                return carry
+
+            lax.fori_loop(1, half, post, 0)
         else:
 
             def post_any(k, carry):
                 index = begin + k
-                slot, other = index // half, lax.rem(index, half)
+                other = lax.rem(index, half)
 
                 @pl.when(other != chip)
                 def _():
-                    send_slice(index, slot, other)
+                    send(index, other)
 
                 return carry
 
             lax.fori_loop(0, count, post_any, 0)
+
+    def send_dense(copy, begin, count):
+        copy.wait()
+        own = pl.ds(begin - dense, count)
+        part16[own] = (flat[own, core] + pair_got[own]).astype(bf16)
+
+        def send(index, other):
+            pltpu.make_async_remote_copy(
+                src_ref=part16.at[index - dense],
+                dst_ref=got16.at[index // half, chip],
+                send_sem=rs_ssem.at[index // half],
+                recv_sem=rs_rsem.at[index // half],
+                device_id=place(2 * other + core),
+                device_id_type=MESH,
+            ).start()
+
+        at = begin
+        while at < begin + count:
+            step = min(half - at % half, begin + count - at)
+            to_chips(at, step, send)
+            at = at + step
+
+    def send_wide(copy, which):
+        copy.wait()
+        for k, piece in enumerate(split(first_f[which, :, core] + first_got[which], 2)):
+            wide16[which, :, k] = piece
+
+        def send(index, other):
+            pltpu.make_async_remote_copy(
+                src_ref=wide16.at[which, index],
+                dst_ref=got_wide.at[which, chip],
+                send_sem=wd_ssem.at[which],
+                recv_sem=wd_rsem.at[which],
+                device_id=place(2 * other + core),
+                device_id_type=MESH,
+            ).start()
+
+        to_chips(0, per_matrix, send)
+
+    def send_low(copy):
+        copy.wait()
+        low_sum[...] = low_f[:, core] + low_got[...]
+        for kind in range(low_kinds):
+
+            def send(index, other, kind=kind):
+                pltpu.make_async_remote_copy(
+                    src_ref=low_sum.at[index - (1 + kind) * per_matrix],
+                    dst_ref=got_low.at[kind, chip],
+                    send_sem=low_ssem.at[kind],
+                    recv_sem=low_rsem.at[kind],
+                    device_id=place(2 * other + core),
+                    device_id_type=MESH,
+                ).start()
+
+            to_chips((1 + kind) * per_matrix, per_matrix, send)
 
     def drain_stats(index, rows):
         span = stat_buf.at[index, pl.ds(0, n - 1), pl.ds(0, rows)]
@@ -307,6 +350,51 @@
     masked = point_mask * a1
     sum_a, sqr_a = row_sum(masked), row_sum(masked * a1)
 
+    weight = [[pos_in[:, 3 * c + d : 3 * c + d + 1] for d in range(3)] for c in range(3)]
+    pos_one = [jnp.zeros((NEAREST, LANES), f32) for _ in range(3)]
+    pos_two = [jnp.zeros((NEAREST, LANES), f32) for _ in range(3)]
+    pairs_local = jnp.zeros((NEAREST, LANES), f32)
+    for b in range(blocks):
+        here = slice(b * LANES, (b + 1) * LANES)
+        index = nbrs[:, here]
+        tile, at = lax.shift_right_logical(index, 7), index & (LANES - 1)
+
+        def fetch(c, t):
+            row = jnp.broadcast_to(coords[c : c + 1, t * LANES : (t + 1) * LANES], index.shape)
+            return jnp.take_along_axis(row, at, axis=1, mode="promise_in_bounds")
+
+        r = []
+        for c in range(3):
+            near = fetch(c, b)
+            if b > 0:
+                near = jnp.where(tile < b, fetch(c, b - 1), near)
+            if b < blocks - 1:
+                near = jnp.where(tile > b, fetch(c, b + 1), near)
+            r.append(near - coords[c : c + 1, here])
+        pm = jnp.where(index.astype(f32) < n_valid, lane_mask[:, here], 0.0)
+        pairs_local = pairs_local + pm
+        for d in range(3):
+            p = weight[0][d] * r[0] + weight[1][d] * r[1] + weight[2][d] * r[2]
+            pos_one[d] = pos_one[d] + pm * p
+            pos_two[d] = pos_two[d] + pm * p * p
+
+    def total(value):
+        return jnp.sum(row_sum(value), axis=1, keepdims=True)
+
+    lane = iota((1, LANES), 1)
+    last = jnp.where(lane == 16, n_valid, 0.0) + jnp.where(lane == 17, total(pairs_local), 0.0)
+    for d in range(3):
+        last = last + jnp.where(lane == d, total(pos_one[d]), 0.0)
+        last = last + jnp.where(lane == 8 + d, total(pos_two[d]), 0.0)
+
+    def fold(row):
+        return jnp.concatenate([row[:, 0:LANES], row[:, LANES:WIDTH]], axis=0)
+
+    def unfold(rows):
+        return jnp.concatenate([rows[0:1], rows[1:2]], axis=1)
+
+    pl.semaphore_wait(barrier, n - 1)
+    collect_first = all_sum(0, jnp.concatenate([fold(sum_a), fold(sqr_a), last], axis=0))
     window_row = iota((WINDOW, LANES), 0)
     for b in range(blocks):
         for j in range(NEAREST):
@@ -321,9 +409,6 @@
     )
     slot0 = (iota((1, PAIRS), 1) < LANES).astype(f32)
     pos_in_cols = [pos_in_col(c) for c in range(3)]
-    sum_p = jnp.zeros((8, 1), f32)
-    sqr_p = jnp.zeros((8, 1), f32)
-    pairs_local = jnp.zeros((1, 1), f32)
     for b in range(blocks):
         here = slice(b * LANES, (b + 1) * LANES)
         fetched = nn(table[:, starts[b] : starts[b] + WINDOW], onehot[b])
@@ -336,26 +421,7 @@
         pos[b] = p
         pmask[b] = pm
         allow[b] = jnp.maximum(mask_n, slot0)
-        sum_p = sum_p + lane_sum(pm * p)
-        sqr_p = sqr_p + lane_sum(pm * p * p)
-        pairs_local = pairs_local + lane_sum(pm[0:1])
-
-    lane = iota((1, LANES), 1)
-    last = (
-        col_to_row(sum_p, 0)
-        + col_to_row(sqr_p, 8)
-        + jnp.where(lane == 16, n_valid, 0.0)
-        + jnp.where(lane == 17, pairs_local, 0.0)
-    )
-
-    def fold(row):
-        return jnp.concatenate([row[:, 0:LANES], row[:, LANES:WIDTH]], axis=0)
-
-    def unfold(rows):
-        return jnp.concatenate([rows[0:1], rows[1:2]], axis=1)
-
-    pl.semaphore_wait(barrier, n - 1)
-    collect_first = all_sum(0, jnp.concatenate([fold(sum_a), fold(sqr_a), last], axis=0))
+
     for copy in late:
         copy.wait()
     for m in range(1, 5):
@@ -405,6 +471,9 @@
     pos_mat = jnp.concatenate(pos_rows + [jnp.zeros((13, WIDTH), f32)], axis=0).astype(bf16)
     pos_cols = nt(reorder, pos_mat)
     pos_cols = [pos_cols[:, d : d + 1] for d in range(3)]
+    feat_f = feat[...].astype(f32)
+    ft_s[...] = feat_f.T.astype(bf16)
+    sum_f = row_sum(point_mask * feat_f)
     stats = collect_first()
 
     def pick(row, at):
@@ -435,8 +504,8 @@
     pos_att = nt(att_in_t, pos_mat)
     pos_att_cols = [pos_att[:, d : d + 1] for d in range(3)]
     back_att = jnp.concatenate([nn(att_in_t, mats[6]), nn(att_in_t, mats[7])], axis=0)
-    for k, piece in enumerate(split(back_att, 2)):
-        ba_s[k] = piece
+    back_split = split(back_att, 2)
+    ba_s[...] = jnp.concatenate([back_split[0], back_split[0], back_split[1]], axis=0)
 
     sum_w = jnp.zeros((GROUPS, LANES), f32)
     sqr_w = jnp.zeros((GROUPS, LANES), f32)
@@ -460,14 +529,15 @@
         two = jnp.sum(two, axis=1, keepdims=True)
         return col_to_row(one, 0) + col_to_row(two, GROUPS)
 
-    collect_w = all_sum(1, pair_row(sum_w, sqr_w))
+    collect_w = all_sum(1, jnp.concatenate([pair_row(sum_w, sqr_w), fold(sum_f)], axis=0))
     v_t = nn(mats[8], h_ts[...]).astype(bf16)
     for b in range(blocks):
         vgat[b] = nn(v_t[:, starts[b] : starts[b] + WINDOW], onehot[b])
     stats = collect_w()
+    mean_f = stats[1:3] * inv_points
     mean_w, rs_w = moments(
-        row_to_col(stats[:, 0:GROUPS], GROUPS),
-        row_to_col(stats[:, GROUPS : 2 * GROUPS], GROUPS),
+        row_to_col(stats[0:1, 0:GROUPS], GROUPS),
+        row_to_col(stats[0:1, GROUPS : 2 * GROUPS], GROUPS),
         inv_pairs,
     )
 
@@ -509,10 +579,34 @@
     z_s[...] = z
     masked = point_mask * z
     collect_o = all_sum(2, jnp.concatenate([fold(row_sum(masked)), fold(row_sum(masked * z))], axis=0))
+    for k in range(2):
+        mu_s[k * LANES : (k + 1) * LANES] = jnp.broadcast_to(
+            row_to_col(mean_f[k : k + 1], LANES), (LANES, LANES)
+        )
+
+    def put_first(which, value):
+        first_f[which] = value.reshape(per_matrix, 2, SLICE_ROWS, LANES)
+        return swap(which, first_f.at[which], first_got.at[which])
+
+    def from_feat(value):
+        return nn(
+            jnp.concatenate([ft_s[...]] * 2, axis=1), jnp.concatenate(split(value, 2), axis=0)
+        )
+
+    ahat = (a1_s[...] - mean_a) * rs_a
+    a1_s[...] = ahat
+    ahat_pair = put_first(0, from_feat(point_mask * ahat))
+    for b in range(blocks):
+        what = (wpre[b] - mean_w) * rs_w
+        wpre[b] = what
+        y = what * gain_w + shift_w
+        dyw[b] = silu_slope(y, silu_parts(y)[1])
+    send_wide(ahat_pair, 0)
     stats = collect_o()
     mean_o, rs_o = moments(unfold(stats[0:2]), unfold(stats[2:4]), inv_points)
 
     zhat = (z_s[...] - mean_o) * rs_o
+    z_s[...] = zhat
     y = feat[...].astype(f32) + zhat * gain_o + shift_o
     value, gate = silu_parts(y)
     outs[0] = (point_mask * value).astype(bf16)
@@ -520,10 +614,25 @@
     dy = point_mask * cot[...].astype(f32) * silu_slope(y, gate)
     dz_s[...] = dy
     shift_grad_o, gain_grad_o = row_sum(dy), row_sum(dy * zhat)
-    stats = all_sum(3, jnp.concatenate([fold(shift_grad_o), fold(gain_grad_o)], axis=0))()
+    collect_o = all_sum(3, jnp.concatenate([fold(shift_grad_o), fold(gain_grad_o)], axis=0))
+    for b in range(blocks):
+        phat = (pos[b] - mean_p) * rs_p
+        pos[b] = phat
+        y = phat * gain_p + shift_p
+        slope_p[b] = silu_slope(y, silu_parts(y)[1])
+    y = a1_s[...] * gain_a + shift_a
+    slope_a[...] = silu_slope(y, silu_parts(y)[1])
+    pos_row = jnp.zeros((1, LANES), f32)
+    for c in range(3):
+        with_hat, alone = jnp.zeros((8, 1), f32), jnp.zeros((8, 1), f32)
+        for b in range(blocks):
+            masked = pmask[b] * rel[b, c : c + 1]
+            with_hat = with_hat + lane_sum(masked * pos[b])
+            alone = alone + lane_sum(masked)
+        pos_row = pos_row + col_to_row(with_hat, 64 + 8 * c) + col_to_row(alone, 88 + 8 * c)
+    stats = collect_o()
     one, two = unfold(stats[0:2]) * inv_points, unfold(stats[2:4]) * inv_points
-    zhat = (z_s[...] - mean_o) * rs_o
-    dz = (gain_o * rs_o * (dz_s[...] - point_mask * (one + zhat * two))).astype(bf16)
+    dz = (gain_o * rs_o * (dz_s[...] - point_mask * (one + z_s[...] * two))).astype(bf16)
     dz16[...] = dz
     do_s[...] = nn(dz, mats[5]).T
 
@@ -545,16 +654,13 @@
             [att[b, :, cols(j)] * (da[j] - mean_da) for j in range(NEAREST)], axis=1
         ).astype(bf16)
         ds_s[b] = ds
-        what = (wpre[b] - mean_w) * rs_w
-        y = what * gain_w + shift_w
-        gate = silu_parts(y)[1]
-        dy = nn(att_out, ds) * silu_slope(y, gate)
+        dy = nn(att_out, ds) * dyw[b]
         dyw[b] = dy
         sum_w = sum_w + lane_fold(dy)
-        sqr_w = sqr_w + lane_fold(dy * what)
+        sqr_w = sqr_w + lane_fold(dy * wpre[b])
 
     back_w = pair_row(sum_w, sqr_w)
-    collect_w = all_sum(4, back_w)
+    collect_w = all_sum(4, back_w + pos_row)
     put_matrix(4, tn(nn(o_s[...], reorder).astype(bf16), dz16[...]))
     dv_s[...] = jnp.zeros(dv_s.shape, f32)
     for b in range(blocks):
@@ -565,75 +671,81 @@
         dv_s[pl.ds(starts[b], WINDOW)] += nt(onehot[b], xs[...])
     dv = nn(dv_s[...].astype(bf16), reorder).astype(bf16)
     put_matrix(3, tn(h_s[...], dv))
-    late_pair = exchange(0, 3 * per_matrix, 2 * per_matrix)
+    square_flat = pl.ds(0, 2 * per_matrix)
+    late_pair = swap(2, flat.at[square_flat], pair_got.at[square_flat])
     dv_s[...] = nt(dv, w_v)
+    add_groups = jnp.where(
+        iota((8, 3 * GROUPS), 1) // GROUPS == iota((8, 3 * GROUPS), 0), 1.0, 0.0
+    ).astype(bf16)
     d_att_out = jnp.zeros((GROUPS, GROUPS), f32)
     for b in range(blocks):
         here = slice(b * LANES, (b + 1) * LANES)
         d_att_out = d_att_out + nt(uact[b], ds_s[b])
-        mix = []
-        for j in range(NEAREST):
-            a = att[b, :, cols(j)]
-            back = [row_sum(dp_s[d * GROUPS : (d + 1) * GROUPS, here] * a) for d in range(3)]
-            mix.append(jnp.concatenate(back + [jnp.zeros((5, LANES), f32)], axis=0))
-        dmix[b] = jnp.concatenate(mix, axis=1)
-    send_group(late_pair)
+        mix = [
+            (tiles(dp_s[d * GROUPS : (d + 1) * GROUPS, here]) * att[b]).astype(bf16) for d in range(3)
+        ]
+        dmix[b] = nn(add_groups, jnp.concatenate(mix, axis=0))
+    send_dense(late_pair, dense, 2 * per_matrix)
     stats = collect_w()
     one = row_to_col(stats[:, 0:GROUPS], GROUPS) * inv_pairs
     two = row_to_col(stats[:, GROUPS : 2 * GROUPS], GROUPS) * inv_pairs
+    pos_hat = [row_to_col(stats[:, 64 + 8 * c : 72 + 8 * c], 8) for c in range(3)]
+    pos_alone = [row_to_col(stats[:, 88 + 8 * c : 96 + 8 * c], 8) for c in range(3)]
 
     sk_s[...] = jnp.zeros(sk_s.shape, f32)
     pos_att_rows = split(pos_att[:, 0:8].T, 3)
     pos_att_rows = jnp.concatenate(pos_att_rows, axis=0)
     dw_sums = []
+    along = [jnp.zeros((8, 1), f32) for _ in range(3)]
     sum_p = jnp.zeros((8, 1), f32)
     sqr_p = jnp.zeros((8, 1), f32)
     for b in range(blocks):
-        what = (wpre[b] - mean_w) * rs_w
-        dw_f = gain_w * rs_w * (dyw[b] - pmask[b, 0:1] * (one + what * two))
-        dw = dw_f.astype(bf16)
+        dw = (gain_w * rs_w * (dyw[b] - pmask[b, 0:1] * (one + wpre[b] * two))).astype(bf16)
         sk_s[pl.ds(starts[b], WINDOW)] += nt(onehot[b], dw)
         dw_sums.append(lane_slots(dw.astype(f32)))
         ds_s[b] = dw
         back = nn(pos_att_rows, dw)
         d_act = dmix[b] + back[0:8] + back[8:16] + back[16:24]
-        phat = (pos[b] - mean_p) * rs_p
-        y = phat * gain_p + shift_p
-        gate = silu_parts(y)[1]
-        dy = d_act * silu_slope(y, gate)
-        dmix[b] = dy
+        dy = d_act * slope_p[b]
         sum_p = sum_p + lane_sum(dy)
-        sqr_p = sqr_p + lane_sum(dy * phat)
+        sqr_p = sqr_p + lane_sum(dy * pos[b])
+        for c in range(3):
+            along[c] = along[c] + lane_sum(dy * rel[b, c : c + 1])
     dq_att = jnp.concatenate(dw_sums, axis=1)
     both_att = jnp.concatenate([dq_att.T, -sk_s[...]], axis=1)
     both_split = split(both_att, 2)
-    dh = nn(both_split[0], ba_s[0]) + nn(both_split[1], ba_s[0]) + nn(both_split[0], ba_s[1])
-    dh = dh + dv_s[...]
-    ahat = (a1_s[...] - mean_a) * rs_a
-    y = ahat * gain_a + shift_a
-    gate = silu_parts(y)[1]
-    dy = dh * silu_slope(y, gate)
+    dh = nn(jnp.concatenate(both_split + both_split[0:1], axis=1), ba_s[...]) + dv_s[...]
+    dy = dh * slope_a[...]
     z_s[...] = dy
-    shift_grad_a, gain_grad_a = row_sum(dy), row_sum(dy * ahat)
+    shift_grad_a = row_sum(dy)
+    away = jnp.concatenate(
+        [mu_s[...] * shift_grad_a[:, k * LANES : (k + 1) * LANES] for k in range(2)], axis=1
+    )
+    first_pair = put_first(1, from_feat(dy) - away)
+    low = nn(
+        jnp.concatenate([h_ts[...]] * 2, axis=1), jnp.concatenate(both_split, axis=0)
+    )
+    low_f[...] = low.reshape(per_matrix, 2, LOW_ROWS, LANES)
+    low_pair = swap(3, low_f, low_got)
+    gain_grad_a = row_sum(z_s[...] * a1_s[...])
     last = col_to_row(sum_p, 0) + col_to_row(sqr_p, 8)
+    for c in range(3):
+        last = last + col_to_row(along[c], 16 + 8 * c)
     collect_a = all_sum(
         5, jnp.concatenate([fold(shift_grad_a), fold(gain_grad_a), last], axis=0)
     )
-
-    dq_split = split(dq_att, 2)
-    dk_split = [piece[:, GROUPS : 2 * GROUPS] for piece in both_split]
-    dq = sum(tn(piece, att_in_t) for piece in dq_split).astype(bf16)
-    dk = sum(nn(piece, att_in_t) for piece in dk_split).astype(bf16)
-    put_matrix(1, tn(h_s[...], dq))
-    put_matrix(2, tn(h_s[...], dk))
-    send_group(exchange(1, per_matrix, 2 * per_matrix))
+    send_wide(first_pair, 1)
+    send_low(low_pair)
+
     d_pos_att = sum(
         nt(jnp.concatenate(split(act[b], 3), axis=0), ds_s[b]) for b in range(blocks)
     )
     d_pos_att = d_pos_att[0:8] + d_pos_att[8:16] + d_pos_att[16:24]
     d_pos_split = split(d_pos_att, 3)
-    d_att_in = sum(nt(q_s[...], piece) for piece in dq_split)
-    d_att_in = d_att_in + sum(nn(k_s[...], piece) for piece in dk_split)
+    d_att_in = sum(
+        nn(q_s[...], piece[:, 0:GROUPS]) + nn(k_s[...], piece[:, GROUPS : 2 * GROUPS])
+        for piece in both_split
+    )
     d_att_in = d_att_in + sum(tn(pos_mat[0:8], piece) for piece in d_pos_split)
     d_pos_out = sum(nn(piece, att_in_t) for piece in d_pos_split)
     do_split = split(do_s[...], 2)
@@ -646,82 +758,126 @@
     cross = jnp.concatenate(cross + [jnp.zeros((5, WIDTH), f32)], axis=0)
     d_pos_out = d_pos_out + sum(nn(piece, reorder) for piece in split(cross, 3))
     d_pos_rows = [d_pos_out[d : d + 1] for d in range(3)]
-    small = 5 * per_matrix
-    pieces_rows = [
-        d_att_in.reshape(WIDTH * GROUPS // LANES, LANES),
-        d_att_out.reshape(GROUPS * GROUPS // LANES, LANES),
-    ]
-    along, along_hat, offsets = [], [], []
-    for c in range(3):
-        one = [jnp.zeros((8, 1), f32) for _ in range(3)]
-        for b in range(blocks):
-            masked = pmask[b] * rel[b, c : c + 1]
-            one[0] = one[0] + lane_sum(dmix[b] * rel[b, c : c + 1])
-            one[1] = one[1] + lane_sum(masked * ((pos[b] - mean_p) * rs_p))
-            one[2] = one[2] + lane_sum(masked)
-        along.append(one[0])
-        along_hat.append(one[1])
-        offsets.append(one[2])
-    stats = collect_a()
-    one, two = unfold(stats[0:2]) * inv_points, unfold(stats[2:4]) * inv_points
-    ahat = (a1_s[...] - mean_a) * rs_a
-    da1 = (gain_a * rs_a * (z_s[...] - point_mask * (one + ahat * two))).astype(bf16)
-    put_matrix(0, tn(feat[...], da1))
-    first_pair = exchange(2, 0, per_matrix)
-    one = row_to_col(stats[4:5, 0:8], 8) * inv_pairs
-    two = row_to_col(stats[4:5, 8:16], 8) * inv_pairs
-    pieces = []
-    for c in range(3):
-        d_pos_in = gain_p * rs_p * (along[c] - one * offsets[c] - two * along_hat[c])
-        pieces.append(col_to_row(d_pos_in, 0)[:, 0:3])
-    pieces = pieces + d_pos_rows
+    pieces = [jnp.zeros((1, TAIL_POS_OUT), f32)] + d_pos_rows
     pieces = pieces + [
         gain_grad_a, col_to_row(sqr_p, 0)[:, 0:3], back_w[:, GROUPS : 2 * GROUPS], gain_grad_o,
         shift_grad_a, col_to_row(sum_p, 0)[:, 0:3], back_w[:, 0:GROUPS], shift_grad_o,
         jnp.zeros((1, TAIL_PAD - TAIL_USED), f32),
     ]
-    pieces_rows.append(jnp.concatenate(pieces, axis=1).reshape(TAIL_PAD // LANES, LANES))
+    small = 5 * per_matrix
     used_rows = OFF_TAIL // LANES + TAIL_PAD // LANES - 5 * SQUARE // LANES
     spare_rows = (sliced - small) * 2 * SLICE_ROWS - used_rows
-    pieces_rows.append(jnp.zeros((spare_rows, LANES), f32))
-    flat[small:sliced] = jnp.concatenate(pieces_rows, axis=0).reshape(
+    pieces_rows = [
+        d_att_in.reshape(WIDTH * GROUPS // LANES, LANES),
+        d_att_out.reshape(GROUPS * GROUPS // LANES, LANES),
+        jnp.concatenate(pieces, axis=1).reshape(TAIL_PAD // LANES, LANES),
+        jnp.zeros((spare_rows, LANES), f32),
+    ]
+    flat[small - dense : sliced - dense] = jnp.concatenate(pieces_rows, axis=0).reshape(
         sliced - small, 2, SLICE_ROWS, LANES
     )
-    small_pair = exchange(3, small, sliced - small)
-    send_group(first_pair)
-    send_group(small_pair)
+    small_flat = pl.ds(small - dense, sliced - small)
+    small_pair = swap(4, flat.at[small_flat], pair_got.at[small_flat])
+    send_dense(small_pair, small, sliced - small)
+
+    stats = collect_a()
+    one, two = unfold(stats[0:2]) * inv_points, unfold(stats[2:4]) * inv_points
+    scale_tile = jnp.concatenate([fold(gain_a * rs_a)] * (SLICE_ROWS // 2), axis=0)
+    two_tile = jnp.concatenate([fold(two)] * (SLICE_ROWS // 2), axis=0)
+    da1 = (gain_a * rs_a * (z_s[...] - point_mask * (one + a1_s[...] * two))).astype(bf16)
     outs[1] = (dz_s[...] + nt(da1, w_in)).astype(bf16)
     store(outs.at[1], gfeat_h)
+    one = row_to_col(stats[4:5, 0:8], 8) * inv_pairs
+    two = row_to_col(stats[4:5, 8:16], 8) * inv_pairs
+    pos_in_row = jnp.zeros((1, LANES), f32)
+    for c in range(3):
+        moved = row_to_col(stats[4:5, 16 + 8 * c : 24 + 8 * c], 8)
+        moved = gain_p * rs_p * (moved - one * pos_alone[c] - two * pos_hat[c])
+        pos_in_row = pos_in_row + col_to_row(moved, 3 * c)
+
+    def slice_of(slot):
+        return 2 * (slot * half + chip) + core
+
+    def when_in(slot, low, high, act_on):
+        if (slot + 1) * n <= low or slot * n >= high:
+            return
+        if slot * n >= low and (slot + 1) * n <= high:
+            act_on()
+        else:
+            number = slice_of(slot)
+            pl.when((number >= low) & (number < high))(act_on)
+
+    def others_sum(total, part):
+        def add(k, total):
+            return total + part(peer(chip, k, half))
+
+        return lax.fori_loop(1, half, add, total, unroll=half <= 16)
+
+    def take_wide(which):
+        got = got_wide.at[which, pl.ds(0, half - 1)]
+        pltpu.make_async_copy(got, got, wd_rsem.at[which]).wait()
+        index = lax.rem(chip, per_matrix)
+
+        def part(other):
+            return got_wide[which, other, 0].astype(f32) + got_wide[which, other, 1].astype(f32)
+
+        return others_sum(first_f[which, index, core] + first_got[which, index], part)
+
+    def take_low(kind):
+        got = got_low.at[kind, pl.ds(0, half - 1)]
+        pltpu.make_async_copy(got, got, low_rsem.at[kind]).wait()
+        index = lax.rem(chip, per_matrix)
+        return others_sum(low_sum[index], lambda other: got_low[kind, other])
+
+    def low_product(factor, which):
+        factor = factor.reshape(SLICE // WIDTH, 2 * GROUPS)[:, which * GROUPS : (which + 1) * GROUPS]
+        return sum(nn(piece, att_in_t) for piece in split(factor, 2)).reshape(SLICE_ROWS, LANES)
 
     squares = jnp.zeros((1, 1), f32)
-    for slot in list(range(1, slots)) + [0]:
+    matrix = SQUARE // SLICE
+    for slot in range(slots):
+        sums[slot] = jnp.zeros((SLICE_ROWS, LANES), f32)
+
+    for slot in list(range(DENSE_FROM, slots)) + list(range(min(DENSE_FROM, slots))):
         index = slot * half + chip
-        if (slot + 1) * half <= sliced:
-            here = None
-        else:
-            here = index < sliced
-
-        def take(slot=slot, index=index):
+
+        def take_dense(slot=slot, index=index):
             got = got16.at[slot, pl.ds(0, half - 1)]
             pltpu.make_async_copy(got, got, rs_rsem.at[slot]).wait()
-            total = flat[index, core] + pair_got[index]
-
-            def add(k, total):
-                return total + got16[slot, peer(chip, k, half)].astype(f32)
-
-            sums[slot] = lax.fori_loop(1, half, add, total, unroll=half <= 16)
-
-        if here is None:
-            take()
+            total = flat[index - dense, core] + pair_got[index - dense]
+            sums[slot] = others_sum(total, lambda other: got16[slot, other].astype(f32))
+
+        def add_pos_in(slot=slot):
+            at_row = iota((SLICE_ROWS, LANES), 0) == OFF_TAIL % SLICE // LANES
+            sums[slot] += jnp.where(at_row, pos_in_row, 0.0)
+
+        def first(slot=slot):
+            sums[slot] = scale_tile * (take_wide(1) - two_tile * take_wide(0))
+
+        when_in(slot, DENSE_FROM * matrix, 2 * sliced, take_dense)
+        when_in(slot, OFF_TAIL // SLICE, OFF_TAIL // SLICE + 1, add_pos_in)
+        when_in(slot, 0, matrix, first)
+    for kind in range(low_kinds):
+        kinds = range(2) if low_kinds == 1 else (kind,)
+
+        def fill(kind=kind, kinds=kinds):
+            factor = take_low(kind)
+            for which in kinds:
+                for slot in range(slots):
+
+                    def product(slot=slot, which=which):
+                        sums[slot] = low_product(factor, which)
+
+                    when_in(slot, (1 + which) * matrix, (2 + which) * matrix, product)
+
+        if low_kinds == 1:
+            fill()
         else:
-            sums[slot] = jnp.zeros((SLICE_ROWS, LANES), f32)
-            pl.when(here)(take)
+            when_in(0, (1 + kind) * matrix, (2 + kind) * matrix, fill)
+    for slot in range(slots):
         squares = squares + lane_sum(row_sum(sums[slot] * sums[slot]))
 
     collect_norm = all_sum(6, jnp.where(lane == 0, squares, 0.0))
-
-    def slice_of(slot):
-        return 2 * (slot * half + chip) + core
 
     def each_owner(slot, act_on):
         number = slice_of(slot)
@@ -902,14 +1058,27 @@
     pltpu.make_async_copy(all_w.at[core], all_w.at[core], fw_ssem).wait()
     rest = all_w.at[core, pl.ds(0, half - 1)]
     pltpu.make_async_copy(rest, rest, ag_ssem).wait()
+    def drain(count, ref, sem):
+        def wait_one(k, carry):
+            pltpu.make_async_copy(ref, ref, sem).wait()
+            return carry
+
+        lax.fori_loop(0, count, wait_one, 0)
+
+    def others(low, high):
+        inside = (chip >= low) & (chip < high)
+        return high - low - inside.astype(jnp.int32)
+
+    for which in range(2):
+        drain(others(0, per_matrix), wide16.at[0, 0], wd_ssem.at[which])
+    for kind in range(low_kinds):
+        low_at = (1 + kind) * per_matrix % half
+        drain(others(low_at, low_at + per_matrix), low_sum.at[0], low_ssem.at[kind])
     for slot in range(slots):
-        count = min(sliced - slot * half, half)
-
-        def drain(k, carry, slot=slot):
-            pltpu.make_async_copy(part16.at[0], part16.at[0], rs_ssem.at[slot]).wait()
-            return carry
-
-        lax.fori_loop(0, count - (chip < count).astype(jnp.int32), drain, 0)
+        low_at = max(dense - slot * half, 0)
+        high_at = min(sliced - slot * half, half)
+        if high_at > low_at:
+            drain(others(low_at, high_at), part16.at[0], rs_ssem.at[slot])
 
         def own_drain(owner, k, side, slot=slot):
             @pl.when(owner != me)
@@ -970,6 +1139,9 @@
     slab_rows = up(shard_rows + CHUNK // LANES, 16)
     sliced = up(-(-total_len // SLICE), 2) // 2
     slots = -(-sliced // half)
+    per_matrix = SQUARE // SLICE // 2
+    dense_pairs = sliced - DENSE_FROM * per_matrix
+    low_kinds = 1 if per_matrix % half == 0 else 2
     sides = (SLICE + shard_len - 2) // shard_len + 1
     span = (SLICE + shard_len - 2) // SLICE + 1
     hbm = pl.BlockSpec(memory_space=pltpu.HBM)
@@ -1016,13 +1188,16 @@
         pairs(8),
         pairs(8),
         pairs(8),
+        pltpu.VMEM((WIDTH, points), bf16),
+        pltpu.VMEM((points, WIDTH), f32),
+        pairs(8),
         pltpu.VMEM((points, WIDTH), f32),
         pltpu.VMEM((points, WIDTH), f32),
         pltpu.VMEM((points, WIDTH), bf16),
         pltpu.VMEM((WIDTH, points), bf16),
         pltpu.VMEM((WIDTH, points), bf16),
         pltpu.VMEM((WIDTH, points), bf16),
-        pltpu.VMEM((2, 2 * GROUPS, WIDTH), bf16),
+        pltpu.VMEM((6 * GROUPS, WIDTH), bf16),
         pltpu.VMEM((points, WIDTH), bf16),
         pltpu.VMEM((WIDTH, points), f32),
         pltpu.VMEM((points, WIDTH), f32),
@@ -1033,20 +1208,33 @@
         pltpu.VMEM((WIDTH, PAIRS), bf16),
         pltpu.VMEM((points, WIDTH), f32),
         pltpu.VMEM((points, WIDTH), bf16),
-        pltpu.VMEM((sliced, 2, SLICE_ROWS, LANES), f32),
-        pltpu.VMEM((sliced, SLICE_ROWS, LANES), f32),
-        pltpu.VMEM((sliced, SLICE_ROWS, LANES), bf16),
+        pltpu.VMEM((WIDTH, LANES), f32),
+        pltpu.VMEM((dense_pairs, 2, SLICE_ROWS, LANES), f32),
+        pltpu.VMEM((dense_pairs, SLICE_ROWS, LANES), f32),
+        pltpu.VMEM((dense_pairs, SLICE_ROWS, LANES), bf16),
         pltpu.VMEM((slots, half, SLICE_ROWS, LANES), bf16),
+        pltpu.VMEM((2, per_matrix, 2, SLICE_ROWS, LANES), f32),
+        pltpu.VMEM((2, per_matrix, SLICE_ROWS, LANES), f32),
+        pltpu.VMEM((2, per_matrix, 2, SLICE_ROWS, LANES), bf16),
+        pltpu.VMEM((2, half, 2, SLICE_ROWS, LANES), bf16),
+        pltpu.VMEM((per_matrix, 2, LOW_ROWS, LANES), f32),
+        pltpu.VMEM((per_matrix, LOW_ROWS, LANES), f32),
+        pltpu.VMEM((per_matrix, LOW_ROWS, LANES), f32),
+        pltpu.VMEM((low_kinds, half, LOW_ROWS, LANES), f32),
         pltpu.VMEM((slots, SLICE_ROWS, LANES), f32),
         pltpu.VMEM((up(max(span * SLICE_ROWS, SLICE_ROWS + shard_rows), SLICE_ROWS), LANES), f32),
         pltpu.VMEM((shard_rows * LANES,), f32),
         pltpu.VMEM((slab_rows, LANES), f32),
         pltpu.VMEM((slab_rows, LANES), bf16),
         pltpu.VMEM((2, half, slab_rows, LANES), bf16),
-        dma((4,)),
-        dma((4,)),
+        dma((5,)),
+        dma((5,)),
         dma((slots,)),
         dma((slots,)),
+        dma((2,)),
+        dma((2,)),
+        dma((low_kinds,)),
+        dma((low_kinds,)),
         dma((slots, sides)),
         dma((span,)),
         dma,
@@ -1069,7 +1257,7 @@
         out_specs=[pl.BlockSpec(memory_space=pl.ANY)] * 6 + [vmem],
         scratch_shapes=scratch,
         compiler_params=pltpu.CompilerParams(
-            collective_id=0, has_side_effects=True, vmem_limit_bytes=40 * 2**20
+            collective_id=0, has_side_effects=True, vmem_limit_bytes=48 * 2**20
         ),
     )(*(pltpu.with_memory_space_constraint(x, pltpu.HBM) for x in (features, coords, valid_mask, neighbors, cotangent, weights, master, first_moment, second_moment)))
     results = pl.pallas_call(

time: 70.7 us -> 67.5 us (0.955)
  Pallas kernels: 69.7 us -> 66.5 us
    pallas_call x1, Pallas kernels: 68.1 us -> 64.9 us  [shards(): pl.pallas_call(functools.partial(block_kernel, n_rows, n_cols), out_shape...]
where the time goes in v3:
time: 67.5 us; the launch traced here: 67.3 us
  Pallas kernels  66.5 us (99%)
  between operations  0.8 us (1%)
    pallas_call x1, Pallas kernels, shards(): pl.pallas_call(functools.partial(block_kernel, n_rows, n_cols), out_shape...  64.9 us
    pallas_call x1, Pallas kernels, shards(): pl.pallas_call(finish_kernel, out_shape=(shape(features.shape, bf16), sha...  1.61 us

profile of v3, /device:TPU:1, one launch (start us, length us, event | category | flops | bytes accessed | tf_op | source)
XLA Modules:
  0.0 67.3 jit_solution(14592265358331842643)
XLA Ops:
  0.6 64.9 %shard_map.144 = (bf16[512,256]{1,0:T(8,128)(2,1)S(1)}, bf16[512,256]{1,0:T(8,128)(2,1)S(1)}, f32[1,128]{1,0:T(1,128)S(1)}, f32[10587]{0:T(1024)S(1)}, f32[10587...) custom-call(bf16[512,256]{1,0:T(8,128)(2,1)} %feat_h.1, f32[3,512]{1,0:T(4,128)} %coords_h.1, ...), custom_call_target="tpu_custom_call" | custom-call | tf_op jit(solution)/shard_map/pallas_call | solution.py:1245
  65.6 1.6 %shard_map.145 = (bf16[512,256]{1,0:T(8,128)(2,1)}, bf16[512,256]{1,0:T(8,128)(2,1)}, f32[1,1]{1,0:T(1,128)}, f32[10587]{0:T(1024)}, f32[10587]{0:T(1024)}, /*index=5*/f32[10587]{0:T(1024)}, bf16[338784]{0:T(1024)(128)(2,1)}) custom-call(bf16[512,256]{1,0:T(8,128)(2,1)S(1)} %get-tuple-element.21.out_t, bf16[512,256]{1,0:T(8,128)(2,1)S(1)} %get-tuple-element.22.gfeat_t, ...), custom_call_target="tpu_custom_call" | custom-call | tf_op jit(solution)/shard_map/pallas_call | solution.py:1263

commit v4 on v3

--- a/solution.py
+++ b/solution.py
@@ -84,6 +84,14 @@
     return lax.broadcasted_iota(jnp.int32, shape, dim)
 
 
+def loop(begin, end, body):
+    if end - begin <= 31:
+        for k in range(begin, end):
+            body(k, 0)
+    else:
+        lax.fori_loop(begin, end, body, 0)
+
+
 def row_to_col(row, count):
     wide = jnp.broadcast_to(row, (count, row.shape[1]))
     same = iota(wide.shape, 0) == iota(wide.shape, 1)
@@ -139,8 +147,8 @@
     feat, coords, valid, nbrs, cot, w_first, pos_first, weights, state, news, outs, norm_s, in_sem, out_sem,
     stat_send, stat_buf, stat_ssem, stat_rsem,
     tail1d, mats, onehot, vgat, att, wpre, uact, dyw, rel, pos, act, pmask, allow, dmix,
-    ft_s, slope_a, slope_p, a1_s, z_s, h_s, h_ts, q_s, k_s, ba_s, o_s, do_s, dv_s, sk_s, bd_s, dp_s, ds_s, xs, dz_s, dz16,
-    mu_s, flat, pair_got, part16, got16, first_f, first_got, wide16, got_wide, low_f, low_got, low_sum, got_low, sums, owned, tail_g, slab_f, shard_w, all_w,
+    ft_s, slope_a, slope_p, a1_s, z_s, h_s, h_ts, q_s, k_s, ba_s, o_s, o_ts, do_s, dv_s, sk_s, bd_s, dp_s, ds_s, dw_s, xs, dz_s, dz16,
+    mu_s, flat, pair_got, part16, got16, first_f, first_got, wide16, got_wide, low_f, low_got, low_sum, got_low, hat_s, sums, owned, tail_g, slab_f, shard_w, all_w,
     pair_ssem, pair_rsem, rs_ssem, rs_rsem, wd_ssem, wd_rsem, low_ssem, low_rsem, own_ssem, own_rsem, ag_ssem, ag_rsem, fw_ssem, fw_rsem,
 ):
     n = n_rows * n_cols
@@ -172,7 +180,7 @@
         pl.semaphore_signal(barrier, inc=1, device_id=place(peer(me, k, n)), device_id_type=MESH)
         return carry
 
-    lax.fori_loop(1, n, greet, 0)
+    loop(1, n, greet)
     loads = []
 
     def load(source, target):
@@ -222,7 +230,7 @@
             ).start()
             return carry
 
-        lax.fori_loop(1, n, post, 0)
+        loop(1, n, post)
         sent.append((index, rows))
 
         def collect():
@@ -233,9 +241,19 @@
         return collect
 
     sibling = (row_id, col_id + 1 - 2 * core)
+    def put_halves(target, value):
+        rows = SLICE_ROWS // 2
+        for k in range(2):
+            part = value[:, k * LANES : (k + 1) * LANES]
+            target[:, :, k * rows : (k + 1) * rows] = part.reshape(per_matrix, 2, rows, LANES)
+
+    def whole_rows(piece):
+        rows = SLICE_ROWS // 2
+        return jnp.concatenate([piece[0:rows], piece[rows:]], axis=1).reshape(SLICE_ROWS, LANES)
+
     def put_matrix(m, grad):
         at = (m - DENSE_FROM) * per_matrix
-        flat[at : at + per_matrix] = grad.reshape(per_matrix, 2, SLICE_ROWS, LANES)
+        put_halves(flat.at[at : at + per_matrix], grad)
 
     def swap(group, source, target):
         copy = pltpu.make_async_remote_copy(
@@ -257,7 +275,7 @@
                 send(begin + other, other)
                 return carry
 
-            lax.fori_loop(1, half, post, 0)
+            loop(1, half, post)
         else:
 
             def post_any(k, carry):
@@ -270,7 +288,7 @@
 
                 return carry
 
-            lax.fori_loop(0, count, post_any, 0)
+            loop(0, count, post_any)
 
     def send_dense(copy, begin, count):
         copy.wait()
@@ -585,7 +603,7 @@
         )
 
     def put_first(which, value):
-        first_f[which] = value.reshape(per_matrix, 2, SLICE_ROWS, LANES)
+        put_halves(first_f.at[which], value)
         return swap(which, first_f.at[which], first_got.at[which])
 
     def from_feat(value):
@@ -602,6 +620,7 @@
         y = what * gain_w + shift_w
         dyw[b] = silu_slope(y, silu_parts(y)[1])
     send_wide(ahat_pair, 0)
+    o_ts[...] = nn(o_s[...], reorder).T.astype(bf16)
     stats = collect_o()
     mean_o, rs_o = moments(unfold(stats[0:2]), unfold(stats[2:4]), inv_points)
 
@@ -661,31 +680,29 @@
 
     back_w = pair_row(sum_w, sqr_w)
     collect_w = all_sum(4, back_w + pos_row)
-    put_matrix(4, tn(nn(o_s[...], reorder).astype(bf16), dz16[...]))
+    put_matrix(4, nn(o_ts[...], dz16[...]))
+    o_flat, v_flat = pl.ds(per_matrix, per_matrix), pl.ds(0, per_matrix)
+    o_pair = swap(2, flat.at[o_flat], pair_got.at[o_flat])
+    add_groups = jnp.where(
+        iota((8, 3 * GROUPS), 1) // GROUPS == iota((8, 3 * GROUPS), 0), 1.0, 0.0
+    ).astype(bf16)
     dv_s[...] = jnp.zeros(dv_s.shape, f32)
     for b in range(blocks):
         here = slice(b * LANES, (b + 1) * LANES)
         do = do_s[:, here]
         for j in range(NEAREST):
-            xs[:, cols(j)] = (each_channel(att[b, :, cols(j)]) * do).astype(bf16)
-        dv_s[pl.ds(starts[b], WINDOW)] += nt(onehot[b], xs[...])
-    dv = nn(dv_s[...].astype(bf16), reorder).astype(bf16)
-    put_matrix(3, tn(h_s[...], dv))
-    square_flat = pl.ds(0, 2 * per_matrix)
-    late_pair = swap(2, flat.at[square_flat], pair_got.at[square_flat])
-    dv_s[...] = nt(dv, w_v)
-    add_groups = jnp.where(
-        iota((8, 3 * GROUPS), 1) // GROUPS == iota((8, 3 * GROUPS), 0), 1.0, 0.0
-    ).astype(bf16)
-    d_att_out = jnp.zeros((GROUPS, GROUPS), f32)
-    for b in range(blocks):
-        here = slice(b * LANES, (b + 1) * LANES)
-        d_att_out = d_att_out + nt(uact[b], ds_s[b])
+            xs[b, :, cols(j)] = (each_channel(att[b, :, cols(j)]) * do).astype(bf16)
         mix = [
             (tiles(dp_s[d * GROUPS : (d + 1) * GROUPS, here]) * att[b]).astype(bf16) for d in range(3)
         ]
         dmix[b] = nn(add_groups, jnp.concatenate(mix, axis=0))
-    send_dense(late_pair, dense, 2 * per_matrix)
+        dv_s[pl.ds(starts[b], WINDOW)] += nt(onehot[b], xs[b])
+    dv = dv_s[...].astype(bf16)
+    dv_s[...] = nn(dv, mats[8])
+    put_matrix(3, nn(h_ts[...], nn(dv, reorder).astype(bf16)))
+    v_pair = swap(5, flat.at[v_flat], pair_got.at[v_flat])
+    send_dense(o_pair, dense + per_matrix, per_matrix)
+    send_dense(v_pair, dense, per_matrix)
     stats = collect_w()
     one = row_to_col(stats[:, 0:GROUPS], GROUPS) * inv_pairs
     two = row_to_col(stats[:, GROUPS : 2 * GROUPS], GROUPS) * inv_pairs
@@ -696,24 +713,19 @@
     pos_att_rows = split(pos_att[:, 0:8].T, 3)
     pos_att_rows = jnp.concatenate(pos_att_rows, axis=0)
     dw_sums = []
-    along = [jnp.zeros((8, 1), f32) for _ in range(3)]
-    sum_p = jnp.zeros((8, 1), f32)
-    sqr_p = jnp.zeros((8, 1), f32)
     for b in range(blocks):
         dw = (gain_w * rs_w * (dyw[b] - pmask[b, 0:1] * (one + wpre[b] * two))).astype(bf16)
         sk_s[pl.ds(starts[b], WINDOW)] += nt(onehot[b], dw)
         dw_sums.append(lane_slots(dw.astype(f32)))
-        ds_s[b] = dw
-        back = nn(pos_att_rows, dw)
-        d_act = dmix[b] + back[0:8] + back[8:16] + back[16:24]
-        dy = d_act * slope_p[b]
-        sum_p = sum_p + lane_sum(dy)
-        sqr_p = sqr_p + lane_sum(dy * pos[b])
-        for c in range(3):
-            along[c] = along[c] + lane_sum(dy * rel[b, c : c + 1])
+        dw_s[b] = dw
     dq_att = jnp.concatenate(dw_sums, axis=1)
     both_att = jnp.concatenate([dq_att.T, -sk_s[...]], axis=1)
     both_split = split(both_att, 2)
+    low = nn(
+        jnp.concatenate([h_ts[...]] * 2, axis=1), jnp.concatenate(both_split, axis=0)
+    )
+    low_f[...] = low.reshape(per_matrix, 2, LOW_ROWS, LANES)
+    low_pair = swap(3, low_f, low_got)
     dh = nn(jnp.concatenate(both_split + both_split[0:1], axis=1), ba_s[...]) + dv_s[...]
     dy = dh * slope_a[...]
     z_s[...] = dy
@@ -722,11 +734,17 @@
         [mu_s[...] * shift_grad_a[:, k * LANES : (k + 1) * LANES] for k in range(2)], axis=1
     )
     first_pair = put_first(1, from_feat(dy) - away)
-    low = nn(
-        jnp.concatenate([h_ts[...]] * 2, axis=1), jnp.concatenate(both_split, axis=0)
-    )
-    low_f[...] = low.reshape(per_matrix, 2, LOW_ROWS, LANES)
-    low_pair = swap(3, low_f, low_got)
+    along = [jnp.zeros((8, 1), f32) for _ in range(3)]
+    sum_p = jnp.zeros((8, 1), f32)
+    sqr_p = jnp.zeros((8, 1), f32)
+    for b in range(blocks):
+        back = nn(pos_att_rows, dw_s[b])
+        d_act = dmix[b] + back[0:8] + back[8:16] + back[16:24]
+        dy = d_act * slope_p[b]
+        sum_p = sum_p + lane_sum(dy)
+        sqr_p = sqr_p + lane_sum(dy * pos[b])
+        for c in range(3):
+            along[c] = along[c] + lane_sum(dy * rel[b, c : c + 1])
     gain_grad_a = row_sum(z_s[...] * a1_s[...])
     last = col_to_row(sum_p, 0) + col_to_row(sqr_p, 8)
     for c in range(3):
@@ -737,8 +755,9 @@
     send_wide(first_pair, 1)
     send_low(low_pair)
 
+    d_att_out = sum(nt(uact[b], ds_s[b]) for b in range(blocks))
     d_pos_att = sum(
-        nt(jnp.concatenate(split(act[b], 3), axis=0), ds_s[b]) for b in range(blocks)
+        nt(jnp.concatenate(split(act[b], 3), axis=0), dw_s[b]) for b in range(blocks)
     )
     d_pos_att = d_pos_att[0:8] + d_pos_att[8:16] + d_pos_att[16:24]
     d_pos_split = split(d_pos_att, 3)
@@ -782,8 +801,16 @@
 
     stats = collect_a()
     one, two = unfold(stats[0:2]) * inv_points, unfold(stats[2:4]) * inv_points
-    scale_tile = jnp.concatenate([fold(gain_a * rs_a)] * (SLICE_ROWS // 2), axis=0)
-    two_tile = jnp.concatenate([fold(two)] * (SLICE_ROWS // 2), axis=0)
+    def halves(row):
+        return jnp.concatenate(
+            [
+                jnp.broadcast_to(row[:, k * LANES : (k + 1) * LANES], (SLICE_ROWS // 2, LANES))
+                for k in range(2)
+            ],
+            axis=0,
+        )
+
+    scale_tile, two_tile = halves(gain_a * rs_a), halves(two)
     da1 = (gain_a * rs_a * (z_s[...] - point_mask * (one + a1_s[...] * two))).astype(bf16)
     outs[1] = (dz_s[...] + nt(da1, w_in)).astype(bf16)
     store(outs.at[1], gfeat_h)
@@ -838,25 +865,31 @@
     for slot in range(slots):
         sums[slot] = jnp.zeros((SLICE_ROWS, LANES), f32)
 
-    for slot in list(range(DENSE_FROM, slots)) + list(range(min(DENSE_FROM, slots))):
+    def take_dense(in_order, slot):
         index = slot * half + chip
-
-        def take_dense(slot=slot, index=index):
-            got = got16.at[slot, pl.ds(0, half - 1)]
-            pltpu.make_async_copy(got, got, rs_rsem.at[slot]).wait()
-            total = flat[index - dense, core] + pair_got[index - dense]
-            sums[slot] = others_sum(total, lambda other: got16[slot, other].astype(f32))
-
-        def add_pos_in(slot=slot):
-            at_row = iota((SLICE_ROWS, LANES), 0) == OFF_TAIL % SLICE // LANES
-            sums[slot] += jnp.where(at_row, pos_in_row, 0.0)
-
-        def first(slot=slot):
-            sums[slot] = scale_tile * (take_wide(1) - two_tile * take_wide(0))
-
-        when_in(slot, DENSE_FROM * matrix, 2 * sliced, take_dense)
-        when_in(slot, OFF_TAIL // SLICE, OFF_TAIL // SLICE + 1, add_pos_in)
-        when_in(slot, 0, matrix, first)
+        got = got16.at[slot, pl.ds(0, half - 1)]
+        pltpu.make_async_copy(got, got, rs_rsem.at[slot]).wait()
+        total = flat[index - dense, core] + pair_got[index - dense]
+        total = others_sum(total, lambda other: got16[slot, other].astype(f32))
+        sums[slot] = total if in_order else whole_rows(total)
+
+    def take_hat():
+        hat_s[...] = two_tile * take_wide(0)
+
+    def first(slot):
+        sums[slot] = whole_rows(scale_tile * (take_wide(1) - hat_s[...]))
+
+    def add_pos_in(slot):
+        at_row = iota((SLICE_ROWS, LANES), 0) == OFF_TAIL % SLICE // LANES
+        sums[slot] += jnp.where(at_row, pos_in_row, 0.0)
+
+    def each_slot(low, high, act_on):
+        for slot in range(slots):
+            when_in(slot, low, high, functools.partial(act_on, slot))
+
+    each_slot(DENSE_FROM * matrix, 5 * matrix, functools.partial(take_dense, False))
+    each_slot(0, matrix, lambda slot: take_hat())
+    each_slot(0, matrix, first)
     for kind in range(low_kinds):
         kinds = range(2) if low_kinds == 1 else (kind,)
 
@@ -874,6 +907,8 @@
             fill()
         else:
             when_in(0, (1 + kind) * matrix, (2 + kind) * matrix, fill)
+    each_slot(5 * matrix, 2 * sliced, functools.partial(take_dense, True))
+    each_slot(OFF_TAIL // SLICE, OFF_TAIL // SLICE + 1, add_pos_in)
     for slot in range(slots):
         squares = squares + lane_sum(row_sum(sums[slot] * sums[slot]))
 
@@ -998,8 +1033,8 @@
         send_slab(shard_w, chip, row_id, peer(row_chip, k, in_row))
         return carry
 
-    lax.fori_loop(1, n_rows, send_along, 0)
-    lax.fori_loop(1, in_row, send_within, 0)
+    loop(1, n_rows, send_along)
+    loop(1, in_row, send_within)
     forward(chip)
     store(norm_s, gnorm_h)
     for source, target in ((0, new_master_h), (1, new_first_h), (2, new_second_h)):
@@ -1013,11 +1048,11 @@
             send_slab(all_w.at[core, other], other, row_id, peer(row_chip, i, in_row))
             return carry
 
-        lax.fori_loop(1, in_row, send_on, 0)
+        loop(1, in_row, send_on)
         forward(other)
         return carry
 
-    lax.fori_loop(1, n_rows, spread_row, 0)
+    loop(1, n_rows, spread_row)
 
     def pass_on(k, carry):
         step = k // (in_row - 1)
@@ -1027,7 +1062,7 @@
         forward(other)
         return carry
 
-    lax.fori_loop(0, n_rows * (in_row - 1), pass_on, 0)
+    loop(0, n_rows * (in_row - 1), pass_on)
     pltpu.make_async_copy(all_w.at[core], all_w.at[core], fw_rsem).wait()
     rows = CHUNK // LANES
 
@@ -1199,13 +1234,15 @@
         pltpu.VMEM((WIDTH, points), bf16),
         pltpu.VMEM((6 * GROUPS, WIDTH), bf16),
         pltpu.VMEM((points, WIDTH), bf16),
+        pltpu.VMEM((WIDTH, points), bf16),
         pltpu.VMEM((WIDTH, points), f32),
         pltpu.VMEM((points, WIDTH), f32),
         pltpu.VMEM((points, GROUPS), f32),
         pltpu.VMEM((3 * GROUPS, points), f32),
         pltpu.VMEM((3 * GROUPS, points), f32),
         pairs(GROUPS, bf16),
-        pltpu.VMEM((WIDTH, PAIRS), bf16),
+        pairs(GROUPS, bf16),
+        pairs(WIDTH, bf16),
         pltpu.VMEM((points, WIDTH), f32),
         pltpu.VMEM((points, WIDTH), bf16),
         pltpu.VMEM((WIDTH, LANES), f32),
@@ -1221,14 +1258,15 @@
         pltpu.VMEM((per_matrix, LOW_ROWS, LANES), f32),
         pltpu.VMEM((per_matrix, LOW_ROWS, LANES), f32),
         pltpu.VMEM((low_kinds, half, LOW_ROWS, LANES), f32),
+        pltpu.VMEM((SLICE_ROWS, LANES), f32),
         pltpu.VMEM((slots, SLICE_ROWS, LANES), f32),
         pltpu.VMEM((up(max(span * SLICE_ROWS, SLICE_ROWS + shard_rows), SLICE_ROWS), LANES), f32),
         pltpu.VMEM((shard_rows * LANES,), f32),
         pltpu.VMEM((slab_rows, LANES), f32),
         pltpu.VMEM((slab_rows, LANES), bf16),
         pltpu.VMEM((2, half, slab_rows, LANES), bf16),
-        dma((5,)),
-        dma((5,)),
+        dma((6,)),
+        dma((6,)),
         dma((slots,)),
         dma((slots,)),
         dma((2,)),

time: 67.5 us -> 65.5 us (0.970)
  Pallas kernels: 66.5 us -> 64.6 us
    pallas_call x1, Pallas kernels: 64.9 us -> 63 us  [shards(): pl.pallas_call(functools.partial(block_kernel, n_rows, n_cols), out_shape...]
where the time goes in v4:
time: 65.5 us; the launch traced here: 65.4 us
  Pallas kernels  64.6 us (99%)
  between operations  0.8 us (1%)
    pallas_call x1, Pallas kernels, shards(): pl.pallas_call(functools.partial(block_kernel, n_rows, n_cols), out_shape...  63 us
    pallas_call x1, Pallas kernels, shards(): pl.pallas_call(finish_kernel, out_shape=(shape(features.shape, bf16), sha...  1.61 us

profile of v4, /device:TPU:1, one launch (start us, length us, event | category | flops | bytes accessed | tf_op | source)
XLA Modules:
  0.0 65.4 jit_solution(10235344862496036522)
XLA Ops:
  0.6 63.0 %shard_map.144 = (bf16[512,256]{1,0:T(8,128)(2,1)S(1)}, bf16[512,256]{1,0:T(8,128)(2,1)S(1)}, f32[1,128]{1,0:T(1,128)S(1)}, f32[10587]{0:T(1024)S(1)}, f32[10587...) custom-call(bf16[512,256]{1,0:T(8,128)(2,1)} %feat_h.1, f32[3,512]{1,0:T(4,128)} %coords_h.1, ...), custom_call_target="tpu_custom_call" | custom-call | tf_op jit(solution)/shard_map/pallas_call | solution.py:1283
  63.6 1.6 %shard_map.145 = (bf16[512,256]{1,0:T(8,128)(2,1)}, bf16[512,256]{1,0:T(8,128)(2,1)}, f32[1,1]{1,0:T(1,128)}, f32[10587]{0:T(1024)}, f32[10587]{0:T(1024)}, /*index=5*/f32[10587]{0:T(1024)}, bf16[338784]{0:T(1024)(128)(2,1)}) custom-call(bf16[512,256]{1,0:T(8,128)(2,1)S(1)} %get-tuple-element.21.out_t, bf16[512,256]{1,0:T(8,128)(2,1)S(1)} %get-tuple-element.22.gfeat_t, ...), custom_call_target="tpu_custom_call" | custom-call | tf_op jit(solution)/shard_map/pallas_call | solution.py:1301

commit v5 on v4

--- a/solution.py
+++ b/solution.py
@@ -30,6 +30,7 @@
 LOW_ROWS = SLICE // WIDTH * 2 * GROUPS // LANES
 DENSE_FROM = 3
 CHUNK = 1024
+POS_ROWS = 32
 
 bn_eps = 1e-05
 clip_norm = 0.01
@@ -147,7 +148,7 @@
     feat, coords, valid, nbrs, cot, w_first, pos_first, weights, state, news, outs, norm_s, in_sem, out_sem,
     stat_send, stat_buf, stat_ssem, stat_rsem,
     tail1d, mats, onehot, vgat, att, wpre, uact, dyw, rel, pos, act, pmask, allow, dmix,
-    ft_s, slope_a, slope_p, a1_s, z_s, h_s, h_ts, q_s, k_s, ba_s, o_s, o_ts, do_s, dv_s, sk_s, bd_s, dp_s, ds_s, dw_s, xs, dz_s, dz16,
+    ft_s, slope_a, slope_p, a1_s, z_s, h_s, h_ts, q_s, k_s, ba_s, o_s, o_ts, do_s, dv_s, sk_s, bd_s, ds_s, dw_s, xs, dz_s, dz16,
     mu_s, flat, pair_got, part16, got16, first_f, first_got, wide16, got_wide, low_f, low_got, low_sum, got_low, hat_s, sums, owned, tail_g, slab_f, shard_w, all_w,
     pair_ssem, pair_rsem, rs_ssem, rs_rsem, wd_ssem, wd_rsem, low_ssem, low_rsem, own_ssem, own_rsem, ag_ssem, ag_rsem, fw_ssem, fw_rsem,
 ):
@@ -417,7 +418,7 @@
     for b in range(blocks):
         for j in range(NEAREST):
             index = nbrs[j : j + 1, b * LANES : (b + 1) * LANES] - starts[b]
-            onehot[b, :, j * LANES : (j + 1) * LANES] = jnp.where(
+            onehot[b, 0:WINDOW, j * LANES : (j + 1) * LANES] = jnp.where(
                 window_row == index, 1.0, 0.0
             ).astype(bf16)
 
@@ -429,7 +430,7 @@
     pos_in_cols = [pos_in_col(c) for c in range(3)]
     for b in range(blocks):
         here = slice(b * LANES, (b + 1) * LANES)
-        fetched = nn(table[:, starts[b] : starts[b] + WINDOW], onehot[b])
+        fetched = nn(table[:, starts[b] : starts[b] + WINDOW], onehot[b, 0:WINDOW])
         place_n = fetched[0:8] + fetched[8:16] + fetched[16:24]
         mask_n = fetched[24:32]
         r = place_n - tiles(coords8[:, here])
@@ -488,6 +489,9 @@
     mats[8] = nt(reorder, w_v).astype(bf16)
     pos_mat = jnp.concatenate(pos_rows + [jnp.zeros((13, WIDTH), f32)], axis=0).astype(bf16)
     pos_cols = nt(reorder, pos_mat)
+    pos_lanes = jnp.concatenate(
+        [pos_cols[:, 0:8]] * 3 + [jnp.zeros((WIDTH, POS_ROWS - 24), f32)], axis=1
+    ).astype(bf16)
     pos_cols = [pos_cols[:, d : d + 1] for d in range(3)]
     feat_f = feat[...].astype(f32)
     ft_s[...] = feat_f.T.astype(bf16)
@@ -520,7 +524,14 @@
     q_att = nn(att_in_t, q_t)
     k_att = jnp.concatenate(split(nn(att_in_t, k_t), 3), axis=0)
     pos_att = nt(att_in_t, pos_mat)
-    pos_att_cols = [pos_att[:, d : d + 1] for d in range(3)]
+    none = jnp.zeros((GROUPS, 8), f32)
+    pos_ext = [piece.astype(f32) for piece in split(-pos_att[:, 0:8], 3)]
+    pos_ext = jnp.concatenate(
+        [
+            jnp.concatenate([pos_ext[k]] * (3 - k) + [none] * (k + 1), axis=1) for k in range(3)
+        ],
+        axis=0,
+    ).astype(bf16)
     back_att = jnp.concatenate([nn(att_in_t, mats[6]), nn(att_in_t, mats[7])], axis=0)
     back_split = split(back_att, 2)
     ba_s[...] = jnp.concatenate([back_split[0], back_split[0], back_split[1]], axis=0)
@@ -531,12 +542,16 @@
         here = slice(b * LANES, (b + 1) * LANES)
         active = silu_parts((pos[b] - mean_p) * rs_p * gain_p + shift_p)[0]
         act[b] = active
-        fetched = nn(k_att[:, starts[b] : starts[b] + WINDOW], onehot[b])
+        pieces = [piece.astype(f32) for piece in split(active, 3)]
+        onehot[b, WINDOW : WINDOW + POS_ROWS] = jnp.concatenate(
+            pieces + [jnp.zeros((POS_ROWS - 24, PAIRS), f32)], axis=0
+        ).astype(bf16)
+        fetched = nn(
+            jnp.concatenate([k_att[:, starts[b] : starts[b] + WINDOW], pos_ext], axis=1), onehot[b]
+        )
         w = tiles(q_att[:, here]) - (
             fetched[0:GROUPS] + fetched[GROUPS : 2 * GROUPS] + fetched[2 * GROUPS : 3 * GROUPS]
         )
-        for d in range(3):
-            w = w + pos_att_cols[d] * active[d : d + 1]
         wpre[b] = w
         mw = w * pmask[b, 0:1]
         sum_w = sum_w + lane_fold(mw)
@@ -550,7 +565,9 @@
     collect_w = all_sum(1, jnp.concatenate([pair_row(sum_w, sqr_w), fold(sum_f)], axis=0))
     v_t = nn(mats[8], h_ts[...]).astype(bf16)
     for b in range(blocks):
-        vgat[b] = nn(v_t[:, starts[b] : starts[b] + WINDOW], onehot[b])
+        vgat[b] = nn(
+            jnp.concatenate([v_t[:, starts[b] : starts[b] + WINDOW], pos_lanes], axis=1), onehot[b]
+        )
     stats = collect_w()
     mean_f = stats[1:3] * inv_points
     mean_w, rs_w = moments(
@@ -582,15 +599,8 @@
         share = 1.0 / functools.reduce(jnp.add, [weight[:, cols(j)] for j in range(NEAREST)])
         att[b] = weight * tiles(share)
         mixed = jnp.zeros((WIDTH, LANES), f32)
-        enc = [jnp.zeros((GROUPS, LANES), f32) for _ in range(3)]
         for j in range(NEAREST):
-            a = att[b, :, cols(j)]
-            mixed = mixed + each_channel(a) * vgat[b, :, cols(j)]
-            for d in range(3):
-                enc[d] = enc[d] + a * act[b, d : d + 1, cols(j)]
-        bd_s[:, here] = jnp.concatenate(enc, axis=0)
-        for d in range(3):
-            mixed = mixed + pos_cols[d] * each_channel(enc[d])
+            mixed = mixed + each_channel(att[b, :, cols(j)]) * vgat[b, :, cols(j)]
         o_s[here, :] = mixed.T.astype(bf16)
 
     z = nn(o_s[...], mats[4])
@@ -621,6 +631,14 @@
         dyw[b] = silu_slope(y, silu_parts(y)[1])
     send_wide(ahat_pair, 0)
     o_ts[...] = nn(o_s[...], reorder).T.astype(bf16)
+    for b in range(blocks):
+        here = slice(b * LANES, (b + 1) * LANES)
+        enc = [jnp.zeros((GROUPS, LANES), f32) for _ in range(3)]
+        for j in range(NEAREST):
+            a = att[b, :, cols(j)]
+            for d in range(3):
+                enc[d] = enc[d] + a * act[b, d : d + 1, cols(j)]
+        bd_s[:, here] = jnp.concatenate(enc, axis=0)
     stats = collect_o()
     mean_o, rs_o = moments(unfold(stats[0:2]), unfold(stats[2:4]), inv_points)
 
@@ -660,14 +678,9 @@
     for b in range(blocks):
         here = slice(b * LANES, (b + 1) * LANES)
         do = do_s[:, here]
-        do_pos = [over_channels(do * pos_cols[d]) for d in range(3)]
-        dp_s[:, here] = jnp.concatenate(do_pos, axis=0)
         da = []
         for j in range(NEAREST):
-            grad = over_channels(do * vgat[b, :, cols(j)])
-            for d in range(3):
-                grad = grad + do_pos[d] * act[b, d : d + 1, cols(j)]
-            da.append(grad)
+            da.append(over_channels(do * vgat[b, :, cols(j)]))
         mean_da = functools.reduce(jnp.add, [da[j] * att[b, :, cols(j)] for j in range(NEAREST)])
         ds = jnp.concatenate(
             [att[b, :, cols(j)] * (da[j] - mean_da) for j in range(NEAREST)], axis=1
@@ -693,10 +706,10 @@
         for j in range(NEAREST):
             xs[b, :, cols(j)] = (each_channel(att[b, :, cols(j)]) * do).astype(bf16)
         mix = [
-            (tiles(dp_s[d * GROUPS : (d + 1) * GROUPS, here]) * att[b]).astype(bf16) for d in range(3)
+            (tiles(over_channels(do * pos_cols[d])) * att[b]).astype(bf16) for d in range(3)
         ]
         dmix[b] = nn(add_groups, jnp.concatenate(mix, axis=0))
-        dv_s[pl.ds(starts[b], WINDOW)] += nt(onehot[b], xs[b])
+        dv_s[pl.ds(starts[b], WINDOW)] += nt(onehot[b, 0:WINDOW], xs[b])
     dv = dv_s[...].astype(bf16)
     dv_s[...] = nn(dv, mats[8])
     put_matrix(3, nn(h_ts[...], nn(dv, reorder).astype(bf16)))
@@ -715,7 +728,7 @@
     dw_sums = []
     for b in range(blocks):
         dw = (gain_w * rs_w * (dyw[b] - pmask[b, 0:1] * (one + wpre[b] * two))).astype(bf16)
-        sk_s[pl.ds(starts[b], WINDOW)] += nt(onehot[b], dw)
+        sk_s[pl.ds(starts[b], WINDOW)] += nt(onehot[b, 0:WINDOW], dw)
         dw_sums.append(lane_slots(dw.astype(f32)))
         dw_s[b] = dw
     dq_att = jnp.concatenate(dw_sums, axis=1)
@@ -822,6 +835,22 @@
         moved = gain_p * rs_p * (moved - one * pos_alone[c] - two * pos_hat[c])
         pos_in_row = pos_in_row + col_to_row(moved, 3 * c)
 
+    begin = me * shard_len
+    lead, skip = lax.rem(begin, CHUNK), lax.rem(begin, LANES)
+    shard_at = pl.ds(lead // LANES, shard_rows)
+    lanes_all = iota((shard_rows, LANES), 1)
+    inside = iota((shard_rows, LANES), 0) * LANES + lanes_all < shard_len
+    main = shard_len // 1024 * 1024
+    parts = [pl.ds(at, size) for at, size in ((0, main), (main, shard_len - main)) if size]
+    for k in range(3):
+        for at in parts:
+            tail_g[at] = state[k][at]
+        rows = jnp.where(inside, tail_g[...].reshape(shard_rows, LANES), 0.0)
+        turned = pltpu.roll(rows, skip, 1)
+        above = pltpu.roll(turned, 1, 0)
+        slab_f[k] = jnp.zeros(slab_f.shape[1:], f32)
+        slab_f[k, shard_at, :] = jnp.where(lanes_all < skip, above, turned)
+
     def slice_of(slot):
         return 2 * (slot * half + chip) + core
 
@@ -860,7 +889,7 @@
         factor = factor.reshape(SLICE // WIDTH, 2 * GROUPS)[:, which * GROUPS : (which + 1) * GROUPS]
         return sum(nn(piece, att_in_t) for piece in split(factor, 2)).reshape(SLICE_ROWS, LANES)
 
-    squares = jnp.zeros((1, 1), f32)
+    squares = jnp.zeros((SLICE_ROWS, LANES), f32)
     matrix = SQUARE // SLICE
     for slot in range(slots):
         sums[slot] = jnp.zeros((SLICE_ROWS, LANES), f32)
@@ -910,7 +939,8 @@
     each_slot(5 * matrix, 2 * sliced, functools.partial(take_dense, True))
     each_slot(OFF_TAIL // SLICE, OFF_TAIL // SLICE + 1, add_pos_in)
     for slot in range(slots):
-        squares = squares + lane_sum(row_sum(sums[slot] * sums[slot]))
+        squares = squares + sums[slot] * sums[slot]
+    squares = total(squares)
 
     collect_norm = all_sum(6, jnp.where(lane == 0, squares, 0.0))
 
@@ -951,7 +981,6 @@
 
         each_owner(slot, hand_over)
 
-    begin = me * shard_len
     first_slice = begin // SLICE
     last_slice = (begin + shard_len - 1) // SLICE
     for k in range(span):
@@ -962,42 +991,18 @@
             rows = owned.at[pl.ds(k * SLICE_ROWS, SLICE_ROWS)]
             pltpu.make_async_copy(rows, rows, own_rsem.at[k]).wait()
 
-    offset = begin - first_slice * SLICE
-    skip = lax.rem(offset, LANES)
-    lanes_all = iota((shard_rows, LANES), 1)
-    rows = owned[pl.ds(offset // LANES, shard_rows), :]
-    turned = pltpu.roll(rows, lax.rem(LANES - skip, LANES), 1)
-    below = pltpu.roll(turned, shard_rows - 1, 0)
-    grad = jnp.where(lanes_all < LANES - skip, turned, below)
-    inside = iota(grad.shape, 0) * LANES + lanes_all < shard_len
-    grad = jnp.where(inside, grad, 0.0)
+    slab_shape = slab_f.shape[1:]
+    flat_at = iota(slab_shape, 0) * LANES + iota(slab_shape, 1) - lead
+    grad = owned[pl.ds((begin - lead - first_slice * SLICE) // LANES, slab_shape[0]), :]
+    grad = jnp.where((flat_at >= 0) & (flat_at < shard_len), grad, 0.0)
 
     stats = collect_norm()
     norm = jnp.sqrt(pick(stats, 0))
+    grad = grad * jnp.minimum(1.0, clip_norm / norm)
+    updated = adam(slab_f[0], slab_f[1], slab_f[2], grad)
+    shard_w[...] = updated[0].astype(bf16)
+    all_w[core, chip] = updated[0].astype(bf16)
     norm_s[...] = jnp.broadcast_to(norm, norm_s.shape)
-    grad = grad * jnp.minimum(1.0, clip_norm / norm)
-
-    main = shard_len // 1024 * 1024
-    spare = shard_len - main
-    tail_g[...] = grad.reshape(shard_rows * LANES)
-    for start, size in ((0, main), (main, spare)):
-        if size == 0:
-            continue
-        at = pl.ds(start, size)
-        p_new, m_new, s_new = adam(state[0][at], state[1][at], state[2][at], tail_g[at])
-        news[0][at] = p_new
-        news[1][at] = m_new
-        news[2][at] = s_new
-        tail_g[at] = p_new
-    moved = jnp.where(inside, tail_g[...].reshape(shard_rows, LANES), 0.0)
-    turned = pltpu.roll(moved, skip, 1)
-    above = pltpu.roll(turned, 1, 0)
-    slab_f[...] = jnp.zeros(slab_f.shape, f32)
-    slab_f[pl.ds(lax.rem(begin, CHUNK) // LANES, shard_rows), :] = jnp.where(
-        lanes_all < skip, above, turned
-    )
-    shard_w[...] = slab_f[...].astype(bf16)
-    all_w[core, chip] = slab_f[...].astype(bf16)
 
     in_row = n_cols // 2
     row_chip = col_id // 2
@@ -1037,8 +1042,51 @@
     loop(1, in_row, send_within)
     forward(chip)
     store(norm_s, gnorm_h)
+    for k in range(3):
+        slab_f[k] = updated[k]
+        turned = pltpu.roll(slab_f[k, shard_at, :], lax.rem(LANES - skip, LANES), 1)
+        below = pltpu.roll(turned, shard_rows - 1, 0)
+        tail_g[...] = jnp.where(lanes_all < LANES - skip, turned, below).reshape(shard_rows * LANES)
+        for at in parts:
+            news[k][at] = tail_g[at]
     for source, target in ((0, new_master_h), (1, new_first_h), (2, new_second_h)):
         store(news[source], target)
+
+    for index, rows in sent:
+        drain_stats(index, rows)
+
+    def drain(low, high, slices, sem):
+        if high - low == half:
+            rest = slices.at[pl.ds(0, half - 1)]
+            pltpu.make_async_copy(rest, rest, sem).wait()
+        else:
+            inside = (chip >= low) & (chip < high)
+
+            def wait_one(k, carry):
+                pltpu.make_async_copy(slices.at[0], slices.at[0], sem).wait()
+                return carry
+
+            lax.fori_loop(0, high - low - inside.astype(jnp.int32), wait_one, 0)
+
+    for which in range(2):
+        drain(0, per_matrix, got_wide.at[which], wd_ssem.at[which])
+    for kind in range(low_kinds):
+        low_at = (1 + kind) * per_matrix % half
+        drain(low_at, low_at + per_matrix, got_low.at[kind], low_ssem.at[kind])
+    for slot in range(slots):
+        low_at = max(dense - slot * half, 0)
+        high_at = min(sliced - slot * half, half)
+        if high_at > low_at:
+            drain(low_at, high_at, got16.at[slot], rs_ssem.at[slot])
+
+        def own_drain(owner, k, side, slot=slot):
+            @pl.when(owner != me)
+            def _():
+                own_copy(slot, owner, k, side).wait_send()
+
+        each_owner(slot, own_drain)
+    for copy in stores:
+        copy.wait()
 
     def spread_row(k, carry):
         other = peer(row_id, n_rows - k, n_rows) * in_row + row_chip
@@ -1086,41 +1134,9 @@
         both = jnp.concatenate(parts, axis=0).astype(bf16).reshape(2 * CHUNK)
         weights_out[pl.ds(2 * CHUNK * whole, left)] = both[0:left]
 
-    for index, rows in sent:
-        drain_stats(index, rows)
-    for copy in stores:
-        copy.wait()
     pltpu.make_async_copy(all_w.at[core], all_w.at[core], fw_ssem).wait()
     rest = all_w.at[core, pl.ds(0, half - 1)]
     pltpu.make_async_copy(rest, rest, ag_ssem).wait()
-    def drain(count, ref, sem):
-        def wait_one(k, carry):
-            pltpu.make_async_copy(ref, ref, sem).wait()
-            return carry
-
-        lax.fori_loop(0, count, wait_one, 0)
-
-    def others(low, high):
-        inside = (chip >= low) & (chip < high)
-        return high - low - inside.astype(jnp.int32)
-
-    for which in range(2):
-        drain(others(0, per_matrix), wide16.at[0, 0], wd_ssem.at[which])
-    for kind in range(low_kinds):
-        low_at = (1 + kind) * per_matrix % half
-        drain(others(low_at, low_at + per_matrix), low_sum.at[0], low_ssem.at[kind])
-    for slot in range(slots):
-        low_at = max(dense - slot * half, 0)
-        high_at = min(sliced - slot * half, half)
-        if high_at > low_at:
-            drain(others(low_at, high_at), part16.at[0], rs_ssem.at[slot])
-
-        def own_drain(owner, k, side, slot=slot):
-            @pl.when(owner != me)
-            def _():
-                own_copy(slot, owner, k, side).wait_send()
-
-        each_owner(slot, own_drain)
 
 
 def finish_kernel(
@@ -1211,7 +1227,7 @@
         dma((7,)),
         pltpu.VMEM((TAIL_PAD,), bf16),
         pltpu.VMEM((9, WIDTH, WIDTH), bf16),
-        pairs(WINDOW, bf16),
+        pairs(WINDOW + POS_ROWS, bf16),
         pairs(WIDTH),
         pairs(GROUPS),
         pairs(GROUPS),
@@ -1239,7 +1255,6 @@
         pltpu.VMEM((points, WIDTH), f32),
         pltpu.VMEM((points, GROUPS), f32),
         pltpu.VMEM((3 * GROUPS, points), f32),
-        pltpu.VMEM((3 * GROUPS, points), f32),
         pairs(GROUPS, bf16),
         pairs(GROUPS, bf16),
         pairs(WIDTH, bf16),
@@ -1260,9 +1275,9 @@
         pltpu.VMEM((low_kinds, half, LOW_ROWS, LANES), f32),
         pltpu.VMEM((SLICE_ROWS, LANES), f32),
         pltpu.VMEM((slots, SLICE_ROWS, LANES), f32),
-        pltpu.VMEM((up(max(span * SLICE_ROWS, SLICE_ROWS + shard_rows), SLICE_ROWS), LANES), f32),
+        pltpu.VMEM((up(max(span * SLICE_ROWS, CHUNK // LANES + slab_rows), SLICE_ROWS), LANES), f32),
         pltpu.VMEM((shard_rows * LANES,), f32),
-        pltpu.VMEM((slab_rows, LANES), f32),
+        pltpu.VMEM((3, slab_rows, LANES), f32),
         pltpu.VMEM((slab_rows, LANES), bf16),
         pltpu.VMEM((2, half, slab_rows, LANES), bf16),
         dma((6,)),

time: 65.5 us -> 64.5 us (0.985)
  Pallas kernels: 64.6 us -> 63.4 us
    pallas_call x1, Pallas kernels: 63 us -> 61.8 us  [shards(): pl.pallas_call(functools.partial(block_kernel, n_rows, n_cols), out_shape...]
where the time goes in v5:
time: 64.5 us; the launch traced here: 64.2 us
  Pallas kernels  63.4 us (98%)
  between operations  0.8 us (1%)
    pallas_call x1, Pallas kernels, shards(): pl.pallas_call(functools.partial(block_kernel, n_rows, n_cols), out_shape...  61.8 us
    pallas_call x1, Pallas kernels, shards(): pl.pallas_call(finish_kernel, out_shape=(shape(features.shape, bf16), sha...  1.61 us

profile of v5, /device:TPU:1, one launch (start us, length us, event | category | flops | bytes accessed | tf_op | source)
XLA Modules:
  0.0 64.2 jit_solution(10106729523995481153)
XLA Ops:
  0.6 61.8 %shard_map.144 = (bf16[512,256]{1,0:T(8,128)(2,1)S(1)}, bf16[512,256]{1,0:T(8,128)(2,1)S(1)}, f32[1,128]{1,0:T(1,128)S(1)}, f32[10587]{0:T(1024)S(1)}, f32[10587...) custom-call(bf16[512,256]{1,0:T(8,128)(2,1)} %feat_h.1, f32[3,512]{1,0:T(4,128)} %coords_h.1, ...), custom_call_target="tpu_custom_call" | custom-call | tf_op jit(solution)/shard_map/pallas_call | solution.py:1298
  62.5 1.6 %shard_map.145 = (bf16[512,256]{1,0:T(8,128)(2,1)}, bf16[512,256]{1,0:T(8,128)(2,1)}, f32[1,1]{1,0:T(1,128)}, f32[10587]{0:T(1024)}, f32[10587]{0:T(1024)}, /*index=5*/f32[10587]{0:T(1024)}, bf16[338784]{0:T(1024)(128)(2,1)}) custom-call(bf16[512,256]{1,0:T(8,128)(2,1)S(1)} %get-tuple-element.21.out_t, bf16[512,256]{1,0:T(8,128)(2,1)S(1)} %get-tuple-element.22.gfeat_t, ...), custom_call_target="tpu_custom_call" | custom-call | tf_op jit(solution)/shard_map/pallas_call | solution.py:1316

commit v6 on v5

--- a/solution.py
+++ b/solution.py
@@ -734,11 +734,6 @@
     dq_att = jnp.concatenate(dw_sums, axis=1)
     both_att = jnp.concatenate([dq_att.T, -sk_s[...]], axis=1)
     both_split = split(both_att, 2)
-    low = nn(
-        jnp.concatenate([h_ts[...]] * 2, axis=1), jnp.concatenate(both_split, axis=0)
-    )
-    low_f[...] = low.reshape(per_matrix, 2, LOW_ROWS, LANES)
-    low_pair = swap(3, low_f, low_got)
     dh = nn(jnp.concatenate(both_split + both_split[0:1], axis=1), ba_s[...]) + dv_s[...]
     dy = dh * slope_a[...]
     z_s[...] = dy
@@ -747,6 +742,11 @@
         [mu_s[...] * shift_grad_a[:, k * LANES : (k + 1) * LANES] for k in range(2)], axis=1
     )
     first_pair = put_first(1, from_feat(dy) - away)
+    low = nn(
+        jnp.concatenate([h_ts[...]] * 2, axis=1), jnp.concatenate(both_split, axis=0)
+    )
+    low_f[...] = low.reshape(per_matrix, 2, LOW_ROWS, LANES)
+    low_pair = swap(3, low_f, low_got)
     along = [jnp.zeros((8, 1), f32) for _ in range(3)]
     sum_p = jnp.zeros((8, 1), f32)
     sqr_p = jnp.zeros((8, 1), f32)
@@ -812,29 +812,6 @@
     small_pair = swap(4, flat.at[small_flat], pair_got.at[small_flat])
     send_dense(small_pair, small, sliced - small)
 
-    stats = collect_a()
-    one, two = unfold(stats[0:2]) * inv_points, unfold(stats[2:4]) * inv_points
-    def halves(row):
-        return jnp.concatenate(
-            [
-                jnp.broadcast_to(row[:, k * LANES : (k + 1) * LANES], (SLICE_ROWS // 2, LANES))
-                for k in range(2)
-            ],
-            axis=0,
-        )
-
-    scale_tile, two_tile = halves(gain_a * rs_a), halves(two)
-    da1 = (gain_a * rs_a * (z_s[...] - point_mask * (one + a1_s[...] * two))).astype(bf16)
-    outs[1] = (dz_s[...] + nt(da1, w_in)).astype(bf16)
-    store(outs.at[1], gfeat_h)
-    one = row_to_col(stats[4:5, 0:8], 8) * inv_pairs
-    two = row_to_col(stats[4:5, 8:16], 8) * inv_pairs
-    pos_in_row = jnp.zeros((1, LANES), f32)
-    for c in range(3):
-        moved = row_to_col(stats[4:5, 16 + 8 * c : 24 + 8 * c], 8)
-        moved = gain_p * rs_p * (moved - one * pos_alone[c] - two * pos_hat[c])
-        pos_in_row = pos_in_row + col_to_row(moved, 3 * c)
-
     begin = me * shard_len
     lead, skip = lax.rem(begin, CHUNK), lax.rem(begin, LANES)
     shard_at = pl.ds(lead // LANES, shard_rows)
@@ -851,6 +828,26 @@
         slab_f[k] = jnp.zeros(slab_f.shape[1:], f32)
         slab_f[k, shard_at, :] = jnp.where(lanes_all < skip, above, turned)
 
+    stats = collect_a()
+    one_a, two_a = unfold(stats[0:2]) * inv_points, unfold(stats[2:4]) * inv_points
+    def halves(row):
+        return jnp.concatenate(
+            [
+                jnp.broadcast_to(row[:, k * LANES : (k + 1) * LANES], (SLICE_ROWS // 2, LANES))
+                for k in range(2)
+            ],
+            axis=0,
+        )
+
+    scale_tile, two_tile = halves(gain_a * rs_a), halves(two_a)
+    one = row_to_col(stats[4:5, 0:8], 8) * inv_pairs
+    two = row_to_col(stats[4:5, 8:16], 8) * inv_pairs
+    pos_in_row = jnp.zeros((1, LANES), f32)
+    for c in range(3):
+        moved = row_to_col(stats[4:5, 16 + 8 * c : 24 + 8 * c], 8)
+        moved = gain_p * rs_p * (moved - one * pos_alone[c] - two * pos_hat[c])
+        pos_in_row = pos_in_row + col_to_row(moved, 3 * c)
+
     def slice_of(slot):
         return 2 * (slot * half + chip) + core
 
@@ -1052,6 +1049,9 @@
     for source, target in ((0, new_master_h), (1, new_first_h), (2, new_second_h)):
         store(news[source], target)
 
+    da1 = (gain_a * rs_a * (z_s[...] - point_mask * (one_a + a1_s[...] * two_a))).astype(bf16)
+    outs[1] = (dz_s[...] + nt(da1, w_in)).astype(bf16)
+    store(outs.at[1], gfeat_h)
     for index, rows in sent:
         drain_stats(index, rows)
 
@@ -1141,8 +1141,8 @@
 
 def finish_kernel(
     out_t, gfeat_t, gnorm_t, master_t, first_t, second_t, weights_t,
-    out_h, gfeat_h, gnorm, master_h, first_h, second_h, weights_h,
-    norm_s, sem,
+    out_h, gfeat_h, gnorm_h, master_h, first_h, second_h, weights_h,
+    norm_s, gnorm, sem,
 ):
     copies = [
         pltpu.make_async_copy(source, target, sem.at[k])
@@ -1162,7 +1162,9 @@
         copy.start()
     copies[-1].wait()
     gnorm[...] = norm_s[0:1, 0:1]
-    for copy in copies[:-1]:
+    copies[-1] = pltpu.make_async_copy(gnorm, gnorm_h, sem.at[len(copies)])
+    copies[-1].start()
+    for copy in copies:
         copy.wait()
 
 
@@ -1325,8 +1327,8 @@
             shape(weights.shape, bf16),
         ),
         in_specs=[pl.BlockSpec(memory_space=pl.ANY)] * 7,
-        out_specs=[hbm, hbm, vmem, hbm, hbm, hbm, hbm],
-        scratch_shapes=[pltpu.VMEM((1, LANES), f32), dma((7,))],
+        out_specs=[hbm] * 7,
+        scratch_shapes=[pltpu.VMEM((1, LANES), f32), pltpu.VMEM((1, 1), f32), dma((8,))],
         compiler_params=pltpu.CompilerParams(vmem_limit_bytes=8 * 2**20),
     )(*results)
     return results[0], results[1], results[2].reshape(()), *results[3:]

time: 64.5 us -> 63.9 us (level)
  no operation moved by 1% of the time
where the time goes in v6:
time: 63.9 us; the launch traced here: 63.7 us
  Pallas kernels  62.9 us (98%)
  between operations  0.8 us (1%)
    pallas_call x1, Pallas kernels, shards(): pl.pallas_call(functools.partial(block_kernel, n_rows, n_cols), out_shape...  61.8 us

profile of v6, /device:TPU:1, one launch (start us, length us, event | category | flops | bytes accessed | tf_op | source)
XLA Modules:
  0.0 63.7 jit_solution(10698100565613788467)
XLA Ops:
  0.6 61.8 %shard_map.144 = (bf16[512,256]{1,0:T(8,128)(2,1)S(1)}, bf16[512,256]{1,0:T(8,128)(2,1)S(1)}, f32[1,128]{1,0:T(1,128)S(1)}, f32[10587]{0:T(1024)S(1)}, f32[10587...) custom-call(bf16[512,256]{1,0:T(8,128)(2,1)} %feat_h.1, f32[3,512]{1,0:T(4,128)} %coords_h.1, ...), custom_call_target="tpu_custom_call" | custom-call | tf_op jit(solution)/shard_map/pallas_call | solution.py:1300
  62.4 1.1 %shard_map.145 = (bf16[512,256]{1,0:T(8,128)(2,1)}, bf16[512,256]{1,0:T(8,128)(2,1)}, f32[1,1]{1,0:T(1,128)}, f32[10587]{0:T(1024)}, f32[10587]{0:T(1024)}, /*index=5*/f32[10587]{0:T(1024)}, bf16[338784]{0:T(1024)(128)(2,1)}) custom-call(bf16[512,256]{1,0:T(8,128)(2,1)S(1)} %get-tuple-element.21.out_t, bf16[512,256]{1,0:T(8,128)(2,1)S(1)} %get-tuple-element.22.gfeat_t, ...), custom_call_target="tpu_custom_call" | custom-call | tf_op jit(solution)/shard_map/pallas_call | solution.py:1318

commit v7 on v6

--- a/solution.py
+++ b/solution.py
@@ -200,7 +200,7 @@
     early = [
         load(feat_h, feat),
         load(weights_h.at[pl.ds(0, SQUARE)], w_first),
-        load(weights_h.at[pl.ds(OFF_TAIL, 1024)], pos_first),
+        load(weights_h.at[pl.ds(OFF_ATT_OUT, SLICE)], pos_first),
         load(nbrs_h, nbrs),
         load(coords_h, coords),
         load(valid_h, valid),
@@ -353,7 +353,8 @@
     w_in = w_first[...].reshape(WIDTH, WIDTH)
     mats[0] = w_in
     w_in = mats[0]
-    pos_in = pos_first[...].reshape(1024 // LANES, LANES)[0:1].astype(f32)
+    at = (OFF_TAIL - OFF_ATT_OUT) // LANES
+    pos_in = pos_first[...].reshape(SLICE_ROWS, LANES).astype(f32)[at : at + 1]
     lane8 = iota((8, 1), 0)
 
     def pos_in_col(c):
@@ -521,16 +522,10 @@
     q_s[...] = q_t
     k_s[...] = k_t
     h_ts[...] = h_t
-    q_att = nn(att_in_t, q_t)
-    k_att = jnp.concatenate(split(nn(att_in_t, k_t), 3), axis=0)
     pos_att = nt(att_in_t, pos_mat)
-    none = jnp.zeros((GROUPS, 8), f32)
-    pos_ext = [piece.astype(f32) for piece in split(-pos_att[:, 0:8], 3)]
-    pos_ext = jnp.concatenate(
-        [
-            jnp.concatenate([pos_ext[k]] * (3 - k) + [none] * (k + 1), axis=1) for k in range(3)
-        ],
-        axis=0,
+    enc_lanes = -jnp.concatenate(pos_rows + [jnp.zeros((5, WIDTH), f32)], axis=0).T
+    enc_lanes = jnp.concatenate(
+        [enc_lanes] * 3 + [jnp.zeros((WIDTH, POS_ROWS - 24), f32)], axis=1
     ).astype(bf16)
     back_att = jnp.concatenate([nn(att_in_t, mats[6]), nn(att_in_t, mats[7])], axis=0)
     back_split = split(back_att, 2)
@@ -546,12 +541,14 @@
         onehot[b, WINDOW : WINDOW + POS_ROWS] = jnp.concatenate(
             pieces + [jnp.zeros((POS_ROWS - 24, PAIRS), f32)], axis=0
         ).astype(bf16)
-        fetched = nn(
-            jnp.concatenate([k_att[:, starts[b] : starts[b] + WINDOW], pos_ext], axis=1), onehot[b]
+        vgat[b] = nn(
+            jnp.concatenate([k_s[:, starts[b] : starts[b] + WINDOW], enc_lanes], axis=1), onehot[b]
         )
-        w = tiles(q_att[:, here]) - (
-            fetched[0:GROUPS] + fetched[GROUPS : 2 * GROUPS] + fetched[2 * GROUPS : 3 * GROUPS]
-        )
+        here_q = q_s[:, here].astype(f32)
+        for j in range(NEAREST):
+            at = slice(j * LANES, (j + 1) * LANES)
+            xs[b, :, at] = (here_q - vgat[b, :, at]).astype(bf16)
+        w = nn(att_in_t, xs[b])
         wpre[b] = w
         mw = w * pmask[b, 0:1]
         sum_w = sum_w + lane_fold(mw)
@@ -1215,7 +1212,7 @@
         pltpu.VMEM(neighbors.shape, jnp.int32),
         pltpu.VMEM(features.shape, bf16),
         pltpu.VMEM((SQUARE,), bf16),
-        pltpu.VMEM((1024,), bf16),
+        pltpu.VMEM((SLICE,), bf16),
         pltpu.VMEM(weights.shape, bf16),
         shard(),
         shard(),

time: 63.9 us -> 65.8 us (1.030)
  Pallas kernels: 62.9 us -> 64.7 us
    pallas_call x1, Pallas kernels: 61.8 us -> 63.6 us  [shards(): pl.pallas_call(functools.partial(block_kernel, n_rows, n_cols), out_shape...]
where the time goes in v7:
time: 65.8 us; the launch traced here: 65.5 us
  Pallas kernels  64.7 us (98%)
  between operations  0.8 us (1%)
    pallas_call x1, Pallas kernels, shards(): pl.pallas_call(functools.partial(block_kernel, n_rows, n_cols), out_shape...  63.6 us

profile of v7, /device:TPU:1, one launch (start us, length us, event | category | flops | bytes accessed | tf_op | source)
XLA Modules:
  0.0 65.5 jit_solution(6650964028679140440)
XLA Ops:
  0.6 63.6 %shard_map.144 = (bf16[512,256]{1,0:T(8,128)(2,1)S(1)}, bf16[512,256]{1,0:T(8,128)(2,1)S(1)}, f32[1,128]{1,0:T(1,128)S(1)}, f32[10587]{0:T(1024)S(1)}, f32[10587...) custom-call(bf16[512,256]{1,0:T(8,128)(2,1)} %feat_h.1, f32[3,512]{1,0:T(4,128)} %coords_h.1, ...), custom_call_target="tpu_custom_call" | custom-call | tf_op jit(solution)/shard_map/pallas_call | solution.py:1297
  64.3 1.1 %shard_map.145 = (bf16[512,256]{1,0:T(8,128)(2,1)}, bf16[512,256]{1,0:T(8,128)(2,1)}, f32[1,1]{1,0:T(1,128)}, f32[10587]{0:T(1024)}, f32[10587]{0:T(1024)}, /*index=5*/f32[10587]{0:T(1024)}, bf16[338784]{0:T(1024)(128)(2,1)}) custom-call(bf16[512,256]{1,0:T(8,128)(2,1)S(1)} %get-tuple-element.21.out_t, bf16[512,256]{1,0:T(8,128)(2,1)S(1)} %get-tuple-element.22.gfeat_t, ...), custom_call_target="tpu_custom_call" | custom-call | tf_op jit(solution)/shard_map/pallas_call | solution.py:1315
